TPU v7x, 32 devices: a whole 2x2x4 slice. The times are simulated.
32 devices in a mesh: fsdp: 8 (over z, y), tensor: 4 (over x, core).
Axes of the slice: x: 2, y: 2, z: 4, core: 2. Of those that a mesh axis runs over, the one named last changes fastest.
Arguments:
- tokens: bfloat16 [8192, 2560], P(('fsdp', 'tensor')), may hold values from -6 to 6
- segments: int32 [8192], P('fsdp'), may hold values from 0 to 3, as said below
- positions: int32 [8192], P('fsdp'), may hold values from 0 to 2046, as said below
- norm_input: bfloat16 [2560], P(('fsdp', 'tensor')), may hold values from 0.5 to 1.5
- norm_query: bfloat16 [768], P(('fsdp', 'tensor')), may hold values from 0.5 to 1.5
- norm_latent: bfloat16 [256], P(('fsdp', 'tensor')), may hold values from 0.5 to 1.5
- norm_hidden: bfloat16 [2560], P(('fsdp', 'tensor')), may hold values from 0.5 to 1.5
- query_down: bfloat16 [2560, 768], P(('fsdp', 'tensor')), may hold values from -0.125 to 0.125
- latent_down: bfloat16 [2560, 288], P(('fsdp', 'tensor')), may hold values from -0.125 to 0.125
- query_up: bfloat16 [768, 3840], P('fsdp', 'tensor'), may hold values from -0.3125 to 0.3125
- latent_up: bfloat16 [256, 5120], P('fsdp', 'tensor'), may hold values from -0.375 to 0.375
- attention_out: bfloat16 [2560, 2560], P('tensor', 'fsdp'), may hold values from -2 to 2
- gate_weight: bfloat16 [2560, 6400], P('fsdp', 'tensor'), may hold values from -0.125 to 0.125
- up_weight: bfloat16 [2560, 6400], P('fsdp', 'tensor'), may hold values from -0.125 to 0.125
- down_weight: bfloat16 [6400, 2560], P('tensor', 'fsdp'), may hold values from -0.4375 to 0.4375
- cotangent: bfloat16 [8192, 2560], P(('fsdp', 'tensor')), may hold values from -6 to 6
Outputs:
- output: bfloat16 [8192, 2560], P(('fsdp', 'tensor'))
- token_grad: float32 [8192, 2560], P(('fsdp', 'tensor'))
- grad_norm_input: float32 [2560], P(('fsdp', 'tensor'))
- grad_norm_query: float32 [768], P(('fsdp', 'tensor'))
- grad_norm_latent: float32 [256], P(('fsdp', 'tensor'))
- grad_norm_hidden: float32 [2560], P(('fsdp', 'tensor'))
- grad_query_down: float32 [2560, 768], P(('fsdp', 'tensor'))
- grad_latent_down: float32 [2560, 288], P(('fsdp', 'tensor'))
- grad_query_up: float32 [768, 3840], P('fsdp', 'tensor')
- grad_latent_up: float32 [256, 5120], P('fsdp', 'tensor')
- grad_attention_out: float32 [2560, 2560], P('tensor', 'fsdp')
- grad_gate_weight: float32 [2560, 6400], P('fsdp', 'tensor')
- grad_up_weight: float32 [2560, 6400], P('fsdp', 'tensor')
- grad_down_weight: float32 [6400, 2560], P('tensor', 'fsdp')
Inputs may be any that keep to these rules, and one draw needn't show every extreme that they name: `segments`: within each sequence of 1024 tokens the ids never fall and each of 0, 1, 2, 3 occurs; document 1 begins within the first 256 tokens and ends within the last 256. Within a document the positions count up by one; in every sequence the last token of document 1 has position 2046.
All inputs are finite; a program needn't handle non-finite values.
Results may differ from a plain program's by a relative error of at most 0.028.
Values may be sent and summed in bfloat16 or wider, within the bound.
No kernel may reach another device: no remote copies, remote signals or barrier semaphores. Data moves between devices by JAX's collectives and lax.ppermute only.
A program may use at most 256 MiB of HBM per device.

v0:
```python
import math

import jax
import jax.numpy as jnp
from jax import lax
from jax.sharding import PartitionSpec as P

HEADS = 40
NOPE = 64
ROPE = 32
VDIM = 64
KVR = 256


EPSILON = 1e-05
RESIDUAL = 1.4 / math.sqrt(62.0)
NEGATIVE = -1e30


def normalize(values, gain):
    inverse = lax.rsqrt(jnp.mean(values * values, axis=-1, keepdims=True) + EPSILON)
    return (values * inverse * gain, inverse)


def normalize_back(values, inverse, gain, upstream):
    scaled = upstream * gain
    inner = jnp.mean(scaled * values, axis=-1, keepdims=True)
    grad_values = inverse * scaled - values * (inverse * inverse * inverse) * inner
    grad_gain = jnp.sum(upstream * values * inverse, axis=0)
    return (grad_values, grad_gain)


def rotary_tables(positions):
    steps = jnp.arange(ROPE // 2, dtype=jnp.float32)
    frequency = jnp.exp(steps * (-2.0 * math.log(10000.0) / ROPE))
    angles = positions.astype(jnp.float32)[:, None] * frequency[None, :]
    return (jnp.cos(angles), jnp.sin(angles))


def rotate(values, cosine, sine):
    half = values.shape[-1] // 2
    first = values[..., :half]
    second = values[..., half:]
    return jnp.concatenate(
        [first * cosine - second * sine, second * cosine + first * sine], axis=-1
    )


def product(left, right):
    return jnp.dot(left, right, preferred_element_type=jnp.float32)


def product_left(left, right):
    return lax.dot_general(
        left, right, (((0,), (0,)), ((), ())), preferred_element_type=jnp.float32
    )


def product_right(left, right):
    return lax.dot_general(
        left, right, (((1,), (1,)), ((), ())), preferred_element_type=jnp.float32
    )


def allowed_block(segment_ids, start, block):
    length = segment_ids.shape[0]
    rows_here = start + jnp.arange(block, dtype=jnp.int32)
    columns = jnp.arange(length, dtype=jnp.int32)
    segment_rows = segment_ids[start : start + block]
    return (segment_rows[:, None] == segment_ids[None, :]) & (
        columns[None, :] <= rows_here[:, None]
    )


def head_forward(query_head, key_head, value_head, segment_ids, scale):
    length = query_head.shape[0]
    block = min(512, length)
    outputs = []
    totals = []
    for start in range(0, length, block):
        scores = product_right(query_head[start : start + block], key_head) * scale
        scores = jnp.where(allowed_block(segment_ids, start, block), scores, NEGATIVE)
        top = jnp.max(scores, axis=-1, keepdims=True)
        weights = jnp.exp(scores - top)
        total = jnp.sum(weights, axis=-1, keepdims=True)
        probability = (weights / total).astype(jnp.bfloat16)
        outputs.append(product(probability, value_head))
        totals.append((top + jnp.log(total))[:, 0])
    return (jnp.concatenate(outputs, axis=0), jnp.concatenate(totals, axis=0))


def head_backward(query_head, key_head, value_head, out_grad, log_total, segment_ids, scale):
    length = query_head.shape[0]
    block = min(512, length)
    query_parts = []
    key_grad = jnp.zeros(key_head.shape, jnp.float32)
    value_grad = jnp.zeros(value_head.shape, jnp.float32)
    for start in range(0, length, block):
        query_block = query_head[start : start + block]
        grad_block = out_grad[start : start + block]
        scores = product_right(query_block, key_head) * scale
        scores = jnp.where(allowed_block(segment_ids, start, block), scores, NEGATIVE)
        probability = jnp.exp(scores - log_total[start : start + block, None])
        prob_grad = product_right(grad_block, value_head)
        delta = jnp.sum(probability * prob_grad, axis=-1, keepdims=True)
        score_grad = (probability * (prob_grad - delta)).astype(jnp.bfloat16)
        query_parts.append(product(score_grad, key_head) * scale)
        key_grad = key_grad + product_left(score_grad, query_block) * scale
        value_grad = value_grad + product_left(probability.astype(jnp.bfloat16), grad_block)
    return (jnp.concatenate(query_parts, axis=0), key_grad, value_grad)


def on_device(
    tokens,
    segments,
    positions,
    norm_input,
    norm_query,
    norm_latent,
    norm_hidden,
    query_down,
    latent_down,
    query_up,
    latent_up,
    attention_out,
    gate_weight,
    up_weight,
    down_weight,
    cotangent,
):
    local_rows = tokens.shape[0]
    shard = lax.axis_index("tensor")
    offset = shard * local_rows
    length = segments.shape[0]
    local_heads = HEADS // lax.axis_size("tensor")
    width = NOPE + ROPE
    scale = 1.0 / math.sqrt(width)
    gain_in, gain_query, gain_latent, gain_hidden, query_down_all, latent_down_all = (
        lax.all_gather(norm_input, ("fsdp", "tensor"), axis=0, tiled=True),
        lax.all_gather(norm_query, ("fsdp", "tensor"), axis=0, tiled=True),
        lax.all_gather(norm_latent, ("fsdp", "tensor"), axis=0, tiled=True),
        lax.all_gather(norm_hidden, ("fsdp", "tensor"), axis=0, tiled=True),
        lax.all_gather(query_down, ("fsdp", "tensor"), axis=0, tiled=True),
        lax.all_gather(latent_down, ("fsdp", "tensor"), axis=0, tiled=True),
    )
    gain_in = gain_in.astype(jnp.float32)
    gain_query = gain_query.astype(jnp.float32)
    gain_latent = gain_latent.astype(jnp.float32)
    gain_hidden = gain_hidden.astype(jnp.float32)
    head_weights = (
        lax.all_gather(query_up, "fsdp", axis=0, tiled=True),
        lax.all_gather(latent_up, "fsdp", axis=0, tiled=True),
        lax.all_gather(attention_out, "fsdp", axis=1, tiled=True),
        lax.all_gather(gate_weight, "fsdp", axis=0, tiled=True),
        lax.all_gather(up_weight, "fsdp", axis=0, tiled=True),
        lax.all_gather(down_weight, "fsdp", axis=1, tiled=True),
    )
    query_up_all, latent_up_all, attention_out_all, gate_all, up_all, down_all = head_weights
    token_values = tokens.astype(jnp.float32)
    attention_normed, inverse_in = normalize(token_values, gain_in)
    attention_input = attention_normed.astype(jnp.bfloat16)
    query_latent = product(attention_input, query_down_all)
    latent_all = product(attention_input, latent_down_all)
    query_normed, inverse_query = normalize(query_latent, gain_query)
    key_part = latent_all[:, :KVR]
    latent_normed, inverse_latent = normalize(key_part, gain_latent)
    local_positions = lax.dynamic_slice_in_dim(positions, offset, local_rows)
    cosine_local, sine_local = rotary_tables(local_positions)
    key_rotated = rotate(latent_all[:, KVR:], cosine_local, sine_local)
    latent_send = jnp.concatenate([latent_normed, key_rotated], axis=1).astype(jnp.bfloat16)
    query_seq, latent_seq = (
        lax.all_gather(query_normed.astype(jnp.bfloat16), "tensor", axis=0, tiled=True),
        lax.all_gather(latent_send, "tensor", axis=0, tiled=True),
    )
    cosine_all, sine_all = rotary_tables(positions)
    query_raw = product(query_seq, query_up_all).reshape(length, local_heads, width)
    query_heads = jnp.concatenate(
        [
            query_raw[..., :NOPE],
            rotate(query_raw[..., NOPE:], cosine_all[:, None, :], sine_all[:, None, :]),
        ],
        axis=-1,
    ).astype(jnp.bfloat16)
    key_value = (
        product(latent_seq[:, :KVR], latent_up_all)
        .reshape(length, local_heads, NOPE + VDIM)
        .astype(jnp.bfloat16)
    )
    key_rope = jnp.broadcast_to(latent_seq[:, None, KVR:], (length, local_heads, ROPE))
    key_heads = jnp.concatenate([key_value[..., :NOPE], key_rope], axis=-1)
    value_heads = key_value[..., NOPE:]
    query_major = jnp.transpose(query_heads, (1, 0, 2))
    key_major = jnp.transpose(key_heads, (1, 0, 2))
    value_major = jnp.transpose(value_heads, (1, 0, 2))

    def forward_head(item):
        return head_forward(item[0], item[1], item[2], segments, scale)

    head_out, log_totals = lax.map(forward_head, (query_major, key_major, value_major))
    heads = (
        jnp.transpose(head_out, (1, 0, 2)).reshape(length, local_heads * VDIM).astype(jnp.bfloat16)
    )
    attention_branch = lax.psum_scatter(
        product(heads, attention_out_all).astype(jnp.bfloat16),
        "tensor",
        scatter_dimension=0,
        tiled=True,
    ).astype(jnp.float32)
    hidden = token_values + RESIDUAL * attention_branch
    feed_normed, inverse_hidden = normalize(hidden, gain_hidden)
    feed_seq = lax.all_gather(feed_normed.astype(jnp.bfloat16), "tensor", axis=0, tiled=True)
    gate = product(feed_seq, gate_all)
    up_values = product(feed_seq, up_all)
    sigmoid = jax.nn.sigmoid(gate)
    swish = gate * sigmoid
    activated = (swish * up_values).astype(jnp.bfloat16)
    feed_branch = lax.psum_scatter(
        product(activated, down_all).astype(jnp.bfloat16), "tensor", scatter_dimension=0, tiled=True
    ).astype(jnp.float32)
    output = (hidden + RESIDUAL * feed_branch).astype(jnp.bfloat16)
    backward_weights = (
        lax.all_gather(query_up, "fsdp", axis=0, tiled=True),
        lax.all_gather(latent_up, "fsdp", axis=0, tiled=True),
        lax.all_gather(attention_out, "fsdp", axis=1, tiled=True),
        lax.all_gather(gate_weight, "fsdp", axis=0, tiled=True),
        lax.all_gather(up_weight, "fsdp", axis=0, tiled=True),
        lax.all_gather(down_weight, "fsdp", axis=1, tiled=True),
    )
    query_up_back, latent_up_back, attention_out_back, gate_back, up_back, down_back = (
        backward_weights
    )
    upstream = cotangent.astype(jnp.float32)
    feed_upstream = lax.all_gather(
        (RESIDUAL * upstream).astype(jnp.bfloat16), "tensor", axis=0, tiled=True
    )
    activated_grad = product_right(feed_upstream, down_back)
    grad_down = product_left(activated, feed_upstream)
    slope = sigmoid * (1.0 + gate * (1.0 - sigmoid))
    gate_grad = (activated_grad * up_values * slope).astype(jnp.bfloat16)
    up_grad = (activated_grad * swish).astype(jnp.bfloat16)
    grad_gate = product_left(feed_seq, gate_grad)
    grad_up = product_left(feed_seq, up_grad)
    feed_terms = product_right(gate_grad, gate_back) + product_right(up_grad, up_back)
    feed_input_grad = lax.psum_scatter(feed_terms, "tensor", scatter_dimension=0, tiled=True)
    hidden_back, grad_gain_hidden = normalize_back(
        hidden, inverse_hidden, gain_hidden, feed_input_grad
    )
    hidden_grad = upstream + hidden_back
    attention_upstream = lax.all_gather(
        (RESIDUAL * hidden_grad).astype(jnp.bfloat16), "tensor", axis=0, tiled=True
    )
    grad_attention = product_left(heads, attention_upstream)
    heads_grad = product_right(attention_upstream, attention_out_back).astype(jnp.bfloat16)
    grad_major = jnp.transpose(heads_grad.reshape(length, local_heads, VDIM), (1, 0, 2))

    def backward_head(item):
        return head_backward(item[0], item[1], item[2], item[3], item[4], segments, scale)

    query_grad, key_grad, value_grad = lax.map(
        backward_head, (query_major, key_major, value_major, grad_major, log_totals)
    )
    query_grad = jnp.transpose(query_grad, (1, 0, 2))
    key_grad = jnp.transpose(key_grad, (1, 0, 2))
    value_grad = jnp.transpose(value_grad, (1, 0, 2))
    query_raw_grad = (
        jnp.concatenate(
            [
                query_grad[..., :NOPE],
                rotate(query_grad[..., NOPE:], cosine_all[:, None, :], -sine_all[:, None, :]),
            ],
            axis=-1,
        )
        .astype(jnp.bfloat16)
        .reshape(length, local_heads * width)
    )
    key_value_grad = (
        jnp.concatenate([key_grad[..., :NOPE], value_grad], axis=-1)
        .astype(jnp.bfloat16)
        .reshape(length, local_heads * (NOPE + VDIM))
    )
    key_rope_grad = jnp.sum(key_grad[..., NOPE:], axis=1)
    grad_query_up = product_left(query_seq, query_raw_grad)
    grad_latent_up = product_left(latent_seq[:, :KVR], key_value_grad)
    query_terms = product_right(query_raw_grad, query_up_back)
    latent_terms = jnp.concatenate(
        [product_right(key_value_grad, latent_up_back), key_rope_grad], axis=1
    )
    query_back, latent_back = (
        lax.psum_scatter(
            query_terms.astype(jnp.bfloat16), "tensor", scatter_dimension=0, tiled=True
        ).astype(jnp.float32),
        lax.psum_scatter(
            latent_terms.astype(jnp.bfloat16), "tensor", scatter_dimension=0, tiled=True
        ).astype(jnp.float32),
    )
    query_latent_back, grad_gain_query = normalize_back(
        query_latent, inverse_query, gain_query, query_back
    )
    latent_part_back, grad_gain_latent = normalize_back(
        key_part, inverse_latent, gain_latent, latent_back[:, :KVR]
    )
    rope_back = rotate(latent_back[:, KVR:], cosine_local, -sine_local)
    query_latent_grad = query_latent_back.astype(jnp.bfloat16)
    latent_all_grad = jnp.concatenate([latent_part_back, rope_back], axis=1).astype(jnp.bfloat16)
    grad_query_down = product_left(attention_input, query_latent_grad)
    grad_latent_down = product_left(attention_input, latent_all_grad)
    input_grad = product_right(query_latent_grad, query_down_all) + product_right(
        latent_all_grad, latent_down_all
    )
    token_back, grad_gain_input = normalize_back(token_values, inverse_in, gain_in, input_grad)
    token_grad = hidden_grad + token_back
    shared = (
        lax.psum_scatter(grad_gain_input, ("fsdp", "tensor"), scatter_dimension=0, tiled=True),
        lax.psum_scatter(grad_gain_query, ("fsdp", "tensor"), scatter_dimension=0, tiled=True),
        lax.psum_scatter(grad_gain_latent, ("fsdp", "tensor"), scatter_dimension=0, tiled=True),
        lax.psum_scatter(grad_gain_hidden, ("fsdp", "tensor"), scatter_dimension=0, tiled=True),
        lax.psum_scatter(grad_query_down, ("fsdp", "tensor"), scatter_dimension=0, tiled=True),
        lax.psum_scatter(grad_latent_down, ("fsdp", "tensor"), scatter_dimension=0, tiled=True),
    )
    owned = (
        lax.psum_scatter(
            grad_query_up.astype(jnp.bfloat16), "fsdp", scatter_dimension=0, tiled=True
        ).astype(jnp.float32),
        lax.psum_scatter(
            grad_latent_up.astype(jnp.bfloat16), "fsdp", scatter_dimension=0, tiled=True
        ).astype(jnp.float32),
        lax.psum_scatter(
            grad_attention.astype(jnp.bfloat16), "fsdp", scatter_dimension=1, tiled=True
        ).astype(jnp.float32),
        lax.psum_scatter(
            grad_gate.astype(jnp.bfloat16), "fsdp", scatter_dimension=0, tiled=True
        ).astype(jnp.float32),
        lax.psum_scatter(
            grad_up.astype(jnp.bfloat16), "fsdp", scatter_dimension=0, tiled=True
        ).astype(jnp.float32),
        lax.psum_scatter(
            grad_down.astype(jnp.bfloat16), "fsdp", scatter_dimension=1, tiled=True
        ).astype(jnp.float32),
    )
    return (
        output,
        token_grad,
        shared[0],
        shared[1],
        shared[2],
        shared[3],
        shared[4],
        shared[5],
        owned[0],
        owned[1],
        owned[2],
        owned[3],
        owned[4],
        owned[5],
    )


def solution(mesh):
    return jax.shard_map(
        on_device,
        mesh=mesh,
        in_specs=(
            P(("fsdp", "tensor"), None),
            P("fsdp"),
            P("fsdp"),
            P(("fsdp", "tensor")),
            P(("fsdp", "tensor")),
            P(("fsdp", "tensor")),
            P(("fsdp", "tensor")),
            P(("fsdp", "tensor"), None),
            P(("fsdp", "tensor"), None),
            P("fsdp", "tensor"),
            P("fsdp", "tensor"),
            P("tensor", "fsdp"),
            P("fsdp", "tensor"),
            P("fsdp", "tensor"),
            P("tensor", "fsdp"),
            P(("fsdp", "tensor"), None),
        ),
        out_specs=(
            P(("fsdp", "tensor"), None),
            P(("fsdp", "tensor"), None),
            P(("fsdp", "tensor")),
            P(("fsdp", "tensor")),
            P(("fsdp", "tensor")),
            P(("fsdp", "tensor")),
            P(("fsdp", "tensor"), None),
            P(("fsdp", "tensor"), None),
            P("fsdp", "tensor"),
            P("fsdp", "tensor"),
            P("tensor", "fsdp"),
            P("fsdp", "tensor"),
            P("fsdp", "tensor"),
            P("tensor", "fsdp"),
        ),
        check_vma=False,
    )
```

profile of v0, /device:TPU:0, one launch (start us, length us, event | category | flops | bytes accessed | tf_op | source)
XLA Modules:
  0.0 2229.1 jit_solution(4724872847959447182)
XLA Ops:
  12.9 42.3 %all-reduce.9 = (bf16[2560]{0:T(1024)(128)(2,1)S(1)}, bf16[2560]{0:T(1024)(128)(2,1)S(1)}, bf16[768]{0:T(1024)(128)(2,1)S(1)}, bf16[256]{0:T(256)(128)(2,1)S(1)}) all-reduce(bf16[2560]{0:T(1024)(128)(2,1)S(1)} %dynamic-update-slice.3, bf16[2560]{0:T(1024)(128)(2,1)S(1)} %dynamic-update-slice, ...), channel_id=1, replica_groups=mesh['fsdp'=8,'tensor'=4] {'fsdp','tensor'}, use_global_device_ids=true, to_apply=%add.3 | all-reduce | flops 6144 | bytes 24576
  57.5 17.4 all-gather.12.cloned.1.call-done
  74.9 3.9 multiply_reduce_fusion.5
  81.4 32.0 %all_gather.65 = bf16[256,1280]{1,0:T(8,128)(2,1)S(1)} all-gather(bf16[32,1280]{1,0:T(8,128)(2,1)S(1)} %copy-done.32), channel_id=1, replica_groups=mesh['fsdp'=8,'tensor'=4] {'fsdp'}, dimensions={0}, use_global_device_ids=true | all-gather | bytes 737280 | tf_op jit(solution)/shard_map/all_gather | solution.py:152
  114.4 18.7 all-gather.18.cloned.1.call-done
  136.5 7.6 all_gather.64
  146.4 4.7 copy.44
  151.1 3.1 slice_bitcast_fusion
  157.1 3.8 copy.47
  160.9 17.4 all-gather.16.cloned.1.call-done
  178.3 20.5 all-gather.14.cloned.1.call-done
  198.8 3.6 fusion.110
  206.9 98.0 %while.26 = (s32[]{:T(128)}, bf16[10,1024,64]{1,2,0:T(8,128)(2,1)}, f32[10,1024]{1,0:T(8,128)S(1)}, s32[1024]{0:T(1024)S(1)}, bf16[10,1024,96]{2,1,0:T(8,128)(2,...) while((s32[]{:T(128)}, bf16[10,1024,64]{1,2,0:T(8,128)(2,1)}, ...), condition=%wide.region_8.9_spmd, body=%wide.region_3.8_spmd.sunk | while | flops 347341312 | bytes 31141552 | solution.py:199
  304.9 8.9 convolution_convert_fusion.4
  315.0 50.3 %reduce-scatter.14.cloned.1.call-done = bf16[256,2560]{1,0:T(8,128)(2,1)} async-done(((bf16[1024,2560]{1,0:T(8,128)(2,1)}), bf16[256,2560]{1,0:T(8,128)(2,1)}) %reduce-scatter.14.cloned.1.call-update) | async-done | bytes 1310736 | tf_op jit(solution)/shard_map/reduce_scatter | solution.py:203
  373.2 121.2 %all-gather.24.cloned.1.call-done = bf16[2560,1600]{1,0:T(8,128)(2,1)} async-done(((bf16[320,1600]{1,0:T(8,128)(2,1)}), bf16[2560,1600]{1,0:T(8,128)(2,1)}) %all-gather.24.cloned.1.call-update) | async-done | bytes 8192016 | tf_op jit(solution)/shard_map/all_gather | solution.py:154
  494.4 40.9 %all-gather.22.cloned.1.call-done = bf16[1024,2560]{1,0:T(8,128)(2,1)} async-done(((bf16[256,2560]{1,0:T(8,128)(2,1)}), bf16[1024,2560]{1,0:T(8,128)(2,1)}) %all-gather.22.cloned.1.call-update) | async-done | bytes 5242896 | tf_op jit(solution)/shard_map/all_gather | solution.py:211
  535.3 14.9 fusion.111
  550.1 114.2 %all-gather.26.cloned.1.call-done = bf16[2560,1600]{1,0:T(8,128)(2,1)} async-done(((bf16[320,1600]{1,0:T(8,128)(2,1)}), bf16[2560,1600]{1,0:T(8,128)(2,1)}) %all-gather.26.cloned.1.call-update) | async-done | bytes 8192016 | tf_op jit(solution)/shard_map/all_gather | solution.py:155
  664.4 14.9 fusion.112
  679.2 25.8 %all-gather.30.cloned.1.call-done = bf16[1024,2560]{1,0:T(8,128)(2,1)} async-done(((bf16[256,2560]{1,0:T(8,128)(2,1)}), bf16[1024,2560]{1,0:T(8,128)(2,1)}) %all-gather.30.cloned.1.call-update) | async-done | bytes 5242896 | tf_op jit(solution)/shard_map/all_gather | solution.py:233
  705.1 129.1 %all-gather.28.cloned.1.call-done = bf16[1600,2560]{0,1:T(8,128)(2,1)} async-done(((bf16[1600,320]{0,1:T(8,128)(2,1)}), bf16[1600,2560]{0,1:T(8,128)(2,1)}) %all-gather.28.cloned.1.call-update) | async-done | bytes 8192016 | tf_op jit(solution)/shard_map/all_gather | solution.py:156
  834.2 21.2 multiply_convert_fusion.2
  855.4 13.2 fusion.113
  868.6 15.8 convolution_add_fusion.2
  884.5 83.6 %reduce-scatter.18.cloned.1.call-done = f32[256,2560]{1,0:T(8,128)} async-done(((f32[1024,2560]{1,0:T(8,128)}), f32[256,2560]{1,0:T(8,128)}) %reduce-scatter.18.cloned.1.call-update) | async-done | bytes 2621456 | tf_op jit(solution)/shard_map/reduce_scatter | solution.py:244
  968.1 3.6 multiply_reduce_fusion.2
  974.3 40.5 %all-gather.32.cloned.1.call-done = bf16[1024,2560]{1,0:T(8,128)(2,1)} async-done(((bf16[256,2560]{1,0:T(8,128)(2,1)}), bf16[1024,2560]{1,0:T(8,128)(2,1)}) %all-gather.32.cloned.1.call-update) | async-done | bytes 5242896 | tf_op jit(solution)/shard_map/all_gather | solution.py:249
  1014.8 7.1 convolution_convert_fusion.10
  1025.1 168.9 %while.27 = (s32[]{:T(128)}, f32[10,1024,96]{1,2,0:T(8,128)}, f32[10,1024,96]{1,2,0:T(8,128)}, bf16[10,1024,64]{1,2,0:T(8,128)(2,1)S(1)}, s32[1024]{0:T(1024)S(1...) while((s32[]{:T(128)}, f32[10,1024,96]{1,2,0:T(8,128)}, ...), condition=%wide.region_17.18_spmd, body=%wide.region_14.17_spmd.sunk | while | flops 885456384 | bytes 37278368 | solution.py:259
  1209.2 13.9 convolution_convert_fusion.2
  1225.0 13.7 convolution_convert_fusion.1
  1240.6 13.9 convolution_convert_fusion
  1258.2 5.2 convolution_convert_fusion.8
  1263.5 14.7 convolution_convert_fusion.3
  1279.5 8.5 convolution_convert_fusion.5
  1295.0 5.6 fusion.97
  1300.6 108.7 %reduce-scatter.34.cloned.1.call-done = bf16[320,1600]{1,0:T(8,128)(2,1)} async-done(((bf16[2560,1600]{1,0:T(8,128)(2,1)}), bf16[320,1600]{1,0:T(8,128)(2,1)}) %reduce-scatter.34.cloned.1.call-update) | async-done | bytes 1024016 | tf_op jit(solution)/shard_map/reduce_scatter | solution.py:330
  1412.0 151.5 %reduce-scatter.36.cloned.1.call-done = bf16[320,1600]{1,0:T(8,128)(2,1)} async-done(((bf16[2560,1600]{1,0:T(8,128)(2,1)}), bf16[320,1600]{1,0:T(8,128)(2,1)}) %reduce-scatter.36.cloned.1.call-update) | async-done | bytes 1024016 | tf_op jit(solution)/shard_map/reduce_scatter | solution.py:333
  1566.3 151.1 %reduce-scatter.38.cloned.1.call-done = bf16[1600,320]{0,1:T(8,128)(2,1)} async-done(((bf16[1600,2560]{0,1:T(8,128)(2,1)}), bf16[1600,320]{0,1:T(8,128)(2,1)}) %reduce-scatter.38.cloned.1.call-update) | async-done | bytes 1024016 | tf_op jit(solution)/shard_map/reduce_scatter | solution.py:336
  1720.1 62.0 %reduce-scatter.30.cloned.1.call-done = bf16[32,1280]{1,0:T(8,128)(2,1)} async-done(((bf16[256,1280]{1,0:T(8,128)(2,1)}), bf16[32,1280]{1,0:T(8,128)(2,1)}) %reduce-scatter.30.cloned.1.call-update) | async-done | bytes 81936 | tf_op jit(solution)/shard_map/reduce_scatter | solution.py:324
  1783.7 66.2 %reduce-scatter.28.cloned.1.call-done = bf16[96,960]{1,0:T(8,128)(2,1)} async-done(((bf16[768,960]{1,0:T(8,128)(2,1)}), bf16[96,960]{1,0:T(8,128)(2,1)}) %reduce-scatter.28.cloned.1.call-update) | async-done | bytes 184336 | tf_op jit(solution)/shard_map/reduce_scatter | solution.py:321
  1851.6 3.5 fusion.108
  1858.0 40.4 %all-reduce.8 = (f32[2560]{0:T(1024)S(1)}, f32[768]{0:T(1024)S(1)}, f32[256]{0:T(256)S(1)}, f32[2560]{0:T(1024)S(1)}) all-reduce(f32[2560]{0:T(1024)S(1)} %get-tuple-element.164, f32[768]{0:T(1024)S(1)} %get-tuple-element.166, f32[256]{0:T(256)S(1)} %get-tuple-element.168, ...), channel_id=7, replica_groups=mesh['fsdp'=8,'tensor'=4] {'fsdp','tensor'}, use_global_device_ids=true, to_apply=%region_25.26.clone | all-reduce | flops 6144 | bytes 49152
  1903.7 6.0 fusion.62
  1909.7 73.7 %reduce-scatter.32.cloned.1.call-done = bf16[640,320]{0,1:T(8,128)(2,1)} async-done(((bf16[640,2560]{0,1:T(8,128)(2,1)}), bf16[640,320]{0,1:T(8,128)(2,1)}) %reduce-scatter.32.cloned.1.call-update) | async-done | bytes 409616 | tf_op jit(solution)/shard_map/reduce_scatter | solution.py:327
  1985.4 107.9 %reduce-scatter.26.cloned.1.call-done = f32[80,288]{1,0:T(8,128)} async-done(((f32[2560,288]{1,0:T(8,128)}), f32[80,288]{1,0:T(8,128)}) %reduce-scatter.26.cloned.1.call-update) | async-done | bytes 92176 | tf_op jit(solution)/shard_map/reduce_scatter | solution.py:318
  2093.4 128.4 %reduce-scatter.24.cloned.1.call-done = f32[80,768]{1,0:T(8,128)} async-done(((f32[2560,768]{1,0:T(8,128)}), f32[80,768]{1,0:T(8,128)}) %reduce-scatter.24.cloned.1.call-update) | async-done | bytes 245776 | tf_op jit(solution)/shard_map/reduce_scatter | solution.py:317
  (558 shorter events, 356.8 us)
Async XLA Ops:
  7.2 67.7 %all-gather.12.cloned.1.call-start = ((), (), s32[]{:S(2)}) async-start(), calls=%async_computation.13 | async-start | bytes 4055040 | tf_op jit(solution)/shard_map/all_gather | solution.py:143
  7.9 125.2 %all-gather.18.cloned.1.call-start = ((), (), s32[]{:S(2)}) async-start(), calls=%async_computation.16 | async-start | bytes 2027520 | tf_op jit(solution)/shard_map/all_gather | solution.py:144
  8.7 169.7 %all-gather.16.cloned.1.call-start = ((), (), s32[]{:S(2)}) async-start(), calls=%async_computation.15 | async-start | bytes 1769472 | tf_op jit(solution)/shard_map/all_gather | solution.py:151
  9.4 189.4 %all-gather.14.cloned.1.call-start = ((), (), s32[]{:S(2)}) async-start(), calls=%async_computation.14 | async-start | bytes 1966080 | tf_op jit(solution)/shard_map/all_gather | solution.py:172
  55.2 77.9 %copy-start.22 = (f32[2560]{0:T(1024)}, f32[2560]{0:T(1024)S(1)}, u32[]{:S(2)}) copy-start(f32[2560]{0:T(1024)S(1)} %convert_element_type.162) | copy-start | bytes 30724
  55.2 24.2 %copy-start.30 = (f32[768]{0:T(1024)}, f32[768]{0:T(1024)S(1)}, u32[]{:S(2)}) copy-start(f32[768]{0:T(1024)S(1)} %convert_element_type.164) | copy-start | bytes 9220
  57.5 75.6 %copy-start.35 = (f32[256]{0:T(256)}, f32[256]{0:T(256)S(1)}, u32[]{:S(2)}) copy-start(f32[256]{0:T(256)S(1)} %get-tuple-element.247) | copy-start | bytes 3076
  74.9 6.3 copy-start.51
  74.9 6.5 copy-start.32
  78.8 54.3 %copy-start = (bf16[256,2560]{1,0:T(8,128)(2,1)S(1)}, bf16[256,2560]{1,0:T(8,128)(2,1)}, u32[]{:S(2)}) copy-start(bf16[256,2560]{1,0:T(8,128)(2,1)} %param.20) | copy-start | bytes 3932164
  80.6 224.3 %all-gather.20.cloned.1.call-start = ((), (), s32[]{:S(2)}) async-start(), calls=%async_computation.17 | async-start | bytes 3686400 | tf_op jit(solution)/shard_map/all_gather | solution.py:153
  81.1 284.2 %reduce-scatter.14.cloned.1.call-start = ((), (), s32[]{:S(2)}) async-start(), calls=%async_computation.18 | async-start | bytes 6553600 | tf_op jit(solution)/shard_map/reduce_scatter | solution.py:203
  81.2 55.0 %copy-start.52 = (f32[16]{0:T(128)}, f32[16]{0:T(128)S(1)}, u32[]{:S(2)}) copy-start(f32[16]{0:T(128)S(1)} %multiply_exponential_fusion) | copy-start | bytes 196
  81.3 55.1 %copy-start.43 = (f32[256]{0:T(256)}, f32[256]{0:T(256)S(1)}, u32[]{:S(2)}) copy-start(f32[256]{0:T(256)S(1)} %convert_element_type.167) | copy-start | bytes 3076
  81.4 54.8 %copy-start.49 = (f32[256]{0:T(256)}, f32[256]{0:T(256)S(1)}, u32[]{:S(2)}) copy-start(f32[256]{0:T(256)S(1)} %dynamic-slice_convert_fusion) | copy-start | bytes 3076
  113.4 30.6 %copy-start.15 = (bf16[256,1280]{1,0:T(8,128)(2,1)}, bf16[256,1280]{1,0:T(8,128)(2,1)S(1)}, u32[]{:S(2)}) copy-start(bf16[256,1280]{1,0:T(8,128)(2,1)S(1)} %all_gather.65) | copy-start | bytes 1966084
  114.4 88.3 %copy-start.24 = (f32[1024,16]{0,1:T(8,128)}, f32[1024,16]{0,1:T(8,128)S(1)}, u32[]{:S(2)}) copy-start(f32[1024,16]{0,1:T(8,128)S(1)} %get-tuple-element.245) | copy-start | bytes 196612
  136.2 10.3 copy-start.41
  144.0 7.1 copy-start.17
  313.8 180.6 %all-gather.24.cloned.1.call-start = ((), (), s32[]{:S(2)}) async-start(), calls=%async_computation.20 | async-start | bytes 9584640 | tf_op jit(solution)/shard_map/all_gather | solution.py:154
  314.5 220.7 %all-gather.22.cloned.1.call-start = ((), (), s32[]{:S(2)}) async-start(), calls=%async_computation.19 | async-start | bytes 6553600 | tf_op jit(solution)/shard_map/all_gather | solution.py:211
  315.0 656.7 %copy-start.27 = (f32[2560]{0:T(1024)}, f32[2560]{0:T(1024)S(1)}, u32[]{:S(2)}) copy-start(f32[2560]{0:T(1024)S(1)} %convert_element_type.176) | copy-start | bytes 30724
  367.3 604.3 %copy-start.39 = (f32[256]{0:T(256)}, f32[256]{0:T(256)S(1)}, u32[]{:S(2)}) copy-start(f32[256]{0:T(256)S(1)} %get-tuple-element.253) | copy-start | bytes 3076
  367.4 604.3 %copy-start.45 = (f32[256]{0:T(256)}, f32[256]{0:T(256)S(1)}, u32[]{:S(2)}) copy-start(f32[256]{0:T(256)S(1)} %get-tuple-element.252) | copy-start | bytes 3076
  369.0 295.3 %all-gather.26.cloned.1.call-start = ((), (), s32[]{:S(2)}) async-start(), calls=%async_computation.21 | async-start | bytes 9584640 | tf_op jit(solution)/shard_map/all_gather | solution.py:155
  369.8 335.3 %all-gather.30.cloned.1.call-start = ((), (), s32[]{:S(2)}) async-start(), calls=%async_computation.24 | async-start | bytes 6553600 | tf_op jit(solution)/shard_map/all_gather | solution.py:233
  372.4 461.7 %all-gather.28.cloned.1.call-start = ((), (), s32[]{:S(2)}) async-start(), calls=%async_computation.22 | async-start | bytes 9584640 | tf_op jit(solution)/shard_map/all_gather | solution.py:156
  373.2 595.0 %reduce-scatter.18.cloned.1.call-start = ((), (), s32[]{:S(2)}) async-start(), calls=%async_computation.25 | async-start | bytes 13107200 | tf_op jit(solution)/shard_map/reduce_scatter | solution.py:244
  884.5 130.3 %all-gather.32.cloned.1.call-start = ((), (), s32[]{:S(2)}) async-start(), calls=%async_computation.26 | async-start | bytes 6553600 | tf_op jit(solution)/shard_map/all_gather | solution.py:249
  974.2 314.0 %reduce-scatter.22.cloned.1.call-start = ((), (), s32[]{:S(2)}) async-start(), calls=%async_computation.28 | async-start | bytes 737280 | tf_op jit(solution)/shard_map/reduce_scatter | solution.py:292
  1201.0 92.0 %reduce-scatter.20.cloned.1.call-start = ((), (), s32[]{:S(2)}) async-start(), calls=%async_computation.27 | async-start | bytes 1966080 | tf_op jit(solution)/shard_map/reduce_scatter | solution.py:289
  1209.1 200.2 %reduce-scatter.34.cloned.1.call-start = ((), (), s32[]{:S(2)}) async-start(), calls=%async_computation.34 | async-start | bytes 9584640 | tf_op jit(solution)/shard_map/reduce_scatter | solution.py:330
  1223.1 340.5 %reduce-scatter.36.cloned.1.call-start = ((), (), s32[]{:S(2)}) async-start(), calls=%async_computation.35 | async-start | bytes 9584640 | tf_op jit(solution)/shard_map/reduce_scatter | solution.py:333
  1238.7 478.7 %reduce-scatter.38.cloned.1.call-start = ((), (), s32[]{:S(2)}) async-start(), calls=%async_computation.36 | async-start | bytes 9584640 | tf_op jit(solution)/shard_map/reduce_scatter | solution.py:336
  1254.6 527.5 %reduce-scatter.30.cloned.1.call-start = ((), (), s32[]{:S(2)}) async-start(), calls=%async_computation.32 | async-start | bytes 737280 | tf_op jit(solution)/shard_map/reduce_scatter | solution.py:324
  1258.2 5.3 copy-start.60
  1258.2 591.7 %reduce-scatter.28.cloned.1.call-start = ((), (), s32[]{:S(2)}) async-start(), calls=%async_computation.31 | async-start | bytes 1769472 | tf_op jit(solution)/shard_map/reduce_scatter | solution.py:321
  1263.4 640.3 %reduce-scatter.16.cloned.1.call-start = ((), (), s32[]{:S(2)}) async-start(), calls=%async_computation.23 | async-start | bytes 6553600 | tf_op jit(solution)/shard_map/reduce_scatter | solution.py:217
  1278.2 705.3 %reduce-scatter.32.cloned.1.call-start = ((), (), s32[]{:S(2)}) async-start(), calls=%async_computation.33 | async-start | bytes 3686400 | tf_op jit(solution)/shard_map/reduce_scatter | solution.py:327
  1288.1 805.3 %reduce-scatter.26.cloned.1.call-start = ((), (), s32[]{:S(2)}) async-start(), calls=%async_computation.30 | async-start | bytes 4055040 | tf_op jit(solution)/shard_map/reduce_scatter | solution.py:318
  1292.6 929.2 %reduce-scatter.24.cloned.1.call-start = ((), (), s32[]{:S(2)}) async-start(), calls=%async_computation.29 | async-start | bytes 8110080 | tf_op jit(solution)/shard_map/reduce_scatter | solution.py:317
  1566.3 285.3 %copy-start.12 = (bf16[256,768]{1,0:T(8,128)(2,1)S(1)}, bf16[256,768]{1,0:T(8,128)(2,1)}, u32[]{:S(2)}) copy-start(bf16[256,768]{1,0:T(8,128)(2,1)} %reduce-scatter.20.cloned.1.call-done) | copy-start | bytes 1179652
  1855.2 48.6 %copy-start.5 = (bf16[256,2560]{1,0:T(8,128)(2,1)S(1)}, bf16[256,2560]{1,0:T(8,128)(2,1)}, u32[]{:S(2)}) copy-start(bf16[256,2560]{1,0:T(8,128)(2,1)} %reduce-scatter.14.cloned.1.call-done) | copy-start | bytes 3932164
  1855.2 48.5 %copy-start.28 = (f32[2560]{0:T(1024)S(1)}, f32[2560]{0:T(1024)}, u32[]{:S(2)}) copy-start(f32[2560]{0:T(1024)} %copy-done.27) | copy-start | bytes 30724
  1855.2 48.5 %copy-start.40 = (f32[256]{0:T(256)S(1)}, f32[256]{0:T(256)}, u32[]{:S(2)}) copy-start(f32[256]{0:T(256)} %copy-done.39) | copy-start | bytes 3076
  1855.2 48.5 %copy-start.46 = (f32[256]{0:T(256)S(1)}, f32[256]{0:T(256)}, u32[]{:S(2)}) copy-start(f32[256]{0:T(256)} %copy-done.45) | copy-start | bytes 3076
  1855.2 48.5 %copy-start.48 = (f32[256]{0:T(256)S(1)}, f32[256]{0:T(256)}, u32[]{:S(2)}) copy-start(f32[256]{0:T(256)} %copy-done.47) | copy-start | bytes 3076
  1855.2 48.5 %copy-start.54 = (f32[256]{0:T(256)S(1)}, f32[256]{0:T(256)}, u32[]{:S(2)}) copy-start(f32[256]{0:T(256)} %get-tuple-element.246) | copy-start | bytes 3076
  (56 other events, 103.4 us)
Sparse Core Ops, SparseCore 0:
  10.9 63.9 all-gather.11
  77.8 55.2 all-gather.17
  135.3 43.0 all-gather.15
  180.3 18.4 all-gather.13
  200.8 61.9 all-gather.19
  313.9 51.3 reduce-scatter.13
  367.7 126.6 all-gather.23
  496.6 38.6 all-gather.21
  537.7 126.6 all-gather.25
  666.4 38.6 all-gather.29
  707.5 126.6 all-gather.27
  884.6 83.4 reduce-scatter.17
  974.3 40.4 all-gather.31
  1201.1 22.0 reduce-scatter.21
  1226.3 28.1 reduce-scatter.19
  1258.0 151.3 reduce-scatter.33
  1413.2 150.3 reduce-scatter.35
  1567.0 150.3 reduce-scatter.37
  1721.0 61.0 reduce-scatter.29
  1785.9 63.9 reduce-scatter.27
  1852.6 51.0 reduce-scatter.15
  1907.3 76.1 reduce-scatter.31
  1990.3 102.9 reduce-scatter.25
  2100.4 121.3 reduce-scatter.23
where the time goes:
time: 2240 us; the launch traced here: 2230 us
  waiting for transfers between devices  1540 us (69%)
  matrix products  417 us (19%)
  blocking collectives  122 us (5%)
  other arithmetic  76.4 us (3%)
  local copies, waits for them, and re-layouts  57 us (3%)
    dot_general x68, matrix products, product_right(): lax.dot_general(left, right, (((1,), (1,)), ((), ())), preferred_element_...  168 us
    reduce_scatter x1, waiting for transfers between devices, on_device(): lax.psum_scatter(grad_up.astype(jnp.bfloat16), 'fsdp', scatter_dimension=...  152 us
    reduce_scatter x1, waiting for transfers between devices, on_device(): lax.psum_scatter(grad_down.astype(jnp.bfloat16), 'fsdp', scatter_dimensio...  151 us
    all_gather x1, waiting for transfers between devices, on_device(): lax.all_gather(down_weight, 'fsdp', axis=1, tiled=True)  129 us
    reduce_scatter x1, waiting for transfers between devices, on_device(): lax.psum_scatter(grad_query_down, ('fsdp', 'tensor'), scatter_dimension=0...  128 us
    dot_general x48, matrix products, product(): return jnp.dot(left, right, preferred_element_type=jnp.float32)  127 us
    dot_general x48, matrix products, product_left(): lax.dot_general(left, right, (((0,), (0,)), ((), ())), preferred_element_...  123 us
    all_gather x1, waiting for transfers between devices, on_device(): lax.all_gather(gate_weight, 'fsdp', axis=0, tiled=True)  121 us
  transfers between devices with their start and end apart: 24, of which 21 were waited for; matrix products, arithmetic and copies ran while one was open for 12% of the time, Pallas kernels for 0%

commit v1 on v0

v1 whole, which is shorter than its diff:
```python
import functools
import math

import jax
import jax.numpy as jnp
from jax import lax
from jax.experimental import pallas as pl
from jax.experimental.pallas import tpu as pltpu
from jax.sharding import PartitionSpec as P

HEADS = 40
NOPE = 64
ROPE = 32
VDIM = 64
KVR = 256
LANES = 128
BLOCK = 256


EPSILON = 1e-05
RESIDUAL = 1.4 / math.sqrt(62.0)
NEGATIVE = -1e30
APART = -(2.0**96)
SCALE = 1.0 / math.sqrt(NOPE + ROPE)
LOG2E = math.log2(math.e)
ROOM = 56 * 1024 * 1024
BRIEF = pl.CostEstimate(flops=1, bytes_accessed=1, transcendentals=0)


def lasting(microseconds):
    return pl.CostEstimate(flops=1, bytes_accessed=microseconds * 3 * 10**6, transcendentals=0)


def normalize(values, gain):
    inverse = lax.rsqrt(jnp.mean(values * values, axis=-1, keepdims=True) + EPSILON)
    return (values * inverse * gain, inverse)


def normalize_back(values, inverse, gain, upstream):
    scaled = upstream * gain
    inner = jnp.mean(scaled * values, axis=-1, keepdims=True)
    return inverse * scaled - values * (inverse * inverse * inverse) * inner


def product(left, right):
    return jnp.dot(left, right, preferred_element_type=jnp.float32)


def product_left(left, right):
    return lax.dot_general(
        left, right, (((0,), (0,)), ((), ())), preferred_element_type=jnp.float32
    )


def product_right(left, right):
    return lax.dot_general(
        left, right, (((1,), (1,)), ((), ())), preferred_element_type=jnp.float32
    )


def rotary_lanes(positions):
    lane = jnp.arange(LANES, dtype=jnp.int32)
    steps = ((lane - NOPE) % (ROPE // 2)).astype(jnp.float32)
    frequency = jnp.exp(steps * (-2.0 * math.log(10000.0) / ROPE))
    angles = positions.astype(jnp.float32)[:, None] * frequency[None, :]
    first = ((lane >= NOPE) & (lane < NOPE + ROPE // 2))[None, :]
    second = ((lane >= NOPE + ROPE // 2) & (lane < NOPE + ROPE))[None, :]
    cosine = jnp.cos(angles)
    sine = jnp.sin(angles)
    here = jnp.where((lane < NOPE)[None, :], 1.0, jnp.where(first | second, cosine, 0.0))
    return (here, jnp.where(first, -sine, 0.0), jnp.where(second, sine, 0.0))


def segment_lanes(segment_ids):
    lane = jnp.arange(LANES, dtype=jnp.int32) - (NOPE + ROPE)
    same = lane[None, :] == segment_ids[:, None]
    used = ((lane >= 0) & (lane < 4))[None, :]
    query = jnp.where(used & same, 1.0, 0.0)
    key = jnp.where(used & ~same, APART, 0.0)
    return (query, key)


def roll_lanes(values, amount):
    return pltpu.roll(values, amount % LANES, 1)


def forward_kernel(
    xq_ref, lat_ref, wq_ref, wkv_ref, rope_ref, feat_ref, here_ref, low_ref, high_ref,
    out_ref, q_ref, kv_ref, lse_ref, k_ref,
):
    length = xq_ref.shape[0]
    lane = lax.broadcasted_iota(jnp.int32, (BLOCK, LANES), 1)
    causal = lax.broadcasted_iota(jnp.int32, (BLOCK, BLOCK), 1) <= lax.broadcasted_iota(
        jnp.int32, (BLOCK, BLOCK), 0
    )
    blocks = [slice(start, start + BLOCK) for start in range(0, length, BLOCK)]
    for rows in blocks:
        q_raw = product(xq_ref[rows, :], wq_ref[...])
        kv_ref[rows, :] = product(lat_ref[rows, :], wkv_ref[...]).astype(jnp.bfloat16)
        for head in range(2):
            part = slice(head * LANES, (head + 1) * LANES)
            raw = q_raw[:, part]
            turned = (
                raw * here_ref[rows, :]
                + roll_lanes(raw, -ROPE // 2) * low_ref[rows, :]
                + roll_lanes(raw, ROPE // 2) * high_ref[rows, :]
                + feat_ref[rows, :]
            )
            q_ref[rows, part] = turned.astype(jnp.bfloat16)
            k_ref[head, rows, :] = jnp.where(lane < NOPE, kv_ref[rows, part], rope_ref[rows, :])
    for rows in blocks:
        results = []
        for head in range(2):
            part = slice(head * LANES, (head + 1) * LANES)
            query = q_ref[rows, part]
            near = product_right(query, k_ref[head, rows, :])
            near = jnp.where(causal, near, NEGATIVE)
            top = jnp.max(near, axis=1, keepdims=True)
            if rows.start:
                far = product_right(query, k_ref[head, : rows.start, :])
                top = jnp.maximum(top, jnp.max(far, axis=1, keepdims=True))
            weights = jnp.exp2((near - top) * (SCALE * LOG2E))
            total = jnp.sum(weights, axis=1, keepdims=True)
            result = product(weights.astype(jnp.bfloat16), kv_ref[rows, part])
            if rows.start:
                weights = jnp.exp2((far - top) * (SCALE * LOG2E))
                total = total + jnp.sum(weights, axis=1, keepdims=True)
                result = result + product(
                    weights.astype(jnp.bfloat16), kv_ref[: rows.start, part]
                )
            results.append(result / total)
            log_total = top * (SCALE * LOG2E) + jnp.log2(total)
            lse_ref[0, head : head + 1, rows] = jnp.transpose(
                jnp.broadcast_to(log_total, (BLOCK, LANES))
            )[0:1, :]
        out_ref[rows, :] = jnp.where(
            lane < VDIM, roll_lanes(results[0], VDIM), results[1]
        ).astype(jnp.bfloat16)


def attention_forward(latents, wq, wkv, rope, feat, tables, pairs):
    length = latents.shape[0]
    rank = wq.shape[0]
    whole = lambda width, at=0: pl.BlockSpec((length, width), lambda j: (0, at))
    mine = lambda width: pl.BlockSpec((length, width), lambda j: (0, j))
    tall = lambda rows: pl.BlockSpec((rows, 2 * LANES), lambda j: (0, j))
    low = jnp.bfloat16
    return pl.pallas_call(
        forward_kernel,
        grid=(pairs,),
        in_specs=[
            whole(rank), whole(KVR, rank // KVR), tall(rank), tall(KVR),
            whole(LANES), whole(LANES), whole(LANES), whole(LANES), whole(LANES),
        ],
        out_specs=[
            mine(LANES), mine(2 * LANES), mine(2 * LANES),
            pl.BlockSpec((1, 2, length), lambda j: (j, 0, 0)),
        ],
        out_shape=[
            jax.ShapeDtypeStruct((length, pairs * LANES), low),
            jax.ShapeDtypeStruct((length, pairs * 2 * LANES), low),
            jax.ShapeDtypeStruct((length, pairs * 2 * LANES), low),
            jax.ShapeDtypeStruct((pairs, 2, length), jnp.float32),
        ],
        scratch_shapes=[pltpu.VMEM((2, length, LANES), low)],
        compiler_params=pltpu.CompilerParams(vmem_limit_bytes=ROOM),
        cost_estimate=BRIEF,
        name="attention_forward",
    )(latents, latents, wq, wkv, rope, feat, *tables)


def backward_kernel(
    q_ref, kv_ref, grad_ref, lse_ref, rope_ref, here_ref, low_ref, high_ref,
    dq_ref, dkv_ref, drope_ref, k_ref, do_ref, dk_ref, dv_ref,
):
    length = q_ref.shape[0]
    lane = lax.broadcasted_iota(jnp.int32, (BLOCK, LANES), 1)
    causal = lax.broadcasted_iota(jnp.int32, (BLOCK, BLOCK), 0) <= lax.broadcasted_iota(
        jnp.int32, (BLOCK, BLOCK), 1
    )
    blocks = [slice(start, start + BLOCK) for start in range(0, length, BLOCK)]

    @pl.when(pl.program_id(0) == 0)
    def _():
        drope_ref[...] = jnp.zeros_like(drope_ref)

    for rows in blocks:
        for head in range(2):
            part = slice(head * LANES, (head + 1) * LANES)
            k_ref[head, rows, :] = jnp.where(lane < NOPE, kv_ref[rows, part], rope_ref[rows, :])
            upstream = grad_ref[rows, :].astype(jnp.float32)
            if head == 0:
                upstream = roll_lanes(upstream, VDIM)
            do_ref[head, rows, :] = jnp.where(lane < NOPE, 0.0, upstream).astype(jnp.bfloat16)
    for head in range(2):
        part = slice(head * LANES, (head + 1) * LANES)
        for rows in reversed(blocks):
            last = rows.stop == length
            query = q_ref[rows, part]
            upstream = do_ref[head, rows, :]
            log_total = lse_ref[0, head : head + 1, rows]
            pieces = [rows] + ([slice(0, rows.start)] if rows.start else [])
            held = []
            delta = None
            for piece in pieces:
                scores = product_right(k_ref[head, piece, :], query)
                probability = jnp.exp2(scores * (SCALE * LOG2E) - log_total)
                if piece is rows:
                    probability = jnp.where(causal, probability, 0.0)
                slope = product_right(kv_ref[piece, part], upstream)
                inner = jnp.sum(probability * slope, axis=0, keepdims=True)
                delta = inner if delta is None else delta + inner
                held.append((piece, probability, slope))
            query_grad = None
            for piece, probability, slope in held:
                score_grad = (probability * (slope - delta)).astype(jnp.bfloat16)
                key_grad = product(score_grad, query)
                value_grad = product(probability.astype(jnp.bfloat16), upstream)
                if last:
                    dk_ref[piece, :] = key_grad
                    dv_ref[piece, :] = value_grad
                else:
                    dk_ref[piece, :] += key_grad
                    dv_ref[piece, :] += value_grad
                term = product_left(score_grad, k_ref[head, piece, :])
                query_grad = term if query_grad is None else query_grad + term
            query_grad = query_grad * SCALE
            dq_ref[rows, part] = (
                query_grad * here_ref[rows, :]
                - roll_lanes(query_grad, -ROPE // 2) * low_ref[rows, :]
                - roll_lanes(query_grad, ROPE // 2) * high_ref[rows, :]
            ).astype(jnp.bfloat16)
        for rows in blocks:
            key_grad = dk_ref[rows, :] * SCALE
            dkv_ref[rows, part] = jnp.where(lane < NOPE, key_grad, dv_ref[rows, :]).astype(
                jnp.bfloat16
            )
            drope_ref[rows, :] += jnp.where(
                (lane >= NOPE) & (lane < NOPE + ROPE), key_grad, 0.0
            )


def attention_backward(query, key_value, grad, lse, rope, tables):
    length = query.shape[0]
    pairs = grad.shape[1] // LANES
    whole = lambda width: pl.BlockSpec((length, width), lambda j: (0, 0))
    mine = lambda width: pl.BlockSpec((length, width), lambda j: (0, j))
    low = jnp.bfloat16
    return pl.pallas_call(
        backward_kernel,
        grid=(pairs,),
        in_specs=[
            mine(2 * LANES), mine(2 * LANES), mine(LANES),
            pl.BlockSpec((1, 2, length), lambda j: (j, 0, 0)),
            whole(LANES), whole(LANES), whole(LANES), whole(LANES),
        ],
        out_specs=[mine(2 * LANES), mine(2 * LANES), whole(LANES)],
        out_shape=[
            jax.ShapeDtypeStruct((length, pairs * 2 * LANES), low),
            jax.ShapeDtypeStruct((length, pairs * 2 * LANES), low),
            jax.ShapeDtypeStruct((length, LANES), jnp.float32),
        ],
        scratch_shapes=[
            pltpu.VMEM((2, length, LANES), low),
            pltpu.VMEM((2, length, LANES), low),
            pltpu.VMEM((length, LANES), jnp.float32),
            pltpu.VMEM((length, LANES), jnp.float32),
        ],
        compiler_params=pltpu.CompilerParams(vmem_limit_bytes=ROOM),
        cost_estimate=BRIEF,
        name="attention_backward",
    )(query, key_value, grad, lse, rope, *tables)


def vector(width):
    return pl.BlockSpec((1, width), lambda *_: (0, 0))


def full(array):
    return pl.BlockSpec(array.shape, lambda *_: (0,) * array.ndim)


ANYWHERE = pl.BlockSpec(memory_space=pl.ANY)
SCALARS = pl.BlockSpec(memory_space=pltpu.SMEM)


def assemble_kernel(copies, count, *refs):
    spots_ref, pieces, outs, sems = refs[0], refs[1 : count + 1], refs[count + 1 : -1], refs[-1]
    started = []
    for number, (piece, row, rows, column, width, out, place) in enumerate(copies):
        start = place if isinstance(place, int) else spots_ref[place[0]] * place[1]
        start = pl.multiple_of(start, 16)
        copy = pltpu.make_async_copy(
            pieces[piece].at[pl.ds(row, rows), pl.ds(column, width)],
            outs[out].at[pl.ds(start, rows), :],
            sems.at[number],
        )
        copy.start()
        started.append(copy)
    for copy in started:
        copy.wait()


def assemble(spots, pieces, copies, shapes):
    return pl.pallas_call(
        functools.partial(assemble_kernel, copies, len(pieces)),
        in_specs=[SCALARS] + [ANYWHERE] * len(pieces),
        out_specs=[pl.BlockSpec(shape, lambda: (0, 0)) for shape in shapes],
        out_shape=[jax.ShapeDtypeStruct(shape, jnp.bfloat16) for shape in shapes],
        scratch_shapes=[pltpu.SemaphoreType.DMA((len(copies),))],
        compiler_params=pltpu.CompilerParams(vmem_limit_bytes=ROOM),
        cost_estimate=BRIEF,
        name="assemble",
    )(spots, *pieces)


def collect_kernel(copies, count, team_ref, *refs):
    pieces, (out_ref, sems) = refs[:count], refs[count:]
    width = out_ref.shape[1]
    started = []
    for number, (piece, row, block, team) in enumerate(copies):
        start = pl.multiple_of((block + team_ref[team]) * 16, 16)
        copy = pltpu.make_async_copy(
            pieces[piece].at[pl.ds(row, 16), pl.ds(pieces[piece].shape[1] - width, width)],
            out_ref.at[pl.ds(start, 16), :],
            sems.at[number],
        )
        copy.start()
        started.append(copy)
    for copy in started:
        copy.wait()


def collect_rows(teams, pieces, copies):
    return pl.pallas_call(
        functools.partial(collect_kernel, copies, len(pieces)),
        in_specs=[SCALARS] + [ANYWHERE] * len(pieces),
        out_specs=pl.BlockSpec((16 * len(copies), LANES), lambda: (0, 0)),
        out_shape=jax.ShapeDtypeStruct((16 * len(copies), LANES), jnp.bfloat16),
        scratch_shapes=[pltpu.SemaphoreType.DMA((len(copies),))],
        cost_estimate=BRIEF,
        name="collect",
    )(teams, *pieces)


def project_kernel(copies, count, rank, *refs):
    (team_ref, tokens_ref, gain_ref, gain_query_ref, gain_latent_ref, here_ref, low_ref, high_ref) = refs[:8]
    pieces = refs[8 : 8 + count]
    send_ref, raw_ref, input_ref, weights_ref, sems = refs[8 + count :]
    started = []
    for number, (piece, row, rows, block, team) in enumerate(copies):
        start = block if team is None else (block + team_ref[team]) * rows
        copy = pltpu.make_async_copy(
            pieces[piece].at[pl.ds(row, rows), :],
            weights_ref.at[pl.ds(pl.multiple_of(start, 16), rows), :],
            sems.at[number],
        )
        copy.start()
        started.append(copy)
    values = tokens_ref[...].astype(jnp.float32)
    input_ref[...] = normalize(values, gain_ref[...])[0].astype(jnp.bfloat16)
    for copy in started:
        copy.wait()
    raw = product(input_ref[...], weights_ref[...])
    raw_ref[...] = raw
    send_ref[:, :rank] = normalize(raw[:, :rank], gain_query_ref[...])[0].astype(jnp.bfloat16)
    send_ref[:, rank : rank + KVR] = normalize(
        raw[:, rank : rank + KVR], gain_latent_ref[...]
    )[0].astype(jnp.bfloat16)
    key = raw[:, rank + KVR :]
    send_ref[:, rank + KVR :] = (
        key * here_ref[...]
        + roll_lanes(key, -ROPE // 2) * low_ref[...]
        + roll_lanes(key, ROPE // 2) * high_ref[...]
    ).astype(jnp.bfloat16)


def project(teams, tokens, gains, tables, pieces, copies, rank):
    rows, width = tokens.shape
    out = rank + KVR + LANES
    low = jnp.bfloat16
    shapes = [((rows, out), low), ((rows, out), jnp.float32), ((rows, width), low), ((width, out), low)]
    return pl.pallas_call(
        functools.partial(project_kernel, copies, len(pieces), rank),
        in_specs=[SCALARS, full(tokens)]
        + [full(gain) for gain in gains]
        + [full(table) for table in tables]
        + [ANYWHERE] * len(pieces),
        out_specs=[pl.BlockSpec(shape, lambda: (0, 0)) for shape, _ in shapes],
        out_shape=[jax.ShapeDtypeStruct(*shape) for shape in shapes],
        scratch_shapes=[pltpu.SemaphoreType.DMA((len(copies),))],
        compiler_params=pltpu.CompilerParams(vmem_limit_bytes=ROOM),
        cost_estimate=BRIEF,
        name="project",
    )(teams, tokens, *gains, *tables, *pieces)


def joined(refs):
    if len(refs) == 1:
        return refs[0][...]
    return jnp.concatenate([ref[...] for ref in refs], axis=0)


def single_kernel(left_ref, *refs):
    refs[-1][...] = product(left_ref[...], joined(refs[:-1]))


def gate_kernel(count, last, left_ref, *refs):
    weights = joined(refs[:count])
    slope_ref, activated_ref, grads_ref = refs[count:]
    rows = left_ref.shape[0] // 2

    def work(width):
        for start in (0, rows):
            part = slice(start, start + rows)
            both = product(left_ref[part, :], weights[:, : 2 * width])
            gate, up = both[:, :width], both[:, width:]
            sigmoid = jax.nn.sigmoid(gate)
            swish = gate * sigmoid
            activated_ref[part, :width] = (swish * up).astype(jnp.bfloat16)
            upstream = slope_ref[part, :width]
            slope = sigmoid * (1.0 + gate * (1.0 - sigmoid))
            grads_ref[part, :width] = (upstream * up * slope).astype(jnp.bfloat16)
            grads_ref[part, width : 2 * width] = (upstream * swish).astype(jnp.bfloat16)
            rest = -width % LANES
            if rest:
                activated_ref[part, width : width + rest] = jnp.zeros((rows, rest), jnp.bfloat16)

    step, final = pl.program_id(0), pl.num_programs(0) - 1

    @pl.when(step < final)
    def _():
        work(TILE)

    @pl.when(step == final)
    def _():
        work(last)


TILE = 256


def piece_specs(pieces, width):
    return [pl.BlockSpec((piece.shape[0], width), lambda j: (0, j)) for piece in pieces]


def pair_columns(width):
    full_width = width
    if 2 * (width % TILE) % LANES:
        full_width = -(-width // LANES) * LANES
    return [
        (start, 2 * start, min(TILE, full_width - start), min(TILE, width - start))
        for start in range(0, full_width, TILE)
    ]


def paired_kernel(gate_ref, up_ref, out_ref):
    for start, place, size, real in pair_columns(gate_ref.shape[1]):
        for side, ref in enumerate((gate_ref, up_ref)):
            tile = ref[:, start : start + real]
            if real < size:
                rest = jnp.zeros((tile.shape[0], size - real), tile.dtype)
                tile = jnp.concatenate([tile, rest], axis=1)
            out_ref[:, place + side * size : place + (side + 1) * size] = tile


def paired(gate, up):
    width = sum(2 * size for _, _, size, _ in pair_columns(gate.shape[1]))
    shape = (gate.shape[0], width)
    return pl.pallas_call(
        paired_kernel,
        in_specs=[full(gate), full(up)],
        out_specs=pl.BlockSpec(shape, lambda: (0, 0)),
        out_shape=jax.ShapeDtypeStruct(shape, gate.dtype),
        compiler_params=pltpu.CompilerParams(vmem_limit_bytes=ROOM),
        cost_estimate=lasting(4),
        name="paired",
    )(gate, up)


def unpaired_kernel(own_ref, low_ref, high_ref, weights_ref, gate_ref, up_ref, sums_ref):
    sums = None
    for start, place, size, real in pair_columns(gate_ref.shape[1]):
        for side, out_ref in enumerate((gate_ref, up_ref)):
            part = slice(place + side * size, place + (side + 1) * size)
            total = own_ref[:, part].astype(jnp.float32) + low_ref[:, part].astype(jnp.float32)
            total = total + high_ref[:, part].astype(jnp.float32)
            out_ref[:, start : start + real] = total[:, :real]
            term = jnp.sum(total * weights_ref[:, part].astype(jnp.float32), axis=1, keepdims=True)
            sums = term if sums is None else sums + term
    sums_ref[...] = jnp.broadcast_to(sums, sums_ref.shape)


def unpaired(own, low, high, weights, width):
    rows = weights.shape[0]
    shapes = [(rows, width), (rows, width), (rows, LANES)]
    return pl.pallas_call(
        unpaired_kernel,
        grid=(1,),
        in_specs=[pl.BlockSpec(weights.shape, lambda _: (0, 0))] * 4,
        out_specs=[pl.BlockSpec(shape, lambda _: (0, 0)) for shape in shapes],
        out_shape=[jax.ShapeDtypeStruct(shape, jnp.float32) for shape in shapes],
        compiler_params=pltpu.CompilerParams(vmem_limit_bytes=ROOM),
        cost_estimate=lasting(5),
        name="unpaired",
    )(own, low, high, weights)


def feed_product(left, pieces):
    rows, width = left.shape[0], pieces[0].shape[1]
    return pl.pallas_call(
        single_kernel,
        grid=(pl.cdiv(width, TILE),),
        in_specs=[full(left)] + piece_specs(pieces, TILE),
        out_specs=pl.BlockSpec((rows, TILE), lambda j: (0, j)),
        out_shape=jax.ShapeDtypeStruct((rows, width), jnp.float32),
        compiler_params=pltpu.CompilerParams(vmem_limit_bytes=ROOM),
        cost_estimate=lasting(15),
        name="feed_product",
    )(left, *pieces)


def feed_gate(left, pieces, upstream):
    rows, width = upstream.shape
    pair_width = pieces[0].shape[1]
    column = lambda size: pl.BlockSpec((rows, size), lambda j: (0, j))
    return pl.pallas_call(
        functools.partial(gate_kernel, len(pieces), pair_width // 2 % TILE or TILE),
        grid=(pl.cdiv(width, TILE),),
        in_specs=[full(left)] + piece_specs(pieces, 2 * TILE) + [column(TILE)],
        out_specs=[column(TILE), column(2 * TILE)],
        out_shape=[
            jax.ShapeDtypeStruct((rows, width), jnp.bfloat16),
            jax.ShapeDtypeStruct((rows, pair_width), jnp.bfloat16),
        ],
        compiler_params=pltpu.CompilerParams(vmem_limit_bytes=ROOM),
        cost_estimate=BRIEF,
        name="feed_gate",
    )(left, *pieces, upstream)


def terms_kernel(count, *refs):
    arrays, out_ref = refs[: count + 1], refs[-4]
    left_ref, right_ref, sems = refs[-3:]
    rows = right_ref.shape[0] // count
    places = [left_ref]
    places += [right_ref.at[pl.ds(number * rows, rows), :] for number in range(count)]
    copies = [
        pltpu.make_async_copy(array, place, sems.at[number])
        for number, (array, place) in enumerate(zip(arrays, places))
    ]
    for copy in copies:
        copy.start()
    copies[0].wait()
    ready = 0
    for start in range(0, right_ref.shape[0], TILE):
        while ready * rows < min(start + TILE, right_ref.shape[0]):
            copies[ready + 1].wait()
            ready += 1
        part = slice(start, start + TILE)
        out_ref[:, part] = product_right(left_ref[...], right_ref[part, :]).astype(jnp.bfloat16)


def feed_terms(left, pieces, total, block, earlier=None, cost=lasting(18)):
    arrays = [left, *pieces]
    rows, width = left.shape
    columns = sum(piece.shape[0] for piece in pieces)
    low = jnp.bfloat16
    return pl.pallas_call(
        functools.partial(terms_kernel, len(pieces)),
        grid=(1,),
        in_specs=[ANYWHERE] * (len(arrays) + (earlier is not None)),
        out_specs=pl.BlockSpec((rows, columns), lambda _: (0, block)),
        out_shape=jax.ShapeDtypeStruct((rows, total), low),
        scratch_shapes=[
            pltpu.VMEM((rows, width), low),
            pltpu.VMEM((columns, width), low),
            pltpu.SemaphoreType.DMA((len(arrays),)),
        ],
        input_output_aliases={} if earlier is None else {len(arrays): 0},
        compiler_params=pltpu.CompilerParams(vmem_limit_bytes=ROOM),
        cost_estimate=cost,
        name="feed_terms",
    )(*arrays, *([] if earlier is None else [earlier]))


def latent_back_kernel(
    copies, rank, team_ref, back_ref, raw_ref, input_ref, gain_query_ref, gain_latent_ref,
    here_ref, low_ref, high_ref, *refs,
):
    outs, (grad_ref, held_ref, sems) = refs[:-3], refs[-3:]
    cuts = [(slice(0, rank), gain_query_ref), (slice(rank, rank + KVR), gain_latent_ref)]
    for part, gain_ref in cuts:
        values = raw_ref[:, part]
        inverse = normalize(values, gain_ref[...])[1]
        grad = normalize_back(
            values, inverse, gain_ref[...], back_ref[:, part].astype(jnp.float32)
        )
        grad_ref[:, part] = grad.astype(jnp.bfloat16)
    key = back_ref[:, rank + KVR :].astype(jnp.float32)
    grad_ref[:, rank + KVR :] = (
        key * here_ref[...]
        - roll_lanes(key, -ROPE // 2) * low_ref[...]
        - roll_lanes(key, ROPE // 2) * high_ref[...]
    ).astype(jnp.bfloat16)
    held_ref[...] = product_left(input_ref[...], grad_ref[...]).astype(jnp.bfloat16)
    started = []
    for number, (out, row, rows, block, team) in enumerate(copies):
        start = block if team is None else (block + team_ref[team]) * rows
        copy = pltpu.make_async_copy(
            held_ref.at[pl.ds(pl.multiple_of(start, 16), rows), :],
            outs[out].at[pl.ds(row, rows), :],
            sems.at[number],
        )
        copy.start()
        started.append(copy)
    for copy in started:
        copy.wait()


def latent_back(teams, back, raw, inputs, gains, tables, copies, heights, rank):
    rows, width = inputs.shape
    out = back.shape[1]
    low = jnp.bfloat16
    shapes = [((rows, out), low)]
    arrays = [back, raw, inputs, *gains, *tables]
    results = pl.pallas_call(
        functools.partial(latent_back_kernel, copies, rank),
        in_specs=[SCALARS] + [full(array) for array in arrays],
        out_specs=[ANYWHERE] * len(heights)
        + [pl.BlockSpec(shape, lambda: (0, 0)) for shape, _ in shapes],
        out_shape=[jax.ShapeDtypeStruct((height, out), low) for height in heights]
        + [jax.ShapeDtypeStruct(*shape) for shape in shapes],
        scratch_shapes=[pltpu.VMEM((width, out), low), pltpu.SemaphoreType.DMA((len(copies),))],
        compiler_params=pltpu.CompilerParams(vmem_limit_bytes=ROOM),
        cost_estimate=BRIEF,
        name="latent_back",
    )(teams, *arrays)
    return results[:-1], results[-1]


def head_sums_kernel(
    copies, rank, spots_ref, latents_ref, query_ref, key_value_ref, upstream_ref, heads_ref,
    out_ref, q_ref, kv_ref, o_ref, sems,
):
    q_ref[...] = product_left(latents_ref[:, :rank], query_ref[...]).astype(jnp.bfloat16)
    kv_ref[...] = product_left(latents_ref[:, rank : rank + KVR], key_value_ref[...]).astype(
        jnp.bfloat16
    )
    started = []

    def send(wanted):
        for number, (side, row, rows, place, column) in enumerate(copies):
            if side not in wanted:
                continue
            start = row if isinstance(row, int) else spots_ref[row[0]] * rows
            held = (q_ref, kv_ref, o_ref)[side]
            copy = pltpu.make_async_copy(
                held.at[pl.ds(pl.multiple_of(start, 16), rows), :],
                out_ref.at[pl.ds(place, rows), pl.ds(column, held.shape[1])],
                sems.at[number],
            )
            copy.start()
            started.append(copy)

    send((0, 1))
    o_ref[...] = product_left(upstream_ref[...], heads_ref[...]).astype(jnp.bfloat16)
    send((2,))
    for copy in started:
        copy.wait()


def head_sums(spots, latents, query, key_value, upstream, heads, rank, query_rows, latent_rows, out_rows):
    width, out_width = query.shape[1], heads.shape[1]
    count = spots.shape[0]
    rows = query_rows + latent_rows + out_rows // 2
    copies = []
    for spot in range(count):
        start = spot * rows
        copies.append((0, (spot,), query_rows, start, 0))
        copies.append((1, (spot,), latent_rows, start + query_rows, 0))
        for side in (0, 1):
            copies.append(
                (2, spot * out_rows + side * (out_rows // 2), out_rows // 2,
                 start + query_rows + latent_rows, side * out_width)
            )
    low = jnp.bfloat16
    arrays = [latents, query, key_value, upstream, heads]
    return pl.pallas_call(
        functools.partial(head_sums_kernel, copies, rank),
        in_specs=[SCALARS] + [full(array) for array in arrays],
        out_specs=pl.BlockSpec((count * rows, width), lambda: (0, 0)),
        out_shape=jax.ShapeDtypeStruct((count * rows, width), low),
        scratch_shapes=[
            pltpu.VMEM((rank, width), low),
            pltpu.VMEM((KVR, width), low),
            pltpu.VMEM((upstream.shape[1], out_width), low),
            pltpu.SemaphoreType.DMA((len(copies),)),
        ],
        compiler_params=pltpu.CompilerParams(vmem_limit_bytes=ROOM),
        cost_estimate=lasting(20),
        name="head_sums",
    )(spots, *arrays)


def token_back_kernel(grad_ref, weights_ref, tokens_ref, hidden_ref, gain_ref, out_ref):
    upstream = product_right(grad_ref[...], weights_ref[...])
    values = tokens_ref[...].astype(jnp.float32)
    inverse = normalize(values, gain_ref[...])[1]
    out_ref[...] = hidden_ref[...] + normalize_back(values, inverse, gain_ref[...], upstream)


def token_back(grad, weights, tokens, hidden_grad, gain):
    arrays = [grad, weights, tokens, hidden_grad, gain]
    return pl.pallas_call(
        token_back_kernel,
        in_specs=[full(array) for array in arrays],
        out_specs=full(hidden_grad),
        out_shape=jax.ShapeDtypeStruct(hidden_grad.shape, jnp.float32),
        compiler_params=pltpu.CompilerParams(vmem_limit_bytes=ROOM),
        cost_estimate=lasting(8),
        name="token_back",
    )(*arrays)


def reorder_kernel(spots_ref, in_ref, out_ref):
    width = in_ref.shape[1]
    count = spots_ref.shape[0]
    size = width // count
    window = min(-(-(size + LANES - 1) // LANES) * LANES, width)
    for place in range(count):
        start = spots_ref[place] * size
        base = jnp.minimum(start // LANES * LANES, width - window)
        held = in_ref[:, pl.ds(pl.multiple_of(base, LANES), window)].astype(jnp.float32)
        held = pltpu.roll(held, lax.rem(window - (start - base), window), 1)
        out_ref[:, place * size : (place + 1) * size] = held[:, :size].astype(out_ref.dtype)


def reorder(values, spots):
    return pl.pallas_call(
        reorder_kernel,
        in_specs=[SCALARS, full(values)],
        out_specs=full(values),
        out_shape=jax.ShapeDtypeStruct(values.shape, values.dtype),
        compiler_params=pltpu.CompilerParams(vmem_limit_bytes=ROOM),
        cost_estimate=lasting(4),
        name="reorder",
    )(spots, values)


class Ring:
    def __init__(self, axis):
        self.axis = axis
        self.count = lax.axis_size(axis)
        self.half = self.count // 2
        order = list(range(0, self.count, 2)) + list(range(self.count - 1, 0, -2))
        self.me = lax.axis_index(axis)
        self.spot = self.place(self.me)
        indices = jnp.arange(self.count, dtype=jnp.int32)
        self.ahead = self.owner(indices)
        self.behind = lax.rem(self.place(indices) - self.spot + self.count, self.count)
        self.up = [(order[i], order[(i + 1) % self.count]) for i in range(self.count)]
        self.down = [(b, a) for a, b in self.up]

    def place(self, index):
        return jnp.where(index % 2 == 0, index // 2, self.count - (index + 1) // 2)

    def owner(self, step):
        spot = lax.rem(self.spot + step + self.count, self.count)
        return jnp.where(spot < self.half, 2 * spot, 2 * self.count - 1 - 2 * spot)

    def send_up(self, block):
        return lax.ppermute(block, self.axis, self.up)

    def send_down(self, block):
        return lax.ppermute(block, self.axis, self.down)


class Gather:
    def __init__(self, ring, shard):
        self.ring = ring
        self.rows = shard.shape[0]
        self.low = self.high = shard
        self.blocks = {0: shard}
        self.step = 0

    def advance(self):
        ring = self.ring
        if self.done:
            return
        self.step += 1
        if self.step < ring.half:
            self.low = ring.send_up(self.low)
            self.high = ring.send_down(self.high)
            self.blocks[self.step] = self.high
            self.blocks[ring.count - self.step] = self.low
        else:
            cut = self.rows // 2
            self.low = ring.send_up(self.low[:cut])
            self.high = ring.send_down(self.high[cut:])
            self.blocks[ring.half] = None

    @property
    def done(self):
        return self.step >= self.ring.half

    def finish(self):
        while not self.done:
            self.advance()
        self.blocks[self.ring.half] = jnp.concatenate([self.low, self.high], axis=0)
        return [self.blocks[spot] for spot in range(self.ring.count)]


class Scatter:
    def __init__(self, ring, take, rows):
        self.ring = ring
        self.take = lambda step, start, size: take(step % ring.count, start, size)
        self.rows = rows
        self.step = 0
        self.low = self.high = None

    def add(self, a, b):
        return (a.astype(jnp.float32) + b.astype(jnp.float32)).astype(b.dtype)

    def advance(self):
        ring, rows, cut = self.ring, self.rows, self.rows // 2
        if self.done:
            return
        ahead = ring.half - self.step
        if self.step:
            self.low, self.high = lax.optimization_barrier((self.low, self.high))
        self.step += 1
        if ahead == ring.half:
            low = self.take(ahead, 0, cut)
            high = self.take(ahead, cut, rows - cut)
        elif ahead == ring.half - 1:
            low = self.take(ahead, 0, rows)
            high = self.take(-ahead, 0, rows)
            low = jnp.concatenate([self.add(self.low, low[:cut]), low[cut:]], axis=0)
            high = jnp.concatenate([high[:cut], self.add(self.high, high[cut:])], axis=0)
        else:
            low = self.add(self.low, self.take(ahead, 0, rows))
            high = self.add(self.high, self.take(-ahead, 0, rows))
        self.sent = (low, high)
        self.low = ring.send_up(low)
        self.high = ring.send_down(high)

    @property
    def done(self):
        return self.step >= self.ring.half

    def finish(self):
        while not self.done:
            self.advance()
        own = self.take(0, 0, self.rows).astype(jnp.float32)
        return own + self.low.astype(jnp.float32) + self.high.astype(jnp.float32)


def stacked(ring, grads):
    rows = grads.shape[0] // ring.count

    def take(spot, start, size):
        return lax.slice_in_dim(grads, spot * rows + start, spot * rows + start + size, axis=0)

    return Scatter(ring, take, rows)


def staged(ring, left, right):
    size = left.shape[1] // ring.count
    low, high = ring.count // 4, ring.count // 4 + ring.half
    parts = {}
    held = [right]

    def take(spot, start, rows):
        name = 1 if low <= spot < high else 0 if spot < low else 2
        first = (0, low, high)[name]
        if name not in parts:
            last = (low, high, ring.count)[name]
            columns = lax.slice_in_dim(left, first * size, last * size, axis=1)
            parts[name] = product_left(columns, held[0]).astype(jnp.bfloat16)
        begin = (spot - first) * size + start
        return lax.slice_in_dim(parts[name], begin, begin + rows, axis=0)

    scatter = Scatter(ring, take, size)
    scatter.held = held
    scatter.parts = parts
    return scatter


def delay(scatter, *others):
    scatter.held[0] = follow(scatter.held[0], *others)


def follow(values, *others):
    return lax.optimization_barrier((values, others))[0]


def ends(*streams):
    return [(stream.low, stream.high) for stream in streams]


def hold(stream, *others):
    stream.low, stream.high = follow((stream.low, stream.high), *others)


def swap(values, bit):
    count = lax.axis_size("tensor")
    return lax.ppermute(values, "tensor", [(i, i ^ bit) for i in range(count)])


def pad_heads(weights, heads):
    rows = weights.shape[0]
    width = weights.shape[1] // heads
    padded = jnp.pad(weights.reshape(rows, heads, width), ((0, 0), (0, 0), (0, LANES - width)))
    return padded.reshape(rows, heads * LANES)


def on_device(
    tokens,
    segments,
    positions,
    norm_input,
    norm_query,
    norm_latent,
    norm_hidden,
    query_down,
    latent_down,
    query_up,
    latent_up,
    attention_out,
    gate_weight,
    up_weight,
    down_weight,
    cotangent,
):
    low = jnp.bfloat16
    local_rows = tokens.shape[0]
    shard = lax.axis_index("tensor")
    offset = shard * local_rows
    length = segments.shape[0]
    local_heads = HEADS // lax.axis_size("tensor")
    pairs = local_heads // 2
    rank = query_down.shape[1]
    ring = Ring("fsdp")
    everyone = lax.axis_size("fsdp") * lax.axis_size("tensor")
    teams = lax.axis_size("tensor")
    gains_own = jnp.concatenate([norm_input, norm_hidden, norm_query, norm_latent])
    gain_sizes = [norm_input.shape[0], norm_hidden.shape[0], norm_query.shape[0], norm_latent.shape[0]]
    gain_width = -(-gains_own.shape[0] // LANES) * LANES
    spare = LANES - NOPE - ROPE
    gain_rows = -(-gains_own.shape[0] // spare)
    down_rows = query_down.shape[0]
    down_width = rank + KVR + LANES
    gain_part = jnp.pad(gains_own, (0, gain_rows * spare - gains_own.shape[0]))
    gain_part = jnp.pad(gain_part.reshape(gain_rows, spare), ((0, down_rows - gain_rows), (0, 0)))
    packed = jnp.concatenate(
        [
            query_down,
            latent_down[:, :KVR],
            jnp.zeros((down_rows, NOPE), low),
            latent_down[:, KVR:],
            gain_part,
        ],
        axis=1,
    )
    feed_width = gate_weight.shape[1]
    feed_rows = gate_weight.shape[0]
    feed_pad = -feed_width % LANES
    widen = lambda weights: jnp.pad(weights, ((0, 0), (0, feed_pad)))
    head_width = 2 * pairs * LANES
    query_rows, latent_rows, out_rows = query_up.shape[0], latent_up.shape[0], attention_out.shape[1]
    out_width = attention_out.shape[0]
    out_t = attention_out.T
    mixed = jnp.concatenate(
        [
            pad_heads(query_up, local_heads),
            latent_up,
            jnp.concatenate([out_t[: out_rows // 2], out_t[out_rows // 2 :]], axis=1),
        ],
        axis=0,
    )
    mixed_up = Gather(ring, mixed)
    down_up = Gather(ring, widen(down_weight.T))
    pair_own = paired(gate_weight, up_weight)
    pair_up = Gather(ring, pair_own)

    tokens_ring = reorder(tokens, ring.ahead)
    upstream = reorder(cotangent, ring.ahead)
    here, turn_low, turn_high = rotary_lanes(positions)
    tables = (here, turn_low, turn_high)
    local_tables = [lax.dynamic_slice_in_dim(table, offset, local_rows) for table in tables]
    query_feat, key_feat = segment_lanes(segments)
    key_feat = key_feat.astype(low)
    ahead, behind = ring.ahead, ring.behind
    team_ids = shard ^ jnp.asarray([0, 2, 1, 3], jnp.int32)

    small_up = Gather(ring, jnp.concatenate([packed, swap(packed, 2)], axis=0))
    pieces, copies = [], []

    def collect(block, spot, team):
        for first, piece in ((team, block), (team + 2, swap(block, 1))):
            for part in range(block.shape[0] // down_rows):
                copies.append(
                    (len(pieces), part * down_rows, down_rows, spot * teams, first + part)
                )
            pieces.append(piece)

    collect(small_up.low, 0, 0)
    mixed_up.advance()
    while not small_up.done:
        swapped = pieces[1::2]
        small_up.advance()
        mixed_up.advance()
        if not small_up.done:
            collect(small_up.high, small_up.step, 0)
            collect(small_up.low, ring.count - small_up.step, 0)
            hold(small_up, ends(mixed_up), swapped)
            hold(mixed_up, ends(small_up))
    collect(small_up.low, ring.half, 0)
    collect(small_up.high, ring.half, 1)
    hold(down_up, ends(mixed_up, small_up))
    down_up.advance()
    if down_rows % 16:
        table = [[None] * teams for _ in range(ring.count)]
        for piece, row, _, block, team in copies:
            table[block // teams][team] = pieces[piece][row : row + gain_rows, down_width - spare :]
        table = jnp.stack([part for group in zip(*table) for part in group])
        table = table.reshape(teams, ring.count, gain_rows * spare)
        places = shard ^ jnp.arange(teams, dtype=jnp.int32)
        places = jnp.where(places == 1, 2, jnp.where(places == 2, 1, places))
        table = jnp.take(table, places, axis=0)
    else:
        table = collect_rows(
            team_ids, pieces, [(piece, row, block, team) for piece, row, _, block, team in copies]
        )
        table = table.reshape(ring.count, teams, 16, LANES)[:, :, :gain_rows, LANES - spare :]
        table = jnp.transpose(table, (1, 0, 2, 3)).reshape(teams, ring.count, gain_rows * spare)
    table = table.astype(jnp.float32)
    gain_parts = []
    start = 0
    for number, size in enumerate(gain_sizes):
        part = jnp.transpose(table[:, :, start : start + size], (1, 0, 2))
        if number >= 2:
            part = jnp.take(part, behind, axis=0)
        gain_parts.append(part.reshape(1, -1))
        start += size
    gain_in, gain_hidden, gain_query, gain_latent = gain_parts
    if down_rows % 16:
        whole = jnp.zeros((everyone * down_rows, down_width), low)
        for piece, row, rows, block, team in copies:
            whole = lax.dynamic_update_slice(
                whole, pieces[piece][row : row + rows], ((block + team_ids[team]) * rows, 0)
            )
        pieces, copies = [whole], [(0, 0, whole.shape[0], 0, None)]
    latent_send, latent_raw, attention_input, down_projections = project(
        team_ids, tokens_ring, (gain_in, gain_query, gain_latent), local_tables, pieces, copies, rank
    )
    latent_send = follow(latent_send, ends(down_up))
    latents = lax.all_gather(latent_send, "tensor", axis=0, tiled=True)
    hold(down_up, latent_send)
    down_up.advance()
    latents = follow(latents, ends(down_up))
    hold(pair_up, ends(down_up))
    mixed_blocks = mixed_up.finish()
    if query_rows % 16 or latent_rows % 16 or out_rows % 32:
        mixed_all = jnp.stack([mixed_blocks[0]] * ring.count)
        for spot, block in enumerate(mixed_blocks):
            mixed_all = lax.dynamic_update_slice(mixed_all, block[None], (ring.owner(spot), 0, 0))
        wq = mixed_all[:, :query_rows].reshape(-1, head_width)
        wkv = mixed_all[:, query_rows : query_rows + latent_rows].reshape(-1, head_width)
        outs = [block[query_rows + latent_rows :] for block in mixed_blocks]
        attention_out_t = jnp.concatenate(
            [block[:, side * out_width : (side + 1) * out_width] for block in outs for side in (0, 1)],
            axis=0,
        )
    else:
        copies = []
        for spot in range(ring.count):
            copies.append((spot, 0, query_rows, 0, head_width, 0, (spot, query_rows)))
            copies.append((spot, query_rows, latent_rows, 0, head_width, 1, (spot, latent_rows)))
            for side in (0, 1):
                copies.append(
                    (spot, query_rows + latent_rows, out_rows // 2, side * out_width, out_width, 2,
                     spot * out_rows + side * (out_rows // 2))
                )
        wq, wkv, attention_out_t = assemble(
            ahead,
            mixed_blocks,
            copies,
            [(ring.count * query_rows, head_width), (ring.count * latent_rows, head_width),
             (ring.count * out_rows, out_width)],
        )
    down_up.advance()
    pair_up.advance()
    feed_upstream = follow(RESIDUAL * upstream.astype(jnp.float32), latents).astype(low)
    feed_upstream = lax.all_gather(feed_upstream, "tensor", axis=0, tiled=True)
    rope = latents[:, rank + KVR :] + key_feat
    heads, query_heads, key_value, log_totals = attention_forward(
        latents, wq, wkv, rope, query_feat, tables, pairs
    )
    branch_terms = product_right(heads, attention_out_t).astype(low)
    branch_terms = follow(branch_terms, feed_upstream, ends(pair_up))
    attention_branch = lax.psum_scatter(branch_terms, "tensor", scatter_dimension=0, tiled=True)
    attention_branch = follow(attention_branch, ends(down_up))
    downs = down_up.finish()
    if ring.count > 8:
        downs = [jnp.concatenate(downs, axis=0)]
    activated_grad = feed_product(feed_upstream, downs)
    hidden = tokens_ring.astype(jnp.float32) + RESIDUAL * attention_branch.astype(jnp.float32)
    feed_normed, inverse_hidden = normalize(hidden, gain_hidden)
    pair_up.advance()
    feed_normed = follow(feed_normed.astype(low), ends(pair_up))
    feed_seq = lax.all_gather(feed_normed, "tensor", axis=0, tiled=True)
    hold(pair_up, ends(down_up))
    pair_up.advance()
    hold(pair_up, activated_grad)
    weights = pair_up.finish()
    if ring.count > 8:
        weights = [jnp.concatenate(weights, axis=0)]
    activated, pair_grad = feed_gate(feed_seq, weights, activated_grad)

    grad_down = staged(ring, feed_upstream, activated)
    grad_down.advance()
    grad_pair = staged(ring, feed_seq, follow(pair_grad, grad_down.sent))
    grad_pair.advance()
    hold(grad_down, grad_pair.sent)
    grad_down.advance()
    half = max(len(weights) // 2, 1)
    width = feed_seq.shape[1]
    pair_grad = follow(pair_grad, grad_down.sent)
    terms = feed_terms(pair_grad, weights[:half], width, 0)
    hold(grad_pair, terms)
    grad_pair.advance()
    if len(weights) > half:
        terms = follow(terms, grad_pair.sent)
        terms = feed_terms(pair_grad, weights[half:], width, 1, terms)
    terms = follow(terms, ends(grad_down))
    feed_back = lax.psum_scatter(terms, "tensor", scatter_dimension=0, tiled=True)
    delay(grad_down, terms)
    hold(grad_down, terms)
    grad_down.advance()
    feed_back = follow(feed_back, grad_down.sent)
    delay(grad_pair, grad_down.sent)
    grad_pair.advance()
    grad_pair.take(0, 0, 1), grad_down.take(0, 0, 1)
    feed_back = follow(feed_back, grad_pair.parts[0], grad_down.parts[0])
    hidden_back = normalize_back(
        hidden, inverse_hidden, gain_hidden, feed_back.astype(jnp.float32)
    )
    hidden_grad = upstream.astype(jnp.float32) + hidden_back
    upstream_send = follow((RESIDUAL * hidden_grad).astype(low), grad_pair.sent, ends(grad_down))
    attention_upstream = lax.all_gather(upstream_send, "tensor", axis=0, tiled=True)
    activated = follow(activated, upstream_send)
    feed_branch = feed_terms(activated, downs[:half], width, 0, None, BRIEF)
    if len(downs) > half:
        feed_branch = feed_terms(activated, downs[half:], width, 1, feed_branch, BRIEF)
    attention_upstream = follow(attention_upstream, feed_branch, ends(grad_pair))
    feed_branch = lax.psum_scatter(feed_branch, "tensor", scatter_dimension=0, tiled=True)
    heads_grad = product(attention_upstream, attention_out_t).astype(low)
    grad_pair.advance()
    heads_grad = follow(heads_grad, grad_pair.sent)
    query_raw_grad, key_value_grad, key_rope_grad = attention_backward(
        query_heads, key_value, heads_grad, log_totals, rope, tables
    )
    query_raw_grad, key_value_grad = follow((query_raw_grad, key_value_grad), ends(grad_pair))
    hold(grad_down, query_raw_grad)
    grad_down.advance()
    latent_terms = jnp.concatenate(
        [
            product_right(query_raw_grad, wq),
            product_right(key_value_grad, wkv),
            key_rope_grad,
        ],
        axis=1,
    ).astype(low)
    latent_terms = follow(latent_terms, feed_branch)
    output = hidden + RESIDUAL * feed_branch.astype(jnp.float32)
    latent_grad = lax.psum_scatter(latent_terms, "tensor", scatter_dimension=0, tiled=True)
    upstream_late, query_raw_grad, key_value_grad = follow(
        (attention_upstream, query_raw_grad, key_value_grad), latent_terms, grad_down.sent
    )
    if query_rows % 16 or latent_rows % 16 or out_rows % 32:
        sums = [
            jnp.take(product_left(left, right).astype(low).reshape(ring.count, -1, head_width), ahead, axis=0)
            for left, right in (
                (latents[:, :rank], query_raw_grad),
                (latents[:, rank : rank + KVR], key_value_grad),
            )
        ]
        out_sums = product_left(upstream_late, heads).astype(low)
        out_sums = out_sums.reshape(ring.count, 2, out_rows // 2, out_width)
        sums.append(jnp.concatenate([out_sums[:, 0], out_sums[:, 1]], axis=2))
        mixed_sums = jnp.concatenate(sums, axis=1).reshape(-1, head_width)
    else:
        mixed_sums = head_sums(
            ahead, latents, query_raw_grad, key_value_grad, upstream_late, heads,
            rank, query_rows, latent_rows, out_rows,
        )
    grad_mixed = stacked(ring, mixed_sums)
    grad_mixed.advance()
    latent_grad = follow(latent_grad, grad_mixed.sent, ends(grad_down))
    pair = 2 * down_rows
    height = ring.count * pair
    heights = [height, height]
    copies = [
        (team // 2, spot * pair + (team % 2) * down_rows, down_rows, spot * teams, team)
        for spot in range(ring.count)
        for team in range(teams)
    ]
    aligned = down_rows % 16 == 0
    if not aligned:
        copies, heights = [(0, 0, 2 * height, 0, None)], [2 * height]
    sent, latent_low = latent_back(
        team_ids, latent_grad, latent_raw, attention_input, (gain_query, gain_latent),
        local_tables, copies, heights, rank,
    )
    if not aligned:
        blocks = jnp.take(
            sent[0].reshape(ring.count, teams, down_rows, down_width), team_ids, axis=1
        )
        sent = [blocks[:, :2].reshape(height, -1), blocks[:, 2:].reshape(height, -1)]

    def add_low(a, b):
        return (a.astype(jnp.float32) + b.astype(jnp.float32)).astype(low)

    other_sums = swap(sent[1], 1)
    token_grad = token_back(
        latent_low, down_projections, tokens_ring, hidden_grad, gain_in
    )
    hold(grad_mixed, latent_low)
    grad_mixed.advance()
    other_sums = follow(other_sums, token_grad, grad_mixed.sent)
    grad_small = stacked(ring, add_low(sent[0], other_sums))
    grad_small.advance()
    token_grad = reorder(follow(token_grad, grad_small.take(0, 0, 1)), ring.behind)
    hold(grad_down, ends(grad_small))
    hold(grad_mixed, grad_small.sent)
    grad_mixed.advance()
    hold(grad_small, token_grad)
    grad_small.advance()
    hold(grad_mixed, grad_small.sent)
    hold(grad_pair, ends(grad_small))
    grad_small.advance()
    output = reorder(follow(output.astype(low), grad_small.sent), ring.behind)
    grad_mixed.advance()
    small_own = grad_small.finish()
    small_other = follow(small_own[down_rows:].astype(low), ends(grad_mixed))
    packed_own = small_own[:down_rows] + swap(small_other, 2).astype(jnp.float32)
    rope_from = rank + KVR + NOPE
    lanes = jnp.arange(down_width) < rope_from + ROPE
    grad_gain_input = jnp.sum(
        jnp.where(lanes, packed.astype(jnp.float32) * packed_own, 0.0), axis=1
    ) / norm_input.astype(jnp.float32)
    grad_mixed_own = grad_mixed.finish()
    while not grad_pair.done:
        grad_pair.advance()
    grad_query_own = grad_mixed_own[:query_rows].reshape(query_rows, local_heads, LANES)
    grad_out_own = grad_mixed_own[query_rows + latent_rows :]
    grad_out_own = jnp.concatenate(
        [grad_out_own[:, :out_width], grad_out_own[:, out_width:]], axis=0
    )
    grad_gate_own, grad_up_own, pair_sums = unpaired(
        grad_pair.take(0, 0, feed_rows), grad_pair.low, grad_pair.high, pair_own, feed_width
    )
    row_sums = lambda weights, grads: jnp.sum(weights.astype(jnp.float32) * grads, axis=1)
    head_rows = query_rows + latent_rows
    gain_sums = jnp.concatenate(
        [pair_sums[:, 0], row_sums(mixed[:head_rows], grad_mixed_own[:head_rows])]
    )
    gain_sums = jnp.pad(gain_sums, (0, -gain_sums.shape[0] % LANES))[None]
    gain_sums = gain_sums + swap(gain_sums, 1)
    gain_sums = (gain_sums + swap(gain_sums, 2))[0]
    gain_grads = []
    start = 0
    for gain in (norm_hidden, norm_query, norm_latent):
        size = gain.shape[0]
        own = lax.dynamic_slice_in_dim(gain_sums, start + shard * size, size)
        gain_grads.append(own / gain.astype(jnp.float32))
        start += size * teams
    return (
        output,
        token_grad,
        grad_gain_input,
        gain_grads[1],
        gain_grads[2],
        gain_grads[0],
        packed_own[:, :rank],
        jnp.concatenate(
            [packed_own[:, rank : rank + KVR], packed_own[:, rope_from : rope_from + ROPE]],
            axis=1,
        ),
        grad_query_own[:, :, : NOPE + ROPE].reshape(query_rows, -1),
        grad_mixed_own[query_rows : query_rows + latent_rows],
        grad_out_own.T,
        grad_gate_own,
        grad_up_own,
        grad_down.finish()[:, :feed_width].T,
    )


def solution(mesh):
    return jax.shard_map(
        on_device,
        mesh=mesh,
        in_specs=(
            P(("fsdp", "tensor"), None),
            P("fsdp"),
            P("fsdp"),
            P(("fsdp", "tensor")),
            P(("fsdp", "tensor")),
            P(("fsdp", "tensor")),
            P(("fsdp", "tensor")),
            P(("fsdp", "tensor"), None),
            P(("fsdp", "tensor"), None),
            P("fsdp", "tensor"),
            P("fsdp", "tensor"),
            P("tensor", "fsdp"),
            P("fsdp", "tensor"),
            P("fsdp", "tensor"),
            P("tensor", "fsdp"),
            P(("fsdp", "tensor"), None),
        ),
        out_specs=(
            P(("fsdp", "tensor"), None),
            P(("fsdp", "tensor"), None),
            P(("fsdp", "tensor")),
            P(("fsdp", "tensor")),
            P(("fsdp", "tensor")),
            P(("fsdp", "tensor")),
            P(("fsdp", "tensor"), None),
            P(("fsdp", "tensor"), None),
            P("fsdp", "tensor"),
            P("fsdp", "tensor"),
            P("tensor", "fsdp"),
            P("fsdp", "tensor"),
            P("fsdp", "tensor"),
            P("tensor", "fsdp"),
        ),
        check_vma=False,
    )
```

time: 2240 us -> 824 us (0.37)
  waiting for transfers between devices: 1540 us -> 320 us
  matrix products: 417 us -> 62 us
  Pallas kernels: 0 us -> 236 us
  blocking collectives: 122 us -> 0 us
  starting transfers between devices: 1.67 us -> 75.4 us
    reduce_scatter x13 -> x4, waiting for transfers between devices: 987 us -> 26.5 us  [the longest x1 22.5 us: on_device(): lax.psum_scatter(branch_terms, 'tensor', scatter_dimension=0, tiled=True)]
    all_gather x11 -> x4, waiting for transfers between devices: 546 us -> 0.01 us  [the longest x1 0.01 us: on_device(): latents = lax.all_gather(latent_send, 'tensor', axis=0, tiled=True)]
    ppermute x0 -> x78, waiting for transfers between devices: none -> 293 us  [the longest x32 151 us: send_up(): return lax.ppermute(block, self.axis, self.up)]
    pallas_call x0 -> x20, Pallas kernels: none -> 236 us  [the longest x4 58.7 us: feed_terms(): pl.pallas_call(functools.partial(terms_kernel, len(pieces)), grid=(1,), i...]
    dot_general x68 -> x3, matrix products: 168 us -> 12.4 us  [product_right(): lax.dot_general(left, right, (((1,), (1,)), ((), ())), preferred_element_...]
    dot_general x48 -> x1, matrix products: 127 us -> 8.89 us  [product(): return jnp.dot(left, right, preferred_element_type=jnp.float32)]
    unnamed x2 -> x0, blocking collectives: 82.7 us -> none
    dot_general x48 -> x6, matrix products: 123 us -> 40.7 us  [product_left(): lax.dot_general(left, right, (((0,), (0,)), ((), ())), preferred_element_...]
  transfers between devices with their start and end apart: 24 -> 86, of which waited for: 21 -> 43; matrix products, arithmetic and copies ran while one was open for 12% -> 18% of each run, Pallas kernels for 0% -> 25%
where the time goes in v1:
time: 824 us; the launch traced here: 815 us
  waiting for transfers between devices  320 us (39%)
  Pallas kernels  236 us (29%)
  starting transfers between devices  75.4 us (9%)
  other arithmetic  68.3 us (8%)
  matrix products  62 us (8%)
  local copies, waits for them, and re-layouts  37.5 us (5%)
  between operations  15.9 us (2%)
    ppermute x32, waiting for transfers between devices, send_up(): return lax.ppermute(block, self.axis, self.up)  151 us
    ppermute x32, waiting for transfers between devices, send_down(): return lax.ppermute(block, self.axis, self.down)  140 us
    pallas_call x4, Pallas kernels, feed_terms(): pl.pallas_call(functools.partial(terms_kernel, len(pieces)), grid=(1,), i...  58.7 us
    ppermute x32, starting transfers between devices, send_up(): return lax.ppermute(block, self.axis, self.up)  49.1 us
    dot_general x6, matrix products, product_left(): lax.dot_general(left, right, (((0,), (0,)), ((), ())), preferred_element_...  40.7 us
    pallas_call x1, Pallas kernels, attention_backward(): pl.pallas_call(backward_kernel, grid=(pairs,), in_specs=[mine(2 * LANES),...  31.3 us
    pallas_call x1, Pallas kernels, feed_gate(): pl.pallas_call(functools.partial(gate_kernel, len(pieces), pair_width //...  26.3 us
    convert_element_type x16, other arithmetic, add(): return (a.astype(jnp.float32) + b.astype(jnp.float32)).astype(b.dtype)  24.9 us
  transfers between devices with their start and end apart: 86, of which 43 were waited for; matrix products, arithmetic and copies ran while one was open for 18% of the time, Pallas kernels for 25%

profile of v1, /device:TPU:0, one launch (start us, length us, event | category | flops | bytes accessed | tf_op | source)
XLA Modules:
  0.0 815.4 jit_solution(3392407799355649100)
XLA Ops:
  15.4 14.2 %collective-permute-done.6.refs_8_ = bf16[288,1280]{1,0:T(8,128)(2,1)} collective-permute-done((bf16[288,1280]{1,0:T(8,128)(2,1)S(1)}, bf16[288,1280]{1,0:T(8,128)(2,1)}, u32[]{:S(2)}, u32[]{:S(2)}) %collective-permute-start.6) | collective-permute-done | bytes 737312 | tf_op jit(solution)/shard_map/ppermute | solution.py:773
  33.8 22.8 %collective-permute-done.2.refs_2_.refs_10_ = bf16[160,1152]{1,0:T(8,128)(2,1)S(1)} collective-permute-done((bf16[160,1152]{1,0:T(8,128)(2,1)S(1)}, bf16[160,1152]{1,0:T(8,128)(2,1)S(1)}, u32[]{:S(2)}, u32[]{:S(2)}) %collective-permute-start.2) | collective-permute-done | bytes 368672 | tf_op jit(solution)/shard_map/ppermute | solution.py:776
  61.6 7.3 collective-permute-done.10.refs_6_.refs_14_
  69.0 15.7 %collective-permute-done.12.refs_8_.refs_16_ = bf16[160,1152]{1,0:T(8,128)(2,1)} collective-permute-done((bf16[160,1152]{1,0:T(8,128)(2,1)S(1)}, bf16[160,1152]{1,0:T(8,128)(2,1)}, u32[]{:S(2)}, u32[]{:S(2)}) %collective-permute-start.12) | collective-permute-done | bytes 368672 | tf_op jit(solution)/shard_map/ppermute | solution.py:773
  92.8 13.0 %collective-permute-done.20 = bf16[144,1280]{1,0:T(8,128)(2,1)S(1)} collective-permute-done((bf16[144,1280]{1,0:T(8,128)(2,1)S(1)}, bf16[144,1280]{1,0:T(8,128)(2,1)S(1)}, u32[]{:S(2)}, u32[]{:S(2)}) %collective-permute-start.20) | collective-permute-done | bytes 368672 | tf_op jit(solution)/shard_map/ppermute | solution.py:773
  117.4 3.7 reorder.4.refs_1_.tokens_ref
  129.6 10.0 %project.1 = (bf16[256,1152]{1,0:T(8,128)(2,1)}, f32[256,1152]{1,0:T(8,128)}, bf16[256,2560]{1,0:T(8,128)(2,1)}, bf16[2560,1152]{1,0:T(8,128)(2,1)}) custom-call(s32[4]{0:T(128)} %broadcast_xor_fusion.team_ref.refs_0_, bf16[256,2560]{1,0:T(8,128)(2,1)} %reorder.4.refs_1_.tokens_ref, f32[1,2560]{1,0:T(1,128)} %reshape.321.refs_2_.gain_ref, ...), custom_call_target="tpu_custom_call" | custom-call | flops 1 | bytes 1 | tf_op jit(solution)/shard_map/project/pallas_call | solution.py:383
  142.7 3.7 reorder.5
  149.0 16.8 %collective-permute-done.28.refs_6_.refs_3_ = bf16[320,1664]{1,0:T(8,128)(2,1)S(1)} collective-permute-done((bf16[320,1664]{1,0:T(8,128)(2,1)}, bf16[320,1664]{1,0:T(8,128)(2,1)S(1)}, u32[]{:S(2)}, u32[]{:S(2)}) %collective-permute-start.28) | collective-permute-done | bytes 1064992 | tf_op jit(solution)/shard_map/ppermute | solution.py:773
  167.4 3.4 paired.1.refs_0_.refs_1_.weights_ref
  174.8 7.1 assemble.1
  183.9 23.4 %attention_forward.1 = (bf16[1024,640]{1,0:T(8,128)(2,1)}, bf16[1024,1280]{1,0:T(8,128)(2,1)}, bf16[1024,1280]{1,0:T(8,128)(2,1)}, f32[5,2,1024]{2,1,0:T(2,128)}) custom-call(bf16[1024,1152]{1,0:T(8,128)(2,1)} %all-gather.5.cloned.1.call-done.xq_ref.lat_ref.latents_ref, bf16[1024,1152]{1,0:T(8,128)(2,1)} %all-gather.5.cloned.1.call-done.xq_ref.lat_ref.latents_ref, ...), custom_call_target="tpu_custom_call" | custom-call | flops 1 | bytes 1 | tf_op jit(solution)/shard_map/attention_forward/pallas_call | solution.py:148
  207.2 7.4 convolution_convert_fusion.4
  221.8 22.5 %collective-permute-done.32.refs_5_.refs_2_ = bf16[320,1664]{1,0:T(8,128)(2,1)S(1)} collective-permute-done((bf16[320,1664]{1,0:T(8,128)(2,1)}, bf16[320,1664]{1,0:T(8,128)(2,1)S(1)}, u32[]{:S(2)}, u32[]{:S(2)}) %collective-permute-start.32) | collective-permute-done | bytes 1064992 | tf_op jit(solution)/shard_map/ppermute | solution.py:773
  246.0 22.5 %reduce-scatter.5.cloned.1.call-done = bf16[256,2560]{1,0:T(8,128)(2,1)} async-done(((bf16[1024,2560]{1,0:T(8,128)(2,1)}), bf16[256,2560]{1,0:T(8,128)(2,1)}) %reduce-scatter.5.cloned.1.call-update) | async-done | bytes 1310736 | tf_op jit(solution)/shard_map/reduce_scatter | solution.py:1103
  272.1 12.5 %collective-permute-done.34.refs_6_.refs_3_ = bf16[320,3200]{1,0:T(8,128)(2,1)} collective-permute-done((bf16[320,3200]{1,0:T(8,128)(2,1)}, bf16[320,3200]{1,0:T(8,128)(2,1)}, u32[]{:S(2)}, u32[]{:S(2)}) %collective-permute-start.34) | collective-permute-done | bytes 2048032 | tf_op jit(solution)/shard_map/ppermute | solution.py:773
  290.3 7.0 collective-permute-done.36
  297.2 4.5 collective-permute-done.37
  305.4 15.4 %feed_product.1.refs_8_ = f32[1024,1664]{1,0:T(8,128)} custom-call(bf16[1024,2560]{1,0:T(8,128)(2,1)} %all-gather.7.cloned.1.call-done.left_ref, bf16[320,1664]{1,0:T(8,128)(2,1)} %copy-done.9, bf16[320,1664]{1,0:T(8,128)(2,1)} %collective-permute-done.27.refs_1_.refs_2_, bf16[320,1664]{1,0:T(8,128)(2,1)} %copy-done.17, ...), custom_call_target="tpu_custom_call" | custom-call | flops 1 | bytes 45000000 | tf_op jit(solution)/shard_map/feed_product/pallas_call | solution.py:511
  320.8 23.7 %collective-permute-done.38.refs_3_.refs_4_ = bf16[320,3200]{1,0:T(8,128)(2,1)S(1)} collective-permute-done((bf16[320,3200]{1,0:T(8,128)(2,1)}, bf16[320,3200]{1,0:T(8,128)(2,1)S(1)}, u32[]{:S(2)}, u32[]{:S(2)}) %collective-permute-start.38) | collective-permute-done | bytes 2048032 | tf_op jit(solution)/shard_map/ppermute | solution.py:776
  347.9 16.4 %collective-permute-done.40 = bf16[160,3200]{1,0:T(8,128)(2,1)S(1)} collective-permute-done((bf16[160,3200]{1,0:T(8,128)(2,1)S(1)}, bf16[160,3200]{1,0:T(8,128)(2,1)S(1)}, u32[]{:S(2)}, u32[]{:S(2)}) %collective-permute-start.40) | collective-permute-done | bytes 1024032 | tf_op jit(solution)/shard_map/ppermute | solution.py:773
  367.0 26.3 %feed_gate.1 = (bf16[1024,1664]{1,0:T(8,128)(2,1)}, bf16[1024,3200]{1,0:T(8,128)(2,1)}) custom-call(bf16[1024,2560]{1,0:T(8,128)(2,1)} %all-gather.9.cloned.1.call-done.left_ref, bf16[320,3200]{1,0:T(8,128)(2,1)} %paired.1.refs_0_.refs_1_.weights_ref, bf16[320,3200]{1,0:T(8,128)(2,1)} %collective-permute-done.31.refs_1_.refs_2_, ...), custom_call_target="tpu_custom_call" | custom-call | flops 1 | bytes 1 | tf_op jit(solution)/shard_map/feed_gate/pallas_call | solution.py:527
  393.3 7.9 convolution_convert_fusion.1
  405.2 9.6 %convolution_convert_fusion = bf16[1280,3200]{1,0:T(8,128)(2,1)S(1)} fusion(bf16[1024,3200]{1,0:T(8,128)(2,1)S(1)} %copy-done.3, bf16[1024,2560]{1,0:T(8,128)(2,1)S(1)} %bitcast.57), kind=kOutput, calls=%fused_computation.2 | convolution fusion | flops 8392704000 | bytes 17367040 | tf_op jit(solution)/shard_map/dot_general | solution.py:50
  426.6 18.1 %feed_terms.4.refs_5_ = bf16[1024,2560]{1,0:T(8,128)(2,1)} custom-call(bf16[1024,3200]{1,0:T(8,128)(2,1)} %get-tuple-element.183.refs_0_, bf16[320,3200]{1,0:T(8,128)(2,1)} %paired.1.refs_0_.refs_1_.weights_ref, bf16[320,3200]{1,0:T(8,128)(2,1)} %collective-permute-done.31.refs_1_.refs_2_, bf16[320,3200]{1,0:T(8,128)(2,1)} %collective-permute-done.35.refs_2_.refs_3_, ...), custom_call_target="tpu_custom_call" | custom-call | flops 1 | bytes 54000000 | tf_op jit(solution)/shard_map/feed_terms/pallas_call | solution.py:569
  451.9 18.1 %feed_terms.5 = bf16[1024,2560]{1,0:T(8,128)(2,1)} custom-call(bf16[1024,3200]{1,0:T(8,128)(2,1)} %get-tuple-element.183.refs_0_, bf16[320,3200]{1,0:T(8,128)(2,1)} %constant_dynamic-update-slice_fusion.2.refs_4_.refs_1_, bf16[320,3200]{1,0:T(8,128)(2,1)} %copy-done.5, ...), custom_call_target="tpu_custom_call", output_to_operand_aliasing={{}: (5, {})} | custom-call | flops 1 | bytes 54000000 | tf_op jit(solution)/shard_map/feed_terms/pallas_call | solution.py:569
  472.4 5.7 convolution_convert_fusion.6
  487.0 5.7 convolution_convert_fusion.5
  492.7 5.3 convolution_convert_fusion.2
  498.0 6.7 convolution_convert_fusion.3
  504.7 13.3 %collective-permute-done.49 = bf16[320,3200]{1,0:T(8,128)(2,1)S(1)} collective-permute-done((bf16[320,3200]{1,0:T(8,128)(2,1)}, bf16[320,3200]{1,0:T(8,128)(2,1)S(1)}, u32[]{:S(2)}, u32[]{:S(2)}) %collective-permute-start.49) | collective-permute-done | bytes 2048032 | tf_op jit(solution)/shard_map/ppermute | solution.py:776
  518.4 3.5 add_convert_fusion.4
  531.2 11.2 %feed_terms.6.refs_5_ = bf16[1024,2560]{1,0:T(8,128)(2,1)} custom-call(bf16[1024,1664]{1,0:T(8,128)(2,1)} %get-tuple-element.188.refs_0_, bf16[320,1664]{1,0:T(8,128)(2,1)} %copy-done.9, bf16[320,1664]{1,0:T(8,128)(2,1)} %collective-permute-done.27.refs_1_.refs_2_, bf16[320,1664]{1,0:T(8,128)(2,1)} %copy-done.17, ...), custom_call_target="tpu_custom_call" | custom-call | flops 1 | bytes 1 | tf_op jit(solution)/shard_map/feed_terms/pallas_call | solution.py:569
  542.5 11.3 %feed_terms.7 = bf16[1024,2560]{1,0:T(8,128)(2,1)} custom-call(bf16[1024,1664]{1,0:T(8,128)(2,1)} %get-tuple-element.188.refs_0_, bf16[320,1664]{1,0:T(8,128)(2,1)} %constant_dynamic-update-slice_fusion.refs_4_.refs_1_, bf16[320,1664]{1,0:T(8,128)(2,1)} %copy-done.11, bf16[320,1664]{1,0:T(8,128)(2,1)} %copy-done.16, ...), custom_call_target="tpu_custom_call", output_to_operand_aliasing={{}: (5, {})} | custom-call | flops 1 | bytes 1 | tf_op jit(solution)/shard_map/feed_terms/pallas_call | solution.py:569
  557.0 37.8 %collective-permute-done.53 = bf16[320,3200]{1,0:T(8,128)(2,1)S(1)} collective-permute-done((bf16[320,3200]{1,0:T(8,128)(2,1)}, bf16[320,3200]{1,0:T(8,128)(2,1)S(1)}, u32[]{:S(2)}, u32[]{:S(2)}) %collective-permute-start.53) | collective-permute-done | bytes 2048032 | tf_op jit(solution)/shard_map/ppermute | solution.py:776
  602.0 8.9 %convolution_convert_fusion.8.grad_ref = bf16[1024,640]{1,0:T(8,128)(2,1)} fusion(bf16[1024,2560]{1,0:T(8,128)(2,1)} %all-gather.11.cloned.1.call-done.upstream_ref, bf16[2560,640]{1,0:T(8,128)(2,1)} %get-tuple-element.152), kind=kOutput, calls=%fused_computation.36 | convolution fusion | flops 3356098560 | bytes 9830400 | tf_op jit(solution)/shard_map/dot_general | solution.py:46
  610.9 31.3 %attention_backward.1 = (bf16[1024,1280]{1,0:T(8,128)(2,1)}, bf16[1024,1280]{1,0:T(8,128)(2,1)}, f32[1024,128]{1,0:T(8,128)}) custom-call(bf16[1024,1280]{1,0:T(8,128)(2,1)} %get-tuple-element.189.q_ref, bf16[1024,1280]{1,0:T(8,128)(2,1)} %get-tuple-element.190.kv_ref, bf16[1024,640]{1,0:T(8,128)(2,1)} %convolution_convert_fusion.8.grad_ref, ...), custom_call_target="tpu_custom_call" | custom-call | flops 1 | bytes 1 | tf_op jit(solution)/shard_map/attention_backward/pallas_call | solution.py:249
  656.3 19.7 %head_sums.1 = bf16[2304,1280]{1,0:T(8,128)(2,1)} custom-call(s32[8]{0:T(128)} %compare_select_fusion.11.spots_ref.refs_0_, bf16[1024,1152]{1,0:T(8,128)(2,1)} %all-gather.5.cloned.1.call-done.xq_ref.lat_ref.latents_ref, bf16[1024,1280]{1,0:T(8,128)(2,1)} %get-tuple-element.206.query_ref, bf16[1024,1280]{1,0:T(8,128)(2,1)} %get-tuple-element.207.key_value_ref, ...), custom_call_target="tpu_custom_call" | custom-call | flops 1 | bytes 60000000 | tf_op jit(solution)/shard_map/head_sums/pallas_call | solution.py:689
  679.4 4.1 reduce-scatter.11.cloned.1.call-done.back_ref
  683.5 7.7 latent_back.1
  696.9 5.6 collective-permute-done.59
  705.9 8.0 token_back.1.in_ref
  716.6 5.1 reorder.6
  726.6 8.1 collective-permute-done.69
  742.7 16.1 %collective-permute-done.64 = bf16[160,1152]{1,0:T(8,128)(2,1)S(1)} collective-permute-done((bf16[160,1152]{1,0:T(8,128)(2,1)S(1)}, bf16[160,1152]{1,0:T(8,128)(2,1)S(1)}, u32[]{:S(2)}, u32[]{:S(2)}) %collective-permute-start.64) | collective-permute-done | bytes 368672 | tf_op jit(solution)/shard_map/ppermute | solution.py:776
  765.2 7.0 collective-permute-done.65
  778.8 3.7 reorder.7
  782.5 6.5 unpaired.1
  (451 shorter events, 214.6 us)
Async XLA Ops:
  7.3 160.1 %all-gather.5.cloned.1.call-start = ((), (), s32[]{:S(2)}) async-start(), calls=%async_computation.4 | async-start | bytes 2949120 | tf_op jit(solution)/shard_map/all_gather | solution.py:1059
  29.6 27.0 %collective-permute-start.7 = (bf16[288,1280]{1,0:T(8,128)(2,1)}, bf16[288,1280]{1,0:T(8,128)(2,1)}, u32[]{:S(2)}, u32[]{:S(2)}) collective-permute-start(bf16[288,1280]{1,0:T(8,128)(2,1)} %collective-permute-done.6.refs_8_), channel_id=1, source_target_pairs={{0,8},{8,16},{16,24},{24,28},{28,20},{20,12},{12,4},{4,0},{1,9},{9... | collective-permute-start | bytes 2211848 | tf_op jit(solution)/shard_map/ppermute | solution.py:773
  31.4 25.2 %collective-permute-start.9 = (bf16[288,1280]{1,0:T(8,128)(2,1)}, bf16[288,1280]{1,0:T(8,128)(2,1)}, u32[]{:S(2)}, u32[]{:S(2)}) collective-permute-start(bf16[288,1280]{1,0:T(8,128)(2,1)} %collective-permute-done.8.refs_2_), channel_id=1, source_target_pairs={{8,0},{16,8},{24,16},{28,24},{20,28},{12,20},{4,12},{0,4},{9,1},{1... | collective-permute-start | bytes 2211848 | tf_op jit(solution)/shard_map/ppermute | solution.py:776
  31.7 24.9 %collective-permute-start.2 = (bf16[160,1152]{1,0:T(8,128)(2,1)S(1)}, bf16[160,1152]{1,0:T(8,128)(2,1)S(1)}, u32[]{:S(2)}, u32[]{:S(2)}) collective-permute-start(bf16[160,1152]{1,0:T(8,128)(2,1)S(1)} %pad_maximum_fusion.8.refs_0_.refs_8_), channel_id=1, source_target_pairs={{8,0},{16,8},{24,16},{28,24},{20,28},{12,20},{4,12},{0,4},{9,1},{1... | collective-permute-start | bytes 1105928 | tf_op jit(solution)/shard_map/ppermute | solution.py:776
  33.5 23.1 %collective-permute-start.1 = (bf16[160,1152]{1,0:T(8,128)(2,1)S(1)}, bf16[160,1152]{1,0:T(8,128)(2,1)S(1)}, u32[]{:S(2)}, u32[]{:S(2)}) collective-permute-start(bf16[160,1152]{1,0:T(8,128)(2,1)S(1)} %pad_maximum_fusion.8.refs_0_.refs_8_), channel_id=1, source_target_pairs={{0,1},{1,0},{2,3},{3,2},{4,5},{5,4},{6,7},{7,6},{8,9},{9,8},{10,11... | collective-permute-start | bytes 1105928 | tf_op jit(solution)/shard_map/ppermute | solution.py:908
  33.5 23.1 %collective-permute-start.4 = (bf16[160,1152]{1,0:T(8,128)(2,1)S(1)}, bf16[160,1152]{1,0:T(8,128)(2,1)S(1)}, u32[]{:S(2)}, u32[]{:S(2)}) collective-permute-start(bf16[160,1152]{1,0:T(8,128)(2,1)S(1)} %pad_maximum_fusion.8.refs_0_.refs_8_), channel_id=1, source_target_pairs={{0,8},{8,16},{16,24},{24,28},{28,20},{20,12},{12,4},{4,0},{1,9},{9... | collective-permute-start | bytes 1105928 | tf_op jit(solution)/shard_map/ppermute | solution.py:773
  57.9 26.8 %collective-permute-start.14 = (bf16[288,1280]{1,0:T(8,128)(2,1)}, bf16[288,1280]{1,0:T(8,128)(2,1)S(1)}, u32[]{:S(2)}, u32[]{:S(2)}) collective-permute-start(bf16[288,1280]{1,0:T(8,128)(2,1)} %collective-permute-done.7.refs_7_), channel_id=1, source_target_pairs={{0,8},{8,16},{16,24},{24,28},{28,20},{20,12},{12,4},{4,0},{1,9},{9... | collective-permute-start | bytes 2211848 | tf_op jit(solution)/shard_map/ppermute | solution.py:773
  59.4 26.1 %collective-permute-start.15 = (bf16[288,1280]{1,0:T(8,128)(2,1)}, bf16[288,1280]{1,0:T(8,128)(2,1)}, u32[]{:S(2)}, u32[]{:S(2)}) collective-permute-start(bf16[288,1280]{1,0:T(8,128)(2,1)} %collective-permute-done.9.refs_3_), channel_id=1, source_target_pairs={{8,0},{16,8},{24,16},{28,24},{20,28},{12,20},{4,12},{0,4},{9,1},{1... | collective-permute-start | bytes 2211848 | tf_op jit(solution)/shard_map/ppermute | solution.py:776
  60.0 24.8 %collective-permute-start.5 = (bf16[160,1152]{1,0:T(8,128)(2,1)S(1)}, bf16[160,1152]{1,0:T(8,128)(2,1)S(1)}, u32[]{:S(2)}, u32[]{:S(2)}) collective-permute-start(bf16[160,1152]{1,0:T(8,128)(2,1)S(1)} %collective-permute-done.4.refs_4_.refs_12_), channel_id=1, source_target_pairs={{0,1},{1,0},{2,3},{3,2},{4,5},{5,4},{6,7},{7,6},{8,9},{9,8},{10,11... | collective-permute-start | bytes 1105928 | tf_op jit(solution)/shard_map/ppermute | solution.py:908
  60.1 24.7 %collective-permute-start.12 = (bf16[160,1152]{1,0:T(8,128)(2,1)S(1)}, bf16[160,1152]{1,0:T(8,128)(2,1)}, u32[]{:S(2)}, u32[]{:S(2)}) collective-permute-start(bf16[160,1152]{1,0:T(8,128)(2,1)S(1)} %collective-permute-done.4.refs_4_.refs_12_), channel_id=1, source_target_pairs={{0,8},{8,16},{16,24},{24,28},{28,20},{20,12},{12,4},{4,0},{1,9},{9... | collective-permute-start | bytes 1105928 | tf_op jit(solution)/shard_map/ppermute | solution.py:773
  114.8 25.2 %collective-permute-start.26 = (bf16[320,1664]{1,0:T(8,128)(2,1)S(1)}, bf16[320,1664]{1,0:T(8,128)(2,1)}, u32[]{:S(2)}, u32[]{:S(2)}) collective-permute-start(bf16[320,1664]{1,0:T(8,128)(2,1)S(1)} %pad.18.refs_0_.refs_1_), channel_id=1, source_target_pairs={{0,8},{8,16},{16,24},{24,28},{28,20},{20,12},{12,4},{4,0},{1,9},{9... | collective-permute-start | bytes 3194888 | tf_op jit(solution)/shard_map/ppermute | solution.py:773
  116.4 24.0 %collective-permute-start.27 = (bf16[320,1664]{1,0:T(8,128)(2,1)S(1)}, bf16[320,1664]{1,0:T(8,128)(2,1)}, u32[]{:S(2)}, u32[]{:S(2)}) collective-permute-start(bf16[320,1664]{1,0:T(8,128)(2,1)S(1)} %pad.18.refs_0_.refs_1_), channel_id=1, source_target_pairs={{8,0},{16,8},{24,16},{28,24},{20,28},{12,20},{4,12},{0,4},{9,1},{1... | collective-permute-start | bytes 3194888 | tf_op jit(solution)/shard_map/ppermute | solution.py:776
  140.4 77.2 %all-gather.7.cloned.1.call-start = ((), (), s32[]{:S(2)}) async-start(), calls=%async_computation.5 | async-start | bytes 6553600 | tf_op jit(solution)/shard_map/all_gather | solution.py:1096
  140.4 25.4 %collective-permute-start.28 = (bf16[320,1664]{1,0:T(8,128)(2,1)}, bf16[320,1664]{1,0:T(8,128)(2,1)S(1)}, u32[]{:S(2)}, u32[]{:S(2)}) collective-permute-start(bf16[320,1664]{1,0:T(8,128)(2,1)} %collective-permute-done.26.refs_7_.refs_4_), channel_id=1, source_target_pairs={{0,8},{8,16},{16,24},{24,28},{28,20},{20,12},{12,4},{4,0},{1,9},{9... | collective-permute-start | bytes 3194888 | tf_op jit(solution)/shard_map/ppermute | solution.py:773
  142.1 25.3 %collective-permute-start.29 = (bf16[320,1664]{1,0:T(8,128)(2,1)}, bf16[320,1664]{1,0:T(8,128)(2,1)S(1)}, u32[]{:S(2)}, u32[]{:S(2)}) collective-permute-start(bf16[320,1664]{1,0:T(8,128)(2,1)} %collective-permute-done.27.refs_1_.refs_2_), channel_id=1, source_target_pairs={{8,0},{16,8},{24,16},{28,24},{20,28},{12,20},{4,12},{0,4},{9,1},{1... | collective-permute-start | bytes 3194888 | tf_op jit(solution)/shard_map/ppermute | solution.py:776
  167.4 101.0 %reduce-scatter.5.cloned.1.call-start = ((), (), s32[]{:S(2)}) async-start(), calls=%async_computation.6 | async-start | bytes 6553600 | tf_op jit(solution)/shard_map/reduce_scatter | solution.py:1103
  170.9 45.3 %collective-permute-start.30 = (bf16[320,3200]{1,0:T(8,128)(2,1)}, bf16[320,3200]{1,0:T(8,128)(2,1)}, u32[]{:S(2)}, u32[]{:S(2)}) collective-permute-start(bf16[320,3200]{1,0:T(8,128)(2,1)} %paired.1.refs_0_.refs_1_.weights_ref), channel_id=1, source_target_pairs={{0,8},{8,16},{16,24},{24,28},{28,20},{20,12},{12,4},{4,0},{1,9},{9... | collective-permute-start | bytes 6144008 | tf_op jit(solution)/shard_map/ppermute | solution.py:773
  172.5 45.1 %collective-permute-start.31 = (bf16[320,3200]{1,0:T(8,128)(2,1)}, bf16[320,3200]{1,0:T(8,128)(2,1)}, u32[]{:S(2)}, u32[]{:S(2)}) collective-permute-start(bf16[320,3200]{1,0:T(8,128)(2,1)} %paired.1.refs_0_.refs_1_.weights_ref), channel_id=1, source_target_pairs={{8,0},{16,8},{24,16},{28,24},{20,28},{12,20},{4,12},{0,4},{9,1},{1... | collective-permute-start | bytes 6144008 | tf_op jit(solution)/shard_map/ppermute | solution.py:776
  217.6 149.4 %all-gather.9.cloned.1.call-start = ((), (), s32[]{:S(2)}) async-start(), calls=%async_computation.7 | async-start | bytes 6553600 | tf_op jit(solution)/shard_map/all_gather | solution.py:1113
  217.6 26.7 %collective-permute-start.32 = (bf16[320,1664]{1,0:T(8,128)(2,1)}, bf16[320,1664]{1,0:T(8,128)(2,1)S(1)}, u32[]{:S(2)}, u32[]{:S(2)}) collective-permute-start(bf16[320,1664]{1,0:T(8,128)(2,1)} %copy-done.16), channel_id=1, source_target_pairs={{0,8},{8,16},{16,24},{24,28},{28,20},{20,12},{12,4},{4,0},{1,9},{9... | collective-permute-start | bytes 3194888 | tf_op jit(solution)/shard_map/ppermute | solution.py:773
  219.2 26.8 %collective-permute-start.33 = (bf16[320,1664]{1,0:T(8,128)(2,1)}, bf16[320,1664]{1,0:T(8,128)(2,1)}, u32[]{:S(2)}, u32[]{:S(2)}) collective-permute-start(bf16[320,1664]{1,0:T(8,128)(2,1)} %copy-done.17), channel_id=1, source_target_pairs={{8,0},{16,8},{24,16},{28,24},{20,28},{12,20},{4,12},{0,4},{9,1},{1... | collective-permute-start | bytes 3194888 | tf_op jit(solution)/shard_map/ppermute | solution.py:776
  219.7 64.9 %collective-permute-start.34 = (bf16[320,3200]{1,0:T(8,128)(2,1)}, bf16[320,3200]{1,0:T(8,128)(2,1)}, u32[]{:S(2)}, u32[]{:S(2)}) collective-permute-start(bf16[320,3200]{1,0:T(8,128)(2,1)} %collective-permute-done.30.refs_7_.refs_4_), channel_id=1, source_target_pairs={{0,8},{8,16},{16,24},{24,28},{28,20},{20,12},{12,4},{4,0},{1,9},{9... | collective-permute-start | bytes 6144008 | tf_op jit(solution)/shard_map/ppermute | solution.py:773
  221.2 64.7 %collective-permute-start.35 = (bf16[320,3200]{1,0:T(8,128)(2,1)}, bf16[320,3200]{1,0:T(8,128)(2,1)}, u32[]{:S(2)}, u32[]{:S(2)}) collective-permute-start(bf16[320,3200]{1,0:T(8,128)(2,1)} %collective-permute-done.31.refs_1_.refs_2_), channel_id=1, source_target_pairs={{8,0},{16,8},{24,16},{28,24},{20,28},{12,20},{4,12},{0,4},{9,1},{1... | collective-permute-start | bytes 6144008 | tf_op jit(solution)/shard_map/ppermute | solution.py:776
  285.9 237.8 %reduce-scatter.7.cloned.1.call-start = ((), (), s32[]{:S(2)}) async-start(), calls=%async_computation.8 | async-start | bytes 6553600 | tf_op jit(solution)/shard_map/reduce_scatter | solution.py:1138
  301.7 42.8 %collective-permute-start.38 = (bf16[320,3200]{1,0:T(8,128)(2,1)}, bf16[320,3200]{1,0:T(8,128)(2,1)S(1)}, u32[]{:S(2)}, u32[]{:S(2)}) collective-permute-start(bf16[320,3200]{1,0:T(8,128)(2,1)} %collective-permute-done.35.refs_2_.refs_3_), channel_id=1, source_target_pairs={{8,0},{16,8},{24,16},{28,24},{20,28},{12,20},{4,12},{0,4},{9,1},{1... | collective-permute-start | bytes 6144008 | tf_op jit(solution)/shard_map/ppermute | solution.py:776
  301.7 42.8 %collective-permute-start.39 = (bf16[320,3200]{1,0:T(8,128)(2,1)}, bf16[320,3200]{1,0:T(8,128)(2,1)S(1)}, u32[]{:S(2)}, u32[]{:S(2)}) collective-permute-start(bf16[320,3200]{1,0:T(8,128)(2,1)} %collective-permute-done.34.refs_6_.refs_3_), channel_id=1, source_target_pairs={{0,8},{8,16},{16,24},{24,28},{28,20},{20,12},{12,4},{4,0},{1,9},{9... | collective-permute-start | bytes 6144008 | tf_op jit(solution)/shard_map/ppermute | solution.py:773
  418.7 26.0 %collective-permute-start.44 = (bf16[160,3200]{1,0:T(8,128)(2,1)}, bf16[160,3200]{1,0:T(8,128)(2,1)}, u32[]{:S(2)}, u32[]{:S(2)}) collective-permute-start(bf16[160,3200]{1,0:T(8,128)(2,1)} %get-tuple-element.281), channel_id=1, source_target_pairs={{0,8},{8,16},{16,24},{24,28},{28,20},{20,12},{12,4},{4,0},{1,9},{9... | collective-permute-start | bytes 3072008 | tf_op jit(solution)/shard_map/ppermute | solution.py:773
  420.5 25.9 %collective-permute-start.45 = (bf16[160,3200]{1,0:T(8,128)(2,1)}, bf16[160,3200]{1,0:T(8,128)(2,1)}, u32[]{:S(2)}, u32[]{:S(2)}) collective-permute-start(bf16[160,3200]{1,0:T(8,128)(2,1)} %get-tuple-element.280), channel_id=1, source_target_pairs={{8,0},{16,8},{24,16},{28,24},{20,28},{12,20},{4,12},{0,4},{9,1},{1... | collective-permute-start | bytes 3072008 | tf_op jit(solution)/shard_map/ppermute | solution.py:776
  423.3 46.7 %collective-permute-start.47 = (bf16[320,1664]{1,0:T(8,128)(2,1)}, bf16[320,1664]{1,0:T(8,128)(2,1)}, u32[]{:S(2)}, u32[]{:S(2)}) collective-permute-start(bf16[320,1664]{1,0:T(8,128)(2,1)} %pad_maximum_fusion.4), channel_id=1, source_target_pairs={{8,0},{16,8},{24,16},{28,24},{20,28},{12,20},{4,12},{0,4},{9,1},{1... | collective-permute-start | bytes 3194888 | tf_op jit(solution)/shard_map/ppermute | solution.py:776
  424.5 45.6 %collective-permute-start.46 = (bf16[320,1664]{1,0:T(8,128)(2,1)}, bf16[320,1664]{1,0:T(8,128)(2,1)}, u32[]{:S(2)}, u32[]{:S(2)}) collective-permute-start(bf16[320,1664]{1,0:T(8,128)(2,1)} %pad_maximum_fusion.3), channel_id=1, source_target_pairs={{0,8},{8,16},{16,24},{24,28},{28,20},{20,12},{12,4},{4,0},{1,9},{9... | collective-permute-start | bytes 3194888 | tf_op jit(solution)/shard_map/ppermute | solution.py:773
  470.1 131.9 %all-gather.11.cloned.1.call-start = ((), (), s32[]{:S(2)}) async-start(), calls=%async_computation.10 | async-start | bytes 6553600 | tf_op jit(solution)/shard_map/all_gather | solution.py:1152
  470.2 47.8 %collective-permute-start.49 = (bf16[320,3200]{1,0:T(8,128)(2,1)}, bf16[320,3200]{1,0:T(8,128)(2,1)S(1)}, u32[]{:S(2)}, u32[]{:S(2)}) collective-permute-start(bf16[320,3200]{1,0:T(8,128)(2,1)} %pad_maximum_fusion.2), channel_id=1, source_target_pairs={{8,0},{16,8},{24,16},{28,24},{20,28},{12,20},{4,12},{0,4},{9,1},{1... | collective-permute-start | bytes 6144008 | tf_op jit(solution)/shard_map/ppermute | solution.py:776
  470.5 47.9 %collective-permute-start.48 = (bf16[320,3200]{1,0:T(8,128)(2,1)}, bf16[320,3200]{1,0:T(8,128)(2,1)S(1)}, u32[]{:S(2)}, u32[]{:S(2)}) collective-permute-start(bf16[320,3200]{1,0:T(8,128)(2,1)} %pad_maximum_fusion.1), channel_id=1, source_target_pairs={{0,8},{8,16},{16,24},{24,28},{28,20},{20,12},{12,4},{4,0},{1,9},{9... | collective-permute-start | bytes 6144008 | tf_op jit(solution)/shard_map/ppermute | solution.py:773
  482.2 48.3 %collective-permute-start.51 = (bf16[320,1664]{1,0:T(8,128)(2,1)}, bf16[320,1664]{1,0:T(8,128)(2,1)}, u32[]{:S(2)}, u32[]{:S(2)}) collective-permute-start(bf16[320,1664]{1,0:T(8,128)(2,1)} %add_convert_fusion.8), channel_id=1, source_target_pairs={{8,0},{16,8},{24,16},{28,24},{20,28},{12,20},{4,12},{0,4},{9,1},{1... | collective-permute-start | bytes 3194888 | tf_op jit(solution)/shard_map/ppermute | solution.py:776
  485.1 45.7 %collective-permute-start.50 = (bf16[320,1664]{1,0:T(8,128)(2,1)}, bf16[320,1664]{1,0:T(8,128)(2,1)}, u32[]{:S(2)}, u32[]{:S(2)}) collective-permute-start(bf16[320,1664]{1,0:T(8,128)(2,1)} %add_convert_fusion.9), channel_id=1, source_target_pairs={{0,8},{8,16},{16,24},{24,28},{28,20},{20,12},{12,4},{4,0},{1,9},{9... | collective-permute-start | bytes 3194888 | tf_op jit(solution)/shard_map/ppermute | solution.py:773
  530.8 119.5 %reduce-scatter.9.cloned.1.call-start = ((), (), s32[]{:S(2)}) async-start(), calls=%async_computation.9 | async-start | bytes 6553600 | tf_op jit(solution)/shard_map/reduce_scatter | solution.py:1158
  553.8 129.7 %reduce-scatter.11.cloned.1.call-start = ((), (), s32[]{:S(2)}) async-start(), calls=%async_computation.11 | async-start | bytes 2949120 | tf_op jit(solution)/shard_map/reduce_scatter | solution.py:1178
  553.8 41.0 %collective-permute-start.53 = (bf16[320,3200]{1,0:T(8,128)(2,1)}, bf16[320,3200]{1,0:T(8,128)(2,1)S(1)}, u32[]{:S(2)}, u32[]{:S(2)}) collective-permute-start(bf16[320,3200]{1,0:T(8,128)(2,1)} %add_convert_fusion.3), channel_id=1, source_target_pairs={{8,0},{16,8},{24,16},{28,24},{20,28},{12,20},{4,12},{0,4},{9,1},{1... | collective-permute-start | bytes 6144008 | tf_op jit(solution)/shard_map/ppermute | solution.py:776
  555.3 40.6 %collective-permute-start.52 = (bf16[320,3200]{1,0:T(8,128)(2,1)S(1)}, bf16[320,3200]{1,0:T(8,128)(2,1)S(1)}, u32[]{:S(2)}, u32[]{:S(2)}) collective-permute-start(bf16[320,3200]{1,0:T(8,128)(2,1)S(1)} %copy-done.30), channel_id=1, source_target_pairs={{0,8},{8,16},{16,24},{24,28},{28,20},{20,12},{12,4},{4,0},{1,9},{9... | collective-permute-start | bytes 6144008 | tf_op jit(solution)/shard_map/ppermute | solution.py:773
  599.8 42.4 %collective-permute-start.55 = (bf16[320,3200]{1,0:T(8,128)(2,1)}, bf16[320,3200]{1,0:T(8,128)(2,1)}, u32[]{:S(2)}, u32[]{:S(2)}) collective-permute-start(bf16[320,3200]{1,0:T(8,128)(2,1)} %add_convert_fusion.1), channel_id=1, source_target_pairs={{8,0},{16,8},{24,16},{28,24},{20,28},{12,20},{4,12},{0,4},{9,1},{1... | collective-permute-start | bytes 6144008 | tf_op jit(solution)/shard_map/ppermute | solution.py:776
  601.3 40.9 %collective-permute-start.54 = (bf16[320,3200]{1,0:T(8,128)(2,1)S(1)}, bf16[320,3200]{1,0:T(8,128)(2,1)}, u32[]{:S(2)}, u32[]{:S(2)}) collective-permute-start(bf16[320,3200]{1,0:T(8,128)(2,1)S(1)} %add_convert_fusion.2), channel_id=1, source_target_pairs={{0,8},{8,16},{16,24},{24,28},{28,20},{20,12},{12,4},{4,0},{1,9},{9... | collective-permute-start | bytes 6144008 | tf_op jit(solution)/shard_map/ppermute | solution.py:773
  654.0 24.4 %collective-permute-start.57 = (bf16[320,1664]{1,0:T(8,128)(2,1)S(1)}, bf16[320,1664]{1,0:T(8,128)(2,1)S(1)}, u32[]{:S(2)}, u32[]{:S(2)}) collective-permute-start(bf16[320,1664]{1,0:T(8,128)(2,1)S(1)} %add_convert_fusion.6), channel_id=1, source_target_pairs={{8,0},{16,8},{24,16},{28,24},{20,28},{12,20},{4,12},{0,4},{9,1},{1... | collective-permute-start | bytes 3194888 | tf_op jit(solution)/shard_map/ppermute | solution.py:776
  655.5 23.9 %collective-permute-start.56 = (bf16[320,1664]{1,0:T(8,128)(2,1)S(1)}, bf16[320,1664]{1,0:T(8,128)(2,1)}, u32[]{:S(2)}, u32[]{:S(2)}) collective-permute-start(bf16[320,1664]{1,0:T(8,128)(2,1)S(1)} %add_convert_fusion.7), channel_id=1, source_target_pairs={{0,8},{8,16},{16,24},{24,28},{28,20},{20,12},{12,4},{4,0},{1,9},{9... | collective-permute-start | bytes 3194888 | tf_op jit(solution)/shard_map/ppermute | solution.py:773
  691.2 30.5 %collective-permute-start.58 = (bf16[1280,1152]{1,0:T(8,128)(2,1)}, bf16[1280,1152]{1,0:T(8,128)(2,1)}, u32[]{:S(2)}, u32[]{:S(2)}) collective-permute-start(bf16[1280,1152]{1,0:T(8,128)(2,1)} %get-tuple-element.213), channel_id=1, source_target_pairs={{0,1},{1,0},{2,3},{3,2},{4,5},{5,4},{6,7},{7,6},{8,9},{9,8},{10,11... | collective-permute-start | bytes 8847368 | tf_op jit(solution)/shard_map/ppermute | solution.py:908
  735.1 27.6 %collective-permute-start.71 = (bf16[288,1280]{1,0:T(8,128)(2,1)S(1)}, bf16[288,1280]{1,0:T(8,128)(2,1)S(1)}, u32[]{:S(2)}, u32[]{:S(2)}) collective-permute-start(bf16[288,1280]{1,0:T(8,128)(2,1)S(1)} %get-tuple-element.287), channel_id=1, source_target_pairs={{0,8},{8,16},{16,24},{24,28},{28,20},{20,12},{12,4},{4,0},{1,9},{9... | collective-permute-start | bytes 2211848 | tf_op jit(solution)/shard_map/ppermute | solution.py:773
  736.6 26.1 %collective-permute-start.72 = (bf16[288,1280]{1,0:T(8,128)(2,1)S(1)}, bf16[288,1280]{1,0:T(8,128)(2,1)S(1)}, u32[]{:S(2)}, u32[]{:S(2)}) collective-permute-start(bf16[288,1280]{1,0:T(8,128)(2,1)S(1)} %get-tuple-element.286), channel_id=1, source_target_pairs={{8,0},{16,8},{24,16},{28,24},{20,28},{12,20},{4,12},{0,4},{9,1},{1... | collective-permute-start | bytes 2211848 | tf_op jit(solution)/shard_map/ppermute | solution.py:776
  763.1 32.1 %collective-permute-start.73 = (bf16[288,1280]{1,0:T(8,128)(2,1)S(1)}, bf16[288,1280]{1,0:T(8,128)(2,1)S(1)}, u32[]{:S(2)}, u32[]{:S(2)}) collective-permute-start(bf16[288,1280]{1,0:T(8,128)(2,1)S(1)} %get-tuple-element.285), channel_id=1, source_target_pairs={{0,8},{8,16},{16,24},{24,28},{28,20},{20,12},{12,4},{4,0},{1,9},{9... | collective-permute-start | bytes 2211848 | tf_op jit(solution)/shard_map/ppermute | solution.py:773
  764.6 30.6 %collective-permute-start.74 = (bf16[288,1280]{1,0:T(8,128)(2,1)S(1)}, bf16[288,1280]{1,0:T(8,128)(2,1)S(1)}, u32[]{:S(2)}, u32[]{:S(2)}) collective-permute-start(bf16[288,1280]{1,0:T(8,128)(2,1)S(1)} %get-tuple-element.284), channel_id=1, source_target_pairs={{8,0},{16,8},{24,16},{28,24},{20,28},{12,20},{4,12},{0,4},{9,1},{1... | collective-permute-start | bytes 2211848 | tf_op jit(solution)/shard_map/ppermute | solution.py:776
  (117 other events, 1850.4 us)
Sparse Core Ops, SparseCore 0:
  140.5 25.1 all-gather.4
  167.9 40.4 all-gather.6
  217.7 50.6 reduce-scatter.4
  286.0 39.1 all-gather.8
  470.2 48.8 reduce-scatter.6
  530.9 40.3 all-gather.10
  573.9 51.3 reduce-scatter.8
  650.4 33.0 reduce-scatter.10

commit v2 on v1

--- a/solution.py
+++ b/solution.py
@@ -164,7 +164,7 @@
         ],
         scratch_shapes=[pltpu.VMEM((2, length, LANES), low)],
         compiler_params=pltpu.CompilerParams(vmem_limit_bytes=ROOM),
-        cost_estimate=BRIEF,
+        cost_estimate=lasting(23),
         name="attention_forward",
     )(latents, latents, wq, wkv, rope, feat, *tables)
 
@@ -267,7 +267,7 @@
             pltpu.VMEM((length, LANES), jnp.float32),
         ],
         compiler_params=pltpu.CompilerParams(vmem_limit_bytes=ROOM),
-        cost_estimate=BRIEF,
+        cost_estimate=lasting(31),
         name="attention_backward",
     )(query, key_value, grad, lse, rope, *tables)
 
@@ -309,7 +309,7 @@
         out_shape=[jax.ShapeDtypeStruct(shape, jnp.bfloat16) for shape in shapes],
         scratch_shapes=[pltpu.SemaphoreType.DMA((len(copies),))],
         compiler_params=pltpu.CompilerParams(vmem_limit_bytes=ROOM),
-        cost_estimate=BRIEF,
+        cost_estimate=lasting(6),
         name="assemble",
     )(spots, *pieces)
 
@@ -338,7 +338,7 @@
         out_specs=pl.BlockSpec((16 * len(copies), LANES), lambda: (0, 0)),
         out_shape=jax.ShapeDtypeStruct((16 * len(copies), LANES), jnp.bfloat16),
         scratch_shapes=[pltpu.SemaphoreType.DMA((len(copies),))],
-        cost_estimate=BRIEF,
+        cost_estimate=lasting(3),
         name="collect",
     )(teams, *pieces)
 
@@ -390,7 +390,7 @@
         out_shape=[jax.ShapeDtypeStruct(*shape) for shape in shapes],
         scratch_shapes=[pltpu.SemaphoreType.DMA((len(copies),))],
         compiler_params=pltpu.CompilerParams(vmem_limit_bytes=ROOM),
-        cost_estimate=BRIEF,
+        cost_estimate=lasting(10),
         name="project",
     )(teams, tokens, *gains, *tables, *pieces)
 
@@ -534,7 +534,7 @@
             jax.ShapeDtypeStruct((rows, pair_width), jnp.bfloat16),
         ],
         compiler_params=pltpu.CompilerParams(vmem_limit_bytes=ROOM),
-        cost_estimate=BRIEF,
+        cost_estimate=lasting(26),
         name="feed_gate",
     )(left, *pieces, upstream)
 
@@ -633,7 +633,7 @@
         + [jax.ShapeDtypeStruct(*shape) for shape in shapes],
         scratch_shapes=[pltpu.VMEM((width, out), low), pltpu.SemaphoreType.DMA((len(copies),))],
         compiler_params=pltpu.CompilerParams(vmem_limit_bytes=ROOM),
-        cost_estimate=BRIEF,
+        cost_estimate=lasting(8),
         name="latent_back",
     )(teams, *arrays)
     return results[:-1], results[-1]
@@ -1007,6 +1007,7 @@
 
     collect(small_up.low, 0, 0)
     mixed_up.advance()
+    down_up.advance()
     while not small_up.done:
         swapped = pieces[1::2]
         small_up.advance()
@@ -1014,7 +1015,7 @@
         if not small_up.done:
             collect(small_up.high, small_up.step, 0)
             collect(small_up.low, ring.count - small_up.step, 0)
-            hold(small_up, ends(mixed_up), swapped)
+            hold(small_up, ends(mixed_up, down_up), swapped)
             hold(mixed_up, ends(small_up))
     collect(small_up.low, ring.half, 0)
     collect(small_up.high, ring.half, 1)
@@ -1101,19 +1102,16 @@
     branch_terms = product_right(heads, attention_out_t).astype(low)
     branch_terms = follow(branch_terms, feed_upstream, ends(pair_up))
     attention_branch = lax.psum_scatter(branch_terms, "tensor", scatter_dimension=0, tiled=True)
-    attention_branch = follow(attention_branch, ends(down_up))
     downs = down_up.finish()
     if ring.count > 8:
         downs = [jnp.concatenate(downs, axis=0)]
     activated_grad = feed_product(feed_upstream, downs)
+    attention_branch = follow(attention_branch, activated_grad)
     hidden = tokens_ring.astype(jnp.float32) + RESIDUAL * attention_branch.astype(jnp.float32)
     feed_normed, inverse_hidden = normalize(hidden, gain_hidden)
     pair_up.advance()
     feed_normed = follow(feed_normed.astype(low), ends(pair_up))
     feed_seq = lax.all_gather(feed_normed, "tensor", axis=0, tiled=True)
-    hold(pair_up, ends(down_up))
-    pair_up.advance()
-    hold(pair_up, activated_grad)
     weights = pair_up.finish()
     if ring.count > 8:
         weights = [jnp.concatenate(weights, axis=0)]
@@ -1150,11 +1148,14 @@
     hidden_grad = upstream.astype(jnp.float32) + hidden_back
     upstream_send = follow((RESIDUAL * hidden_grad).astype(low), grad_pair.sent, ends(grad_down))
     attention_upstream = lax.all_gather(upstream_send, "tensor", axis=0, tiled=True)
+    grad_down.advance()
     activated = follow(activated, upstream_send)
-    feed_branch = feed_terms(activated, downs[:half], width, 0, None, BRIEF)
+    feed_branch = feed_terms(activated, downs[:half], width, 0, None, lasting(11))
     if len(downs) > half:
-        feed_branch = feed_terms(activated, downs[half:], width, 1, feed_branch, BRIEF)
-    attention_upstream = follow(attention_upstream, feed_branch, ends(grad_pair))
+        feed_branch = feed_terms(activated, downs[half:], width, 1, feed_branch, lasting(11))
+    attention_upstream = follow(
+        attention_upstream, feed_branch, ends(grad_pair), grad_down.sent
+    )
     feed_branch = lax.psum_scatter(feed_branch, "tensor", scatter_dimension=0, tiled=True)
     heads_grad = product(attention_upstream, attention_out_t).astype(low)
     grad_pair.advance()
@@ -1162,9 +1163,7 @@
     query_raw_grad, key_value_grad, key_rope_grad = attention_backward(
         query_heads, key_value, heads_grad, log_totals, rope, tables
     )
-    query_raw_grad, key_value_grad = follow((query_raw_grad, key_value_grad), ends(grad_pair))
-    hold(grad_down, query_raw_grad)
-    grad_down.advance()
+    query_raw_grad, key_value_grad = follow((query_raw_grad, key_value_grad), ends(grad_down))
     latent_terms = jnp.concatenate(
         [
             product_right(query_raw_grad, wq),
@@ -1177,7 +1176,7 @@
     output = hidden + RESIDUAL * feed_branch.astype(jnp.float32)
     latent_grad = lax.psum_scatter(latent_terms, "tensor", scatter_dimension=0, tiled=True)
     upstream_late, query_raw_grad, key_value_grad = follow(
-        (attention_upstream, query_raw_grad, key_value_grad), latent_terms, grad_down.sent
+        (attention_upstream, query_raw_grad, key_value_grad), latent_terms
     )
     if query_rows % 16 or latent_rows % 16 or out_rows % 32:
         sums = [
@@ -1198,7 +1197,8 @@
         )
     grad_mixed = stacked(ring, mixed_sums)
     grad_mixed.advance()
-    latent_grad = follow(latent_grad, grad_mixed.sent, ends(grad_down))
+    grad_mixed.advance()
+    latent_grad = follow(latent_grad, grad_mixed.sent, ends(grad_pair))
     pair = 2 * down_rows
     height = ring.count * pair
     heights = [height, height]
@@ -1227,12 +1227,10 @@
     token_grad = token_back(
         latent_low, down_projections, tokens_ring, hidden_grad, gain_in
     )
-    hold(grad_mixed, latent_low)
-    grad_mixed.advance()
-    other_sums = follow(other_sums, token_grad, grad_mixed.sent)
+    other_sums = follow(other_sums, token_grad)
     grad_small = stacked(ring, add_low(sent[0], other_sums))
     grad_small.advance()
-    token_grad = reorder(follow(token_grad, grad_small.take(0, 0, 1)), ring.behind)
+    token_grad = reorder(follow(token_grad, grad_small.sent), ring.behind)
     hold(grad_down, ends(grad_small))
     hold(grad_mixed, grad_small.sent)
     grad_mixed.advance()
@@ -1260,7 +1258,7 @@
         [grad_out_own[:, :out_width], grad_out_own[:, out_width:]], axis=0
     )
     grad_gate_own, grad_up_own, pair_sums = unpaired(
-        grad_pair.take(0, 0, feed_rows), grad_pair.low, grad_pair.high, pair_own, feed_width
+        grad_pair.parts[0], grad_pair.low, grad_pair.high, pair_own, feed_width
     )
     row_sums = lambda weights, grads: jnp.sum(weights.astype(jnp.float32) * grads, axis=1)
     head_rows = query_rows + latent_rows

time: 824 us -> 824 us (level)
  other arithmetic: 68.3 us -> 77.6 us
    ppermute x32, waiting for transfers between devices: 151 us -> 176 us  [send_up(): return lax.ppermute(block, self.axis, self.up)]
    ppermute x32, waiting for transfers between devices: 140 us -> 116 us  [send_down(): return lax.ppermute(block, self.axis, self.down)]
    ppermute x32, starting transfers between devices: 49.1 us -> 35.5 us  [send_up(): return lax.ppermute(block, self.axis, self.up)]
    ppermute x32, starting transfers between devices: 21.2 us -> 33.6 us  [send_down(): return lax.ppermute(block, self.axis, self.down)]
  transfers between devices with their start and end apart: 86 -> 86, of which waited for: 43 -> 38; matrix products, arithmetic and copies ran while one was open for 18% -> 18% of each run, Pallas kernels for 25% -> 25%
where the time goes in v2:
time: 824 us; the launch traced here: 815 us
  waiting for transfers between devices  313 us (38%)
  Pallas kernels  237 us (29%)
  other arithmetic  77.6 us (9%)
  starting transfers between devices  74.6 us (9%)
  matrix products  61.6 us (7%)
  local copies, waits for them, and re-layouts  35.8 us (4%)
  between operations  15.8 us (2%)
    ppermute x32, waiting for transfers between devices, send_up(): return lax.ppermute(block, self.axis, self.up)  176 us
    ppermute x32, waiting for transfers between devices, send_down(): return lax.ppermute(block, self.axis, self.down)  116 us
    pallas_call x4, Pallas kernels, feed_terms(): pl.pallas_call(functools.partial(terms_kernel, len(pieces)), grid=(1,), i...  58.7 us
    dot_general x6, matrix products, product_left(): lax.dot_general(left, right, (((0,), (0,)), ((), ())), preferred_element_...  40.5 us
    ppermute x32, starting transfers between devices, send_up(): return lax.ppermute(block, self.axis, self.up)  35.5 us
    ppermute x32, starting transfers between devices, send_down(): return lax.ppermute(block, self.axis, self.down)  33.6 us
    pallas_call x1, Pallas kernels, attention_backward(): pl.pallas_call(backward_kernel, grid=(pairs,), in_specs=[mine(2 * LANES),...  31.3 us
    convert_element_type x16, other arithmetic, add(): return (a.astype(jnp.float32) + b.astype(jnp.float32)).astype(b.dtype)  30.6 us
  transfers between devices with their start and end apart: 86, of which 38 were waited for; matrix products, arithmetic and copies ran while one was open for 18% of the time, Pallas kernels for 25%

profile of v2, /device:TPU:0, one launch (start us, length us, event | category | flops | bytes accessed | tf_op | source)
XLA Modules:
  0.0 815.4 jit_solution(13643011765721469075)
XLA Ops:
  10.7 3.0 collective-permute-start
  23.5 11.2 %collective-permute-done.6.refs_8_ = bf16[288,1280]{1,0:T(8,128)(2,1)S(1)} collective-permute-done((bf16[288,1280]{1,0:T(8,128)(2,1)S(1)}, bf16[288,1280]{1,0:T(8,128)(2,1)S(1)}, u32[]{:S(2)}, u32[]{:S(2)}) %collective-permute-start.6) | collective-permute-done | bytes 737312 | tf_op jit(solution)/shard_map/ppermute | solution.py:773
  36.8 30.3 %collective-permute-done.2.refs_2_.refs_10_ = bf16[160,1152]{1,0:T(8,128)(2,1)S(1)} collective-permute-done((bf16[160,1152]{1,0:T(8,128)(2,1)S(1)}, bf16[160,1152]{1,0:T(8,128)(2,1)S(1)}, u32[]{:S(2)}, u32[]{:S(2)}) %collective-permute-start.2) | collective-permute-done | bytes 368672 | tf_op jit(solution)/shard_map/ppermute | solution.py:776
  68.6 11.3 %collective-permute-done.4.refs_4_.refs_12_ = bf16[160,1152]{1,0:T(8,128)(2,1)} collective-permute-done((bf16[160,1152]{1,0:T(8,128)(2,1)S(1)}, bf16[160,1152]{1,0:T(8,128)(2,1)}, u32[]{:S(2)}, u32[]{:S(2)}) %collective-permute-start.4) | collective-permute-done | bytes 368672 | tf_op jit(solution)/shard_map/ppermute | solution.py:773
  86.1 7.3 collective-permute-done.12.refs_6_.refs_14_
  93.5 16.7 %collective-permute-done.14.refs_8_.refs_16_ = bf16[160,1152]{1,0:T(8,128)(2,1)} collective-permute-done((bf16[160,1152]{1,0:T(8,128)(2,1)}, bf16[160,1152]{1,0:T(8,128)(2,1)}, u32[]{:S(2)}, u32[]{:S(2)}) %collective-permute-start.14) | collective-permute-done | bytes 368672 | tf_op jit(solution)/shard_map/ppermute | solution.py:773
  119.4 12.2 %collective-permute-done.22 = bf16[144,1280]{1,0:T(8,128)(2,1)S(1)} collective-permute-done((bf16[144,1280]{1,0:T(8,128)(2,1)S(1)}, bf16[144,1280]{1,0:T(8,128)(2,1)S(1)}, u32[]{:S(2)}, u32[]{:S(2)}) %collective-permute-start.22) | collective-permute-done | bytes 368672 | tf_op jit(solution)/shard_map/ppermute | solution.py:773
  143.0 3.7 reorder.4.refs_1_.tokens_ref
  156.0 10.0 %project.1 = (bf16[256,1152]{1,0:T(8,128)(2,1)}, f32[256,1152]{1,0:T(8,128)}, bf16[256,2560]{1,0:T(8,128)(2,1)}, bf16[2560,1152]{1,0:T(8,128)(2,1)}) custom-call(s32[4]{0:T(128)} %broadcast_xor_fusion.team_ref.refs_0_, bf16[256,2560]{1,0:T(8,128)(2,1)} %reorder.4.refs_1_.tokens_ref, f32[1,2560]{1,0:T(1,128)} %reshape.321.refs_2_.gain_ref, ...), custom_call_target="tpu_custom_call" | custom-call | flops 1 | bytes 30000000 | tf_op jit(solution)/shard_map/project/pallas_call | solution.py:383
  168.3 3.7 reorder.5
  174.7 17.5 %collective-permute-done.30.refs_5_.refs_2_ = bf16[320,1664]{1,0:T(8,128)(2,1)S(1)} collective-permute-done((bf16[320,1664]{1,0:T(8,128)(2,1)}, bf16[320,1664]{1,0:T(8,128)(2,1)S(1)}, u32[]{:S(2)}, u32[]{:S(2)}) %collective-permute-start.30) | collective-permute-done | bytes 1064992 | tf_op jit(solution)/shard_map/ppermute | solution.py:773
  192.9 3.4 paired.1.refs_0_.refs_1_.weights_ref
  200.3 7.2 assemble.1
  209.4 23.3 %attention_forward.1 = (bf16[1024,640]{1,0:T(8,128)(2,1)}, bf16[1024,1280]{1,0:T(8,128)(2,1)}, bf16[1024,1280]{1,0:T(8,128)(2,1)}, f32[5,2,1024]{2,1,0:T(2,128)}) custom-call(bf16[1024,1152]{1,0:T(8,128)(2,1)} %all-gather.5.cloned.1.call-done.xq_ref.lat_ref.latents_ref, bf16[1024,1152]{1,0:T(8,128)(2,1)} %all-gather.5.cloned.1.call-done.xq_ref.lat_ref.latents_ref, ...), custom_call_target="tpu_custom_call" | custom-call | flops 1 | bytes 69000000 | tf_op jit(solution)/shard_map/attention_forward/pallas_call | solution.py:148
  232.7 7.4 convolution_convert_fusion.4
  248.1 10.9 %collective-permute-done.34 = bf16[160,1664]{1,0:T(8,128)(2,1)S(1)} collective-permute-done((bf16[160,1664]{1,0:T(8,128)(2,1)S(1)}, bf16[160,1664]{1,0:T(8,128)(2,1)S(1)}, u32[]{:S(2)}, u32[]{:S(2)}) %collective-permute-start.34) | collective-permute-done | bytes 532512 | tf_op jit(solution)/shard_map/ppermute | solution.py:773
  261.8 16.2 %feed_product.1.refs_8_ = f32[1024,1664]{1,0:T(8,128)} custom-call(bf16[1024,2560]{1,0:T(8,128)(2,1)} %all-gather.7.cloned.1.call-done.left_ref, bf16[320,1664]{1,0:T(8,128)(2,1)} %copy-done.8, bf16[320,1664]{1,0:T(8,128)(2,1)} %copy-done.19, bf16[320,1664]{1,0:T(8,128)(2,1)} %collective-permute-done.29.refs_2_.refs_3_, bf16[320,1664]{1,0:T(8,128)(2,1)} %copy-done.12, ...), custom_call_target="tpu_custom_call" | custom-call | flops 1 | bytes 45000000 | tf_op jit(solution)/shard_map/feed_product/pallas_call | solution.py:511
  278.1 16.7 %reduce-scatter.5.cloned.1.call-done = bf16[256,2560]{1,0:T(8,128)(2,1)} async-done(((bf16[1024,2560]{1,0:T(8,128)(2,1)}), bf16[256,2560]{1,0:T(8,128)(2,1)}) %reduce-scatter.5.cloned.1.call-update) | async-done | bytes 1310736 | tf_op jit(solution)/shard_map/reduce_scatter | solution.py:1104
  303.7 42.5 %collective-permute-done.39.refs_5_.refs_2_ = bf16[320,3200]{1,0:T(8,128)(2,1)S(1)} collective-permute-done((bf16[320,3200]{1,0:T(8,128)(2,1)}, bf16[320,3200]{1,0:T(8,128)(2,1)S(1)}, u32[]{:S(2)}, u32[]{:S(2)}) %collective-permute-start.39) | collective-permute-done | bytes 2048032 | tf_op jit(solution)/shard_map/ppermute | solution.py:773
  349.0 18.3 %collective-permute-done.40 = bf16[160,3200]{1,0:T(8,128)(2,1)S(1)} collective-permute-done((bf16[160,3200]{1,0:T(8,128)(2,1)S(1)}, bf16[160,3200]{1,0:T(8,128)(2,1)S(1)}, u32[]{:S(2)}, u32[]{:S(2)}) %collective-permute-start.40) | collective-permute-done | bytes 1024032 | tf_op jit(solution)/shard_map/ppermute | solution.py:773
  369.6 26.3 %feed_gate.1 = (bf16[1024,1664]{1,0:T(8,128)(2,1)}, bf16[1024,3200]{1,0:T(8,128)(2,1)}) custom-call(bf16[1024,2560]{1,0:T(8,128)(2,1)} %all-gather.9.cloned.1.call-done.left_ref, bf16[320,3200]{1,0:T(8,128)(2,1)} %paired.1.refs_0_.refs_1_.weights_ref, bf16[320,3200]{1,0:T(8,128)(2,1)} %collective-permute-done.33.refs_1_.refs_2_, ...), custom_call_target="tpu_custom_call" | custom-call | flops 1 | bytes 78000000 | tf_op jit(solution)/shard_map/feed_gate/pallas_call | solution.py:527
  395.9 7.9 convolution_convert_fusion.1
  407.8 9.6 %convolution_convert_fusion = bf16[1280,3200]{1,0:T(8,128)(2,1)S(1)} fusion(bf16[1024,3200]{1,0:T(8,128)(2,1)S(1)} %copy-done.3, bf16[1024,2560]{1,0:T(8,128)(2,1)S(1)} %bitcast.55), kind=kOutput, calls=%fused_computation.2 | convolution fusion | flops 8392704000 | bytes 17367040 | tf_op jit(solution)/shard_map/dot_general | solution.py:50
  429.2 18.1 %feed_terms.4.refs_5_ = bf16[1024,2560]{1,0:T(8,128)(2,1)} custom-call(bf16[1024,3200]{1,0:T(8,128)(2,1)} %get-tuple-element.172.refs_0_, bf16[320,3200]{1,0:T(8,128)(2,1)} %paired.1.refs_0_.refs_1_.weights_ref, bf16[320,3200]{1,0:T(8,128)(2,1)} %collective-permute-done.33.refs_1_.refs_2_, bf16[320,3200]{1,0:T(8,128)(2,1)} %collective-permute-done.37.refs_2_.refs_3_, ...), custom_call_target="tpu_custom_call" | custom-call | flops 1 | bytes 54000000 | tf_op jit(solution)/shard_map/feed_terms/pallas_call | solution.py:569
  454.2 18.1 %feed_terms.5 = bf16[1024,2560]{1,0:T(8,128)(2,1)} custom-call(bf16[1024,3200]{1,0:T(8,128)(2,1)} %get-tuple-element.172.refs_0_, bf16[320,3200]{1,0:T(8,128)(2,1)} %constant_dynamic-update-slice_fusion.2.refs_4_.refs_1_, bf16[320,3200]{1,0:T(8,128)(2,1)} %copy-done.5, ...), custom_call_target="tpu_custom_call", output_to_operand_aliasing={{}: (5, {})} | custom-call | flops 1 | bytes 54000000 | tf_op jit(solution)/shard_map/feed_terms/pallas_call | solution.py:569
  474.7 5.9 convolution_convert_fusion.6
  489.5 5.3 convolution_convert_fusion.5
  494.9 5.3 convolution_convert_fusion.2
  500.2 6.6 convolution_convert_fusion.3.own_ref
  506.8 13.5 %collective-permute-done.49 = bf16[320,3200]{1,0:T(8,128)(2,1)S(1)} collective-permute-done((bf16[320,3200]{1,0:T(8,128)(2,1)}, bf16[320,3200]{1,0:T(8,128)(2,1)S(1)}, u32[]{:S(2)}, u32[]{:S(2)}) %collective-permute-start.49) | collective-permute-done | bytes 2048032 | tf_op jit(solution)/shard_map/ppermute | solution.py:776
  521.0 3.4 add_convert_fusion.4
  528.5 3.4 multiply_convert_fusion
  536.6 11.2 %feed_terms.6.refs_5_ = bf16[1024,2560]{1,0:T(8,128)(2,1)} custom-call(bf16[1024,1664]{1,0:T(8,128)(2,1)} %get-tuple-element.177.refs_0_, bf16[320,1664]{1,0:T(8,128)(2,1)} %copy-done.8, bf16[320,1664]{1,0:T(8,128)(2,1)} %copy-done.19, bf16[320,1664]{1,0:T(8,128)(2,1)} %collective-permute-done.29.refs_2_.refs_3_, bf16[320,1664]{1,0:T(8,128)(2,1)} %copy-done.12), custom_call_target="tpu_custom_call" | custom-call | flops 1 | bytes 33000000 | tf_op jit(solution)/shard_map/feed_terms/pallas_call | solution.py:569
  547.9 11.2 %feed_terms.7 = bf16[1024,2560]{1,0:T(8,128)(2,1)} custom-call(bf16[1024,1664]{1,0:T(8,128)(2,1)} %get-tuple-element.177.refs_0_, bf16[320,1664]{1,0:T(8,128)(2,1)} %copy-done.13, bf16[320,1664]{1,0:T(8,128)(2,1)} %copy-done.11, bf16[320,1664]{1,0:T(8,128)(2,1)} %collective-permute-done.28.refs_6_.refs_3_, ...), custom_call_target="tpu_custom_call", output_to_operand_aliasing={{}: (5, {})} | custom-call | flops 1 | bytes 33000000 | tf_op jit(solution)/shard_map/feed_terms/pallas_call | solution.py:569
  568.9 38.1 %collective-permute-done.53 = bf16[320,3200]{1,0:T(8,128)(2,1)S(1)} collective-permute-done((bf16[320,3200]{1,0:T(8,128)(2,1)}, bf16[320,3200]{1,0:T(8,128)(2,1)S(1)}, u32[]{:S(2)}, u32[]{:S(2)}) %collective-permute-start.53) | collective-permute-done | bytes 2048032 | tf_op jit(solution)/shard_map/ppermute | solution.py:776
  612.2 8.8 %convolution_convert_fusion.8.grad_ref = bf16[1024,640]{1,0:T(8,128)(2,1)} fusion(bf16[1024,2560]{1,0:T(8,128)(2,1)} %all-gather.11.cloned.1.call-done.upstream_ref, bf16[2560,640]{1,0:T(8,128)(2,1)} %get-tuple-element.145), kind=kOutput, calls=%fused_computation.36 | convolution fusion | flops 3356098560 | bytes 9830400 | tf_op jit(solution)/shard_map/dot_general | solution.py:46
  621.0 31.3 %attention_backward.1 = (bf16[1024,1280]{1,0:T(8,128)(2,1)}, bf16[1024,1280]{1,0:T(8,128)(2,1)}, f32[1024,128]{1,0:T(8,128)}) custom-call(bf16[1024,1280]{1,0:T(8,128)(2,1)} %get-tuple-element.178.q_ref, bf16[1024,1280]{1,0:T(8,128)(2,1)} %get-tuple-element.179.kv_ref, bf16[1024,640]{1,0:T(8,128)(2,1)} %convolution_convert_fusion.8.grad_ref, ...), custom_call_target="tpu_custom_call" | custom-call | flops 1 | bytes 93000000 | tf_op jit(solution)/shard_map/attention_backward/pallas_call | solution.py:249
  662.7 20.0 %head_sums.1 = bf16[2304,1280]{1,0:T(8,128)(2,1)} custom-call(s32[8]{0:T(128)} %compare_select_fusion.11.spots_ref.refs_0_, bf16[1024,1152]{1,0:T(8,128)(2,1)} %all-gather.5.cloned.1.call-done.xq_ref.lat_ref.latents_ref, bf16[1024,1280]{1,0:T(8,128)(2,1)} %get-tuple-element.193.query_ref, bf16[1024,1280]{1,0:T(8,128)(2,1)} %get-tuple-element.194.key_value_ref, ...), custom_call_target="tpu_custom_call" | custom-call | flops 1 | bytes 60000000 | tf_op jit(solution)/shard_map/head_sums/pallas_call | solution.py:689
  686.2 15.2 %collective-permute-done.56 = bf16[144,1280]{1,0:T(8,128)(2,1)S(1)} collective-permute-done((bf16[144,1280]{1,0:T(8,128)(2,1)S(1)}, bf16[144,1280]{1,0:T(8,128)(2,1)S(1)}, u32[]{:S(2)}, u32[]{:S(2)}) %collective-permute-start.56) | collective-permute-done | bytes 368672 | tf_op jit(solution)/shard_map/ppermute | solution.py:773
  704.5 7.7 latent_back.1
  715.7 8.0 token_back.1.in_ref
  723.7 3.5 add_convert_fusion
  738.1 5.1 reorder.6
  749.2 12.5 %collective-permute-done.64 = bf16[160,1152]{1,0:T(8,128)(2,1)S(1)} collective-permute-done((bf16[160,1152]{1,0:T(8,128)(2,1)S(1)}, bf16[160,1152]{1,0:T(8,128)(2,1)S(1)}, u32[]{:S(2)}, u32[]{:S(2)}) %collective-permute-start.64) | collective-permute-done | bytes 368672 | tf_op jit(solution)/shard_map/ppermute | solution.py:776
  768.0 5.5 collective-permute-done.65
  777.0 3.2 add_bitcast_fusion
  780.2 3.7 reorder.7
  783.9 6.5 unpaired.1
  (433 shorter events, 212.1 us)
Async XLA Ops:
  7.2 185.6 %all-gather.5.cloned.1.call-start = ((), (), s32[]{:S(2)}) async-start(), calls=%async_computation.4 | async-start | bytes 2949120 | tf_op jit(solution)/shard_map/all_gather | solution.py:1060
  19.6 60.2 %collective-permute-start.10 = (bf16[320,1664]{1,0:T(8,128)(2,1)S(1)}, bf16[320,1664]{1,0:T(8,128)(2,1)S(1)}, u32[]{:S(2)}, u32[]{:S(2)}) collective-permute-start(bf16[320,1664]{1,0:T(8,128)(2,1)S(1)} %pad.18.refs_0_.refs_1_), channel_id=1, source_target_pairs={{0,8},{8,16},{16,24},{24,28},{28,20},{20,12},{12,4},{4,0},{1,9},{9... | collective-permute-start | bytes 3194888 | tf_op jit(solution)/shard_map/ppermute | solution.py:773
  21.5 58.4 %collective-permute-start.11 = (bf16[320,1664]{1,0:T(8,128)(2,1)S(1)}, bf16[320,1664]{1,0:T(8,128)(2,1)S(1)}, u32[]{:S(2)}, u32[]{:S(2)}) collective-permute-start(bf16[320,1664]{1,0:T(8,128)(2,1)S(1)} %pad.18.refs_0_.refs_1_), channel_id=1, source_target_pairs={{8,0},{16,8},{24,16},{28,24},{20,28},{12,20},{4,12},{0,4},{9,1},{1... | collective-permute-start | bytes 3194888 | tf_op jit(solution)/shard_map/ppermute | solution.py:776
  21.7 45.3 %collective-permute-start.2 = (bf16[160,1152]{1,0:T(8,128)(2,1)S(1)}, bf16[160,1152]{1,0:T(8,128)(2,1)S(1)}, u32[]{:S(2)}, u32[]{:S(2)}) collective-permute-start(bf16[160,1152]{1,0:T(8,128)(2,1)S(1)} %pad_maximum_fusion.8.refs_0_.refs_8_), channel_id=1, source_target_pairs={{8,0},{16,8},{24,16},{28,24},{20,28},{12,20},{4,12},{0,4},{9,1},{1... | collective-permute-start | bytes 1105928 | tf_op jit(solution)/shard_map/ppermute | solution.py:776
  34.7 46.1 %collective-permute-start.7 = (bf16[288,1280]{1,0:T(8,128)(2,1)S(1)}, bf16[288,1280]{1,0:T(8,128)(2,1)}, u32[]{:S(2)}, u32[]{:S(2)}) collective-permute-start(bf16[288,1280]{1,0:T(8,128)(2,1)S(1)} %collective-permute-done.6.refs_8_), channel_id=1, source_target_pairs={{0,8},{8,16},{16,24},{24,28},{28,20},{20,12},{12,4},{4,0},{1,9},{9... | collective-permute-start | bytes 2211848 | tf_op jit(solution)/shard_map/ppermute | solution.py:773
  36.3 45.6 %collective-permute-start.9 = (bf16[288,1280]{1,0:T(8,128)(2,1)S(1)}, bf16[288,1280]{1,0:T(8,128)(2,1)}, u32[]{:S(2)}, u32[]{:S(2)}) collective-permute-start(bf16[288,1280]{1,0:T(8,128)(2,1)S(1)} %collective-permute-done.8.refs_2_), channel_id=1, source_target_pairs={{8,0},{16,8},{24,16},{28,24},{20,28},{12,20},{4,12},{0,4},{9,1},{1... | collective-permute-start | bytes 2211848 | tf_op jit(solution)/shard_map/ppermute | solution.py:776
  83.4 26.8 %collective-permute-start.16 = (bf16[288,1280]{1,0:T(8,128)(2,1)}, bf16[288,1280]{1,0:T(8,128)(2,1)S(1)}, u32[]{:S(2)}, u32[]{:S(2)}) collective-permute-start(bf16[288,1280]{1,0:T(8,128)(2,1)} %collective-permute-done.7.refs_7_), channel_id=1, source_target_pairs={{0,8},{8,16},{16,24},{24,28},{28,20},{20,12},{12,4},{4,0},{1,9},{9... | collective-permute-start | bytes 2211848 | tf_op jit(solution)/shard_map/ppermute | solution.py:773
  83.9 27.2 %collective-permute-start.17 = (bf16[288,1280]{1,0:T(8,128)(2,1)}, bf16[288,1280]{1,0:T(8,128)(2,1)}, u32[]{:S(2)}, u32[]{:S(2)}) collective-permute-start(bf16[288,1280]{1,0:T(8,128)(2,1)} %collective-permute-done.9.refs_3_), channel_id=1, source_target_pairs={{8,0},{16,8},{24,16},{28,24},{20,28},{12,20},{4,12},{0,4},{9,1},{1... | collective-permute-start | bytes 2211848 | tf_op jit(solution)/shard_map/ppermute | solution.py:776
  85.5 24.8 %collective-permute-start.5 = (bf16[160,1152]{1,0:T(8,128)(2,1)}, bf16[160,1152]{1,0:T(8,128)(2,1)}, u32[]{:S(2)}, u32[]{:S(2)}) collective-permute-start(bf16[160,1152]{1,0:T(8,128)(2,1)} %collective-permute-done.4.refs_4_.refs_12_), channel_id=1, source_target_pairs={{0,1},{1,0},{2,3},{3,2},{4,5},{5,4},{6,7},{7,6},{8,9},{9,8},{10,11... | collective-permute-start | bytes 1105928 | tf_op jit(solution)/shard_map/ppermute | solution.py:908
  85.6 24.7 %collective-permute-start.14 = (bf16[160,1152]{1,0:T(8,128)(2,1)}, bf16[160,1152]{1,0:T(8,128)(2,1)}, u32[]{:S(2)}, u32[]{:S(2)}) collective-permute-start(bf16[160,1152]{1,0:T(8,128)(2,1)} %collective-permute-done.4.refs_4_.refs_12_), channel_id=1, source_target_pairs={{0,8},{8,16},{16,24},{24,28},{28,20},{20,12},{12,4},{4,0},{1,9},{9... | collective-permute-start | bytes 1105928 | tf_op jit(solution)/shard_map/ppermute | solution.py:773
  93.4 22.4 %collective-permute-start.13 = (bf16[160,1152]{1,0:T(8,128)(2,1)}, bf16[160,1152]{1,0:T(8,128)(2,1)}, u32[]{:S(2)}, u32[]{:S(2)}) collective-permute-start(bf16[160,1152]{1,0:T(8,128)(2,1)} %collective-permute-done.12.refs_6_.refs_14_), channel_id=1, source_target_pairs={{0,1},{1,0},{2,3},{3,2},{4,5},{5,4},{6,7},{7,6},{8,9},{9,8},{10,11... | collective-permute-start | bytes 1105928 | tf_op jit(solution)/shard_map/ppermute | solution.py:908
  111.1 20.4 %collective-permute-start.18 = (bf16[160,1152]{1,0:T(8,128)(2,1)}, bf16[160,1152]{1,0:T(8,128)(2,1)S(1)}, u32[]{:S(2)}, u32[]{:S(2)}) collective-permute-start(bf16[160,1152]{1,0:T(8,128)(2,1)} %collective-permute-done.12.refs_6_.refs_14_), channel_id=1, source_target_pairs={{8,0},{16,8},{24,16},{28,24},{20,28},{12,20},{4,12},{0,4},{9,1},{1... | collective-permute-start | bytes 1105928 | tf_op jit(solution)/shard_map/ppermute | solution.py:776
  140.4 25.5 %collective-permute-start.28 = (bf16[320,1664]{1,0:T(8,128)(2,1)}, bf16[320,1664]{1,0:T(8,128)(2,1)}, u32[]{:S(2)}, u32[]{:S(2)}) collective-permute-start(bf16[320,1664]{1,0:T(8,128)(2,1)} %copy-done.18), channel_id=1, source_target_pairs={{0,8},{8,16},{16,24},{24,28},{28,20},{20,12},{12,4},{4,0},{1,9},{9... | collective-permute-start | bytes 3194888 | tf_op jit(solution)/shard_map/ppermute | solution.py:773
  141.1 24.9 %collective-permute-start.29 = (bf16[320,1664]{1,0:T(8,128)(2,1)}, bf16[320,1664]{1,0:T(8,128)(2,1)}, u32[]{:S(2)}, u32[]{:S(2)}) collective-permute-start(bf16[320,1664]{1,0:T(8,128)(2,1)} %copy-done.19), channel_id=1, source_target_pairs={{8,0},{16,8},{24,16},{28,24},{20,28},{12,20},{4,12},{0,4},{9,1},{1... | collective-permute-start | bytes 3194888 | tf_op jit(solution)/shard_map/ppermute | solution.py:776
  166.0 77.8 %all-gather.7.cloned.1.call-start = ((), (), s32[]{:S(2)}) async-start(), calls=%async_computation.5 | async-start | bytes 6553600 | tf_op jit(solution)/shard_map/all_gather | solution.py:1097
  166.0 26.2 %collective-permute-start.30 = (bf16[320,1664]{1,0:T(8,128)(2,1)}, bf16[320,1664]{1,0:T(8,128)(2,1)S(1)}, u32[]{:S(2)}, u32[]{:S(2)}) collective-permute-start(bf16[320,1664]{1,0:T(8,128)(2,1)} %collective-permute-done.28.refs_6_.refs_3_), channel_id=1, source_target_pairs={{0,8},{8,16},{16,24},{24,28},{28,20},{20,12},{12,4},{4,0},{1,9},{9... | collective-permute-start | bytes 3194888 | tf_op jit(solution)/shard_map/ppermute | solution.py:773
  166.7 26.0 %collective-permute-start.31 = (bf16[320,1664]{1,0:T(8,128)(2,1)}, bf16[320,1664]{1,0:T(8,128)(2,1)S(1)}, u32[]{:S(2)}, u32[]{:S(2)}) collective-permute-start(bf16[320,1664]{1,0:T(8,128)(2,1)} %collective-permute-done.29.refs_2_.refs_3_), channel_id=1, source_target_pairs={{8,0},{16,8},{24,16},{28,24},{20,28},{12,20},{4,12},{0,4},{9,1},{1... | collective-permute-start | bytes 3194888 | tf_op jit(solution)/shard_map/ppermute | solution.py:776
  192.8 102.0 %reduce-scatter.5.cloned.1.call-start = ((), (), s32[]{:S(2)}) async-start(), calls=%async_computation.6 | async-start | bytes 6553600 | tf_op jit(solution)/shard_map/reduce_scatter | solution.py:1104
  196.3 46.3 %collective-permute-start.32 = (bf16[320,3200]{1,0:T(8,128)(2,1)}, bf16[320,3200]{1,0:T(8,128)(2,1)}, u32[]{:S(2)}, u32[]{:S(2)}) collective-permute-start(bf16[320,3200]{1,0:T(8,128)(2,1)} %paired.1.refs_0_.refs_1_.weights_ref), channel_id=1, source_target_pairs={{0,8},{8,16},{16,24},{24,28},{28,20},{20,12},{12,4},{4,0},{1,9},{9... | collective-permute-start | bytes 6144008 | tf_op jit(solution)/shard_map/ppermute | solution.py:773
  197.9 45.9 %collective-permute-start.33 = (bf16[320,3200]{1,0:T(8,128)(2,1)}, bf16[320,3200]{1,0:T(8,128)(2,1)}, u32[]{:S(2)}, u32[]{:S(2)}) collective-permute-start(bf16[320,3200]{1,0:T(8,128)(2,1)} %paired.1.refs_0_.refs_1_.weights_ref), channel_id=1, source_target_pairs={{8,0},{16,8},{24,16},{28,24},{20,28},{12,20},{4,12},{0,4},{9,1},{1... | collective-permute-start | bytes 6144008 | tf_op jit(solution)/shard_map/ppermute | solution.py:776
  243.8 125.8 %all-gather.9.cloned.1.call-start = ((), (), s32[]{:S(2)}) async-start(), calls=%async_computation.7 | async-start | bytes 6553600 | tf_op jit(solution)/shard_map/all_gather | solution.py:1114
  246.1 54.1 %collective-permute-start.36 = (bf16[320,3200]{1,0:T(8,128)(2,1)}, bf16[320,3200]{1,0:T(8,128)(2,1)}, u32[]{:S(2)}, u32[]{:S(2)}) collective-permute-start(bf16[320,3200]{1,0:T(8,128)(2,1)} %collective-permute-done.32.refs_7_.refs_4_), channel_id=1, source_target_pairs={{0,8},{8,16},{16,24},{24,28},{28,20},{20,12},{12,4},{4,0},{1,9},{9... | collective-permute-start | bytes 6144008 | tf_op jit(solution)/shard_map/ppermute | solution.py:773
  247.7 53.9 %collective-permute-start.37 = (bf16[320,3200]{1,0:T(8,128)(2,1)}, bf16[320,3200]{1,0:T(8,128)(2,1)}, u32[]{:S(2)}, u32[]{:S(2)}) collective-permute-start(bf16[320,3200]{1,0:T(8,128)(2,1)} %collective-permute-done.33.refs_1_.refs_2_), channel_id=1, source_target_pairs={{8,0},{16,8},{24,16},{28,24},{20,28},{12,20},{4,12},{0,4},{9,1},{1... | collective-permute-start | bytes 6144008 | tf_op jit(solution)/shard_map/ppermute | solution.py:776
  301.6 224.6 %reduce-scatter.7.cloned.1.call-start = ((), (), s32[]{:S(2)}) async-start(), calls=%async_computation.8 | async-start | bytes 6553600 | tf_op jit(solution)/shard_map/reduce_scatter | solution.py:1136
  301.7 44.6 %collective-permute-start.39 = (bf16[320,3200]{1,0:T(8,128)(2,1)}, bf16[320,3200]{1,0:T(8,128)(2,1)S(1)}, u32[]{:S(2)}, u32[]{:S(2)}) collective-permute-start(bf16[320,3200]{1,0:T(8,128)(2,1)} %collective-permute-done.36.refs_6_.refs_3_), channel_id=1, source_target_pairs={{0,8},{8,16},{16,24},{24,28},{28,20},{20,12},{12,4},{4,0},{1,9},{9... | collective-permute-start | bytes 6144008 | tf_op jit(solution)/shard_map/ppermute | solution.py:773
  303.2 45.0 %collective-permute-start.38 = (bf16[320,3200]{1,0:T(8,128)(2,1)}, bf16[320,3200]{1,0:T(8,128)(2,1)S(1)}, u32[]{:S(2)}, u32[]{:S(2)}) collective-permute-start(bf16[320,3200]{1,0:T(8,128)(2,1)} %collective-permute-done.37.refs_2_.refs_3_), channel_id=1, source_target_pairs={{8,0},{16,8},{24,16},{28,24},{20,28},{12,20},{4,12},{0,4},{9,1},{1... | collective-permute-start | bytes 6144008 | tf_op jit(solution)/shard_map/ppermute | solution.py:776
  346.3 21.0 %collective-permute-start.40 = (bf16[160,3200]{1,0:T(8,128)(2,1)S(1)}, bf16[160,3200]{1,0:T(8,128)(2,1)S(1)}, u32[]{:S(2)}, u32[]{:S(2)}) collective-permute-start(bf16[160,3200]{1,0:T(8,128)(2,1)S(1)} %slice.363), channel_id=1, source_target_pairs={{0,8},{8,16},{16,24},{24,28},{28,20},{20,12},{12,4},{4,0},{1,9},{9... | collective-permute-start | bytes 3072008 | tf_op jit(solution)/shard_map/ppermute | solution.py:773
  421.3 26.0 %collective-permute-start.44 = (bf16[160,3200]{1,0:T(8,128)(2,1)}, bf16[160,3200]{1,0:T(8,128)(2,1)}, u32[]{:S(2)}, u32[]{:S(2)}) collective-permute-start(bf16[160,3200]{1,0:T(8,128)(2,1)} %get-tuple-element.267), channel_id=1, source_target_pairs={{0,8},{8,16},{16,24},{24,28},{28,20},{20,12},{12,4},{4,0},{1,9},{9... | collective-permute-start | bytes 3072008 | tf_op jit(solution)/shard_map/ppermute | solution.py:773
  422.8 25.9 %collective-permute-start.45 = (bf16[160,3200]{1,0:T(8,128)(2,1)}, bf16[160,3200]{1,0:T(8,128)(2,1)}, u32[]{:S(2)}, u32[]{:S(2)}) collective-permute-start(bf16[160,3200]{1,0:T(8,128)(2,1)} %get-tuple-element.266), channel_id=1, source_target_pairs={{8,0},{16,8},{24,16},{28,24},{20,28},{12,20},{4,12},{0,4},{9,1},{1... | collective-permute-start | bytes 3072008 | tf_op jit(solution)/shard_map/ppermute | solution.py:776
  425.9 46.4 %collective-permute-start.47 = (bf16[320,1664]{1,0:T(8,128)(2,1)}, bf16[320,1664]{1,0:T(8,128)(2,1)}, u32[]{:S(2)}, u32[]{:S(2)}) collective-permute-start(bf16[320,1664]{1,0:T(8,128)(2,1)} %pad_maximum_fusion.4), channel_id=1, source_target_pairs={{8,0},{16,8},{24,16},{28,24},{20,28},{12,20},{4,12},{0,4},{9,1},{1... | collective-permute-start | bytes 3194888 | tf_op jit(solution)/shard_map/ppermute | solution.py:776
  428.0 44.4 %collective-permute-start.46 = (bf16[320,1664]{1,0:T(8,128)(2,1)}, bf16[320,1664]{1,0:T(8,128)(2,1)}, u32[]{:S(2)}, u32[]{:S(2)}) collective-permute-start(bf16[320,1664]{1,0:T(8,128)(2,1)} %pad_maximum_fusion.3), channel_id=1, source_target_pairs={{0,8},{8,16},{16,24},{24,28},{28,20},{20,12},{12,4},{4,0},{1,9},{9... | collective-permute-start | bytes 3194888 | tf_op jit(solution)/shard_map/ppermute | solution.py:773
  472.4 139.8 %all-gather.11.cloned.1.call-start = ((), (), s32[]{:S(2)}) async-start(), calls=%async_computation.10 | async-start | bytes 6553600 | tf_op jit(solution)/shard_map/all_gather | solution.py:1150
  472.5 47.8 %collective-permute-start.49 = (bf16[320,3200]{1,0:T(8,128)(2,1)}, bf16[320,3200]{1,0:T(8,128)(2,1)S(1)}, u32[]{:S(2)}, u32[]{:S(2)}) collective-permute-start(bf16[320,3200]{1,0:T(8,128)(2,1)} %pad_maximum_fusion.2), channel_id=1, source_target_pairs={{8,0},{16,8},{24,16},{28,24},{20,28},{12,20},{4,12},{0,4},{9,1},{1... | collective-permute-start | bytes 6144008 | tf_op jit(solution)/shard_map/ppermute | solution.py:776
  473.1 47.9 %collective-permute-start.48 = (bf16[320,3200]{1,0:T(8,128)(2,1)}, bf16[320,3200]{1,0:T(8,128)(2,1)S(1)}, u32[]{:S(2)}, u32[]{:S(2)}) collective-permute-start(bf16[320,3200]{1,0:T(8,128)(2,1)} %pad_maximum_fusion.1), channel_id=1, source_target_pairs={{0,8},{8,16},{16,24},{24,28},{28,20},{20,12},{12,4},{4,0},{1,9},{9... | collective-permute-start | bytes 6144008 | tf_op jit(solution)/shard_map/ppermute | solution.py:773
  484.7 49.8 %collective-permute-start.51 = (bf16[320,1664]{1,0:T(8,128)(2,1)}, bf16[320,1664]{1,0:T(8,128)(2,1)}, u32[]{:S(2)}, u32[]{:S(2)}) collective-permute-start(bf16[320,1664]{1,0:T(8,128)(2,1)} %add_convert_fusion.8), channel_id=1, source_target_pairs={{8,0},{16,8},{24,16},{28,24},{20,28},{12,20},{4,12},{0,4},{9,1},{1... | collective-permute-start | bytes 3194888 | tf_op jit(solution)/shard_map/ppermute | solution.py:776
  487.6 48.6 %collective-permute-start.50 = (bf16[320,1664]{1,0:T(8,128)(2,1)}, bf16[320,1664]{1,0:T(8,128)(2,1)}, u32[]{:S(2)}, u32[]{:S(2)}) collective-permute-start(bf16[320,1664]{1,0:T(8,128)(2,1)} %add_convert_fusion.9), channel_id=1, source_target_pairs={{0,8},{8,16},{16,24},{24,28},{28,20},{20,12},{12,4},{4,0},{1,9},{9... | collective-permute-start | bytes 3194888 | tf_op jit(solution)/shard_map/ppermute | solution.py:773
  536.2 124.2 %reduce-scatter.9.cloned.1.call-start = ((), (), s32[]{:S(2)}) async-start(), calls=%async_computation.9 | async-start | bytes 6553600 | tf_op jit(solution)/shard_map/reduce_scatter | solution.py:1159
  559.1 145.4 %reduce-scatter.11.cloned.1.call-start = ((), (), s32[]{:S(2)}) async-start(), calls=%async_computation.11 | async-start | bytes 2949120 | tf_op jit(solution)/shard_map/reduce_scatter | solution.py:1177
  559.2 47.8 %collective-permute-start.53 = (bf16[320,3200]{1,0:T(8,128)(2,1)}, bf16[320,3200]{1,0:T(8,128)(2,1)S(1)}, u32[]{:S(2)}, u32[]{:S(2)}) collective-permute-start(bf16[320,3200]{1,0:T(8,128)(2,1)} %add_convert_fusion.3), channel_id=1, source_target_pairs={{8,0},{16,8},{24,16},{28,24},{20,28},{12,20},{4,12},{0,4},{9,1},{1... | collective-permute-start | bytes 6144008 | tf_op jit(solution)/shard_map/ppermute | solution.py:776
  561.0 47.7 %collective-permute-start.52 = (bf16[320,3200]{1,0:T(8,128)(2,1)}, bf16[320,3200]{1,0:T(8,128)(2,1)S(1)}, u32[]{:S(2)}, u32[]{:S(2)}) collective-permute-start(bf16[320,3200]{1,0:T(8,128)(2,1)} %add_convert_fusion.4), channel_id=1, source_target_pairs={{0,8},{8,16},{16,24},{24,28},{28,20},{20,12},{12,4},{4,0},{1,9},{9... | collective-permute-start | bytes 6144008 | tf_op jit(solution)/shard_map/ppermute | solution.py:773
  564.2 88.1 %collective-permute-start.55 = (bf16[320,1664]{1,0:T(8,128)(2,1)}, bf16[320,1664]{1,0:T(8,128)(2,1)}, u32[]{:S(2)}, u32[]{:S(2)}) collective-permute-start(bf16[320,1664]{1,0:T(8,128)(2,1)} %add_convert_fusion.6), channel_id=1, source_target_pairs={{8,0},{16,8},{24,16},{28,24},{20,28},{12,20},{4,12},{0,4},{9,1},{1... | collective-permute-start | bytes 3194888 | tf_op jit(solution)/shard_map/ppermute | solution.py:776
  568.4 83.9 %collective-permute-start.54 = (bf16[320,1664]{1,0:T(8,128)(2,1)}, bf16[320,1664]{1,0:T(8,128)(2,1)}, u32[]{:S(2)}, u32[]{:S(2)}) collective-permute-start(bf16[320,1664]{1,0:T(8,128)(2,1)} %add_convert_fusion.7), channel_id=1, source_target_pairs={{0,8},{8,16},{16,24},{24,28},{28,20},{20,12},{12,4},{4,0},{1,9},{9... | collective-permute-start | bytes 3194888 | tf_op jit(solution)/shard_map/ppermute | solution.py:773
  660.4 44.1 %collective-permute-start.59 = (bf16[320,3200]{1,0:T(8,128)(2,1)}, bf16[320,3200]{1,0:T(8,128)(2,1)}, u32[]{:S(2)}, u32[]{:S(2)}) collective-permute-start(bf16[320,3200]{1,0:T(8,128)(2,1)} %add_convert_fusion.1), channel_id=1, source_target_pairs={{8,0},{16,8},{24,16},{28,24},{20,28},{12,20},{4,12},{0,4},{9,1},{1... | collective-permute-start | bytes 6144008 | tf_op jit(solution)/shard_map/ppermute | solution.py:776
  661.8 42.7 %collective-permute-start.58 = (bf16[320,3200]{1,0:T(8,128)(2,1)}, bf16[320,3200]{1,0:T(8,128)(2,1)}, u32[]{:S(2)}, u32[]{:S(2)}) collective-permute-start(bf16[320,3200]{1,0:T(8,128)(2,1)} %add_convert_fusion.2), channel_id=1, source_target_pairs={{0,8},{8,16},{16,24},{24,28},{28,20},{20,12},{12,4},{4,0},{1,9},{9... | collective-permute-start | bytes 6144008 | tf_op jit(solution)/shard_map/ppermute | solution.py:773
  736.0 28.0 %collective-permute-start.71 = (bf16[288,1280]{1,0:T(8,128)(2,1)S(1)}, bf16[288,1280]{1,0:T(8,128)(2,1)S(1)}, u32[]{:S(2)}, u32[]{:S(2)}) collective-permute-start(bf16[288,1280]{1,0:T(8,128)(2,1)S(1)} %get-tuple-element.273), channel_id=1, source_target_pairs={{0,8},{8,16},{16,24},{24,28},{28,20},{20,12},{12,4},{4,0},{1,9},{9... | collective-permute-start | bytes 2211848 | tf_op jit(solution)/shard_map/ppermute | solution.py:773
  737.1 26.9 %collective-permute-start.72 = (bf16[288,1280]{1,0:T(8,128)(2,1)S(1)}, bf16[288,1280]{1,0:T(8,128)(2,1)}, u32[]{:S(2)}, u32[]{:S(2)}) collective-permute-start(bf16[288,1280]{1,0:T(8,128)(2,1)S(1)} %get-tuple-element.272), channel_id=1, source_target_pairs={{8,0},{16,8},{24,16},{28,24},{20,28},{12,20},{4,12},{0,4},{9,1},{1... | collective-permute-start | bytes 2211848 | tf_op jit(solution)/shard_map/ppermute | solution.py:776
  766.0 29.2 %collective-permute-start.73 = (bf16[288,1280]{1,0:T(8,128)(2,1)S(1)}, bf16[288,1280]{1,0:T(8,128)(2,1)S(1)}, u32[]{:S(2)}, u32[]{:S(2)}) collective-permute-start(bf16[288,1280]{1,0:T(8,128)(2,1)S(1)} %get-tuple-element.271), channel_id=1, source_target_pairs={{0,8},{8,16},{16,24},{24,28},{28,20},{20,12},{12,4},{4,0},{1,9},{9... | collective-permute-start | bytes 2211848 | tf_op jit(solution)/shard_map/ppermute | solution.py:773
  766.9 28.2 %collective-permute-start.74 = (bf16[288,1280]{1,0:T(8,128)(2,1)S(1)}, bf16[288,1280]{1,0:T(8,128)(2,1)S(1)}, u32[]{:S(2)}, u32[]{:S(2)}) collective-permute-start(bf16[288,1280]{1,0:T(8,128)(2,1)S(1)} %get-tuple-element.270), channel_id=1, source_target_pairs={{8,0},{16,8},{24,16},{28,24},{20,28},{12,20},{4,12},{0,4},{9,1},{1... | collective-permute-start | bytes 2211848 | tf_op jit(solution)/shard_map/ppermute | solution.py:776
  (108 other events, 1967.9 us)
Sparse Core Ops, SparseCore 0:
  166.1 23.5 all-gather.4
  192.9 40.6 all-gather.6
  243.9 50.7 reduce-scatter.4
  301.7 39.1 all-gather.8
  472.5 49.9 reduce-scatter.6
  536.3 39.5 all-gather.10
  578.4 51.3 reduce-scatter.8
  660.5 31.0 reduce-scatter.10

commit v3 on v2

--- a/solution.py
+++ b/solution.py
@@ -1007,7 +1007,6 @@
 
     collect(small_up.low, 0, 0)
     mixed_up.advance()
-    down_up.advance()
     while not small_up.done:
         swapped = pieces[1::2]
         small_up.advance()
@@ -1015,7 +1014,7 @@
         if not small_up.done:
             collect(small_up.high, small_up.step, 0)
             collect(small_up.low, ring.count - small_up.step, 0)
-            hold(small_up, ends(mixed_up, down_up), swapped)
+            hold(small_up, ends(mixed_up), swapped)
             hold(mixed_up, ends(small_up))
     collect(small_up.low, ring.half, 0)
     collect(small_up.high, ring.half, 1)
@@ -1102,16 +1101,19 @@
     branch_terms = product_right(heads, attention_out_t).astype(low)
     branch_terms = follow(branch_terms, feed_upstream, ends(pair_up))
     attention_branch = lax.psum_scatter(branch_terms, "tensor", scatter_dimension=0, tiled=True)
+    attention_branch = follow(attention_branch, ends(down_up))
     downs = down_up.finish()
     if ring.count > 8:
         downs = [jnp.concatenate(downs, axis=0)]
     activated_grad = feed_product(feed_upstream, downs)
-    attention_branch = follow(attention_branch, activated_grad)
     hidden = tokens_ring.astype(jnp.float32) + RESIDUAL * attention_branch.astype(jnp.float32)
     feed_normed, inverse_hidden = normalize(hidden, gain_hidden)
     pair_up.advance()
     feed_normed = follow(feed_normed.astype(low), ends(pair_up))
     feed_seq = lax.all_gather(feed_normed, "tensor", axis=0, tiled=True)
+    hold(pair_up, ends(down_up))
+    pair_up.advance()
+    hold(pair_up, activated_grad)
     weights = pair_up.finish()
     if ring.count > 8:
         weights = [jnp.concatenate(weights, axis=0)]
@@ -1134,6 +1136,8 @@
         terms = feed_terms(pair_grad, weights[half:], width, 1, terms)
     terms = follow(terms, ends(grad_down))
     feed_back = lax.psum_scatter(terms, "tensor", scatter_dimension=0, tiled=True)
+    activated = follow(activated, terms)
+    feed_branch = feed_terms(activated, downs[:half], width, 0, None, lasting(11))
     delay(grad_down, terms)
     hold(grad_down, terms)
     grad_down.advance()
@@ -1141,29 +1145,23 @@
     delay(grad_pair, grad_down.sent)
     grad_pair.advance()
     grad_pair.take(0, 0, 1), grad_down.take(0, 0, 1)
-    feed_back = follow(feed_back, grad_pair.parts[0], grad_down.parts[0])
+    feed_back = follow(feed_back, grad_pair.parts[0], grad_down.parts[0], feed_branch)
     hidden_back = normalize_back(
         hidden, inverse_hidden, gain_hidden, feed_back.astype(jnp.float32)
     )
     hidden_grad = upstream.astype(jnp.float32) + hidden_back
     upstream_send = follow((RESIDUAL * hidden_grad).astype(low), grad_pair.sent, ends(grad_down))
     attention_upstream = lax.all_gather(upstream_send, "tensor", axis=0, tiled=True)
-    grad_down.advance()
-    activated = follow(activated, upstream_send)
-    feed_branch = feed_terms(activated, downs[:half], width, 0, None, lasting(11))
-    if len(downs) > half:
-        feed_branch = feed_terms(activated, downs[half:], width, 1, feed_branch, lasting(11))
-    attention_upstream = follow(
-        attention_upstream, feed_branch, ends(grad_pair), grad_down.sent
-    )
-    feed_branch = lax.psum_scatter(feed_branch, "tensor", scatter_dimension=0, tiled=True)
+    attention_upstream = follow(attention_upstream, ends(grad_pair))
     heads_grad = product(attention_upstream, attention_out_t).astype(low)
     grad_pair.advance()
     heads_grad = follow(heads_grad, grad_pair.sent)
     query_raw_grad, key_value_grad, key_rope_grad = attention_backward(
         query_heads, key_value, heads_grad, log_totals, rope, tables
     )
-    query_raw_grad, key_value_grad = follow((query_raw_grad, key_value_grad), ends(grad_down))
+    query_raw_grad, key_value_grad = follow((query_raw_grad, key_value_grad), ends(grad_pair))
+    hold(grad_down, query_raw_grad)
+    grad_down.advance()
     latent_terms = jnp.concatenate(
         [
             product_right(query_raw_grad, wq),
@@ -1172,11 +1170,9 @@
         ],
         axis=1,
     ).astype(low)
-    latent_terms = follow(latent_terms, feed_branch)
-    output = hidden + RESIDUAL * feed_branch.astype(jnp.float32)
     latent_grad = lax.psum_scatter(latent_terms, "tensor", scatter_dimension=0, tiled=True)
     upstream_late, query_raw_grad, key_value_grad = follow(
-        (attention_upstream, query_raw_grad, key_value_grad), latent_terms
+        (attention_upstream, query_raw_grad, key_value_grad), latent_terms, grad_down.sent
     )
     if query_rows % 16 or latent_rows % 16 or out_rows % 32:
         sums = [
@@ -1195,10 +1191,13 @@
             ahead, latents, query_raw_grad, key_value_grad, upstream_late, heads,
             rank, query_rows, latent_rows, out_rows,
         )
-    grad_mixed = stacked(ring, mixed_sums)
+    grad_mixed = stacked(ring, follow(mixed_sums, ends(grad_down)))
     grad_mixed.advance()
-    grad_mixed.advance()
-    latent_grad = follow(latent_grad, grad_mixed.sent, ends(grad_pair))
+    if len(downs) > half:
+        activated = follow(activated, grad_mixed.sent)
+        feed_branch = feed_terms(activated, downs[half:], width, 1, feed_branch, lasting(11))
+    latent_grad = follow(latent_grad, ends(grad_mixed), feed_branch)
+    feed_branch = lax.psum_scatter(feed_branch, "tensor", scatter_dimension=0, tiled=True)
     pair = 2 * down_rows
     height = ring.count * pair
     heights = [height, height]
@@ -1224,25 +1223,30 @@
         return (a.astype(jnp.float32) + b.astype(jnp.float32)).astype(low)
 
     other_sums = swap(sent[1], 1)
+    hold(grad_mixed, latent_low)
+    grad_mixed.advance()
     token_grad = token_back(
         latent_low, down_projections, tokens_ring, hidden_grad, gain_in
     )
     other_sums = follow(other_sums, token_grad)
     grad_small = stacked(ring, add_low(sent[0], other_sums))
     grad_small.advance()
-    token_grad = reorder(follow(token_grad, grad_small.sent), ring.behind)
-    hold(grad_down, ends(grad_small))
     hold(grad_mixed, grad_small.sent)
     grad_mixed.advance()
+    grad_small.advance()
+    token_grad = reorder(follow(token_grad, grad_small.sent), ring.behind)
+    hold(grad_mixed, grad_small.sent)
+    hold(grad_down, ends(grad_small))
     hold(grad_small, token_grad)
     grad_small.advance()
-    hold(grad_mixed, grad_small.sent)
-    hold(grad_pair, ends(grad_small))
+    hold(grad_pair, grad_small.sent)
+    grad_mixed.advance()
     grad_small.advance()
-    output = reorder(follow(output.astype(low), grad_small.sent), ring.behind)
-    grad_mixed.advance()
+    feed_branch = follow(feed_branch, grad_small.sent)
+    output = hidden + RESIDUAL * feed_branch.astype(jnp.float32)
+    output = reorder(output.astype(low), ring.behind)
     small_own = grad_small.finish()
-    small_other = follow(small_own[down_rows:].astype(low), ends(grad_mixed))
+    small_other = follow(small_own[down_rows:].astype(low), ends(grad_mixed), output)
     packed_own = small_own[:down_rows] + swap(small_other, 2).astype(jnp.float32)
     rope_from = rank + KVR + NOPE
     lanes = jnp.arange(down_width) < rope_from + ROPE
@@ -1266,6 +1270,7 @@
         [pair_sums[:, 0], row_sums(mixed[:head_rows], grad_mixed_own[:head_rows])]
     )
     gain_sums = jnp.pad(gain_sums, (0, -gain_sums.shape[0] % LANES))[None]
+    gain_sums = follow(gain_sums, small_other)
     gain_sums = gain_sums + swap(gain_sums, 1)
     gain_sums = (gain_sums + swap(gain_sums, 2))[0]
     gain_grads = []

time: 824 us -> 812 us (0.985)
  waiting for transfers between devices: 313 us -> 287 us
    ppermute x32, waiting for transfers between devices: 176 us -> 154 us  [send_up(): return lax.ppermute(block, self.axis, self.up)]
    ppermute x32, starting transfers between devices: 35.5 us -> 45.8 us  [send_up(): return lax.ppermute(block, self.axis, self.up)]
    ppermute x32, starting transfers between devices: 33.6 us -> 23.4 us  [send_down(): return lax.ppermute(block, self.axis, self.down)]
  transfers between devices with their start and end apart: 86 -> 86, of which waited for: 38 -> 36; matrix products, arithmetic and copies ran while one was open for 18% -> 19% of each run, Pallas kernels for 25% -> 25%
where the time goes in v3:
time: 812 us; the launch traced here: 803 us
  waiting for transfers between devices  287 us (35%)
  Pallas kernels  238 us (29%)
  other arithmetic  82.7 us (10%)
  starting transfers between devices  74.2 us (9%)
  matrix products  67.6 us (8%)
  local copies, waits for them, and re-layouts  37.5 us (5%)
  between operations  16 us (2%)
    ppermute x32, waiting for transfers between devices, send_up(): return lax.ppermute(block, self.axis, self.up)  154 us
    ppermute x32, waiting for transfers between devices, send_down(): return lax.ppermute(block, self.axis, self.down)  108 us
    pallas_call x4, Pallas kernels, feed_terms(): pl.pallas_call(functools.partial(terms_kernel, len(pieces)), grid=(1,), i...  58.8 us
    dot_general x6, matrix products, product_left(): lax.dot_general(left, right, (((0,), (0,)), ((), ())), preferred_element_...  45.8 us
    ppermute x32, starting transfers between devices, send_up(): return lax.ppermute(block, self.axis, self.up)  45.8 us
    convert_element_type x16, other arithmetic, add(): return (a.astype(jnp.float32) + b.astype(jnp.float32)).astype(b.dtype)  35 us
    pallas_call x1, Pallas kernels, attention_backward(): pl.pallas_call(backward_kernel, grid=(pairs,), in_specs=[mine(2 * LANES),...  31.6 us
    pallas_call x1, Pallas kernels, feed_gate(): pl.pallas_call(functools.partial(gate_kernel, len(pieces), pair_width //...  26.3 us
  transfers between devices with their start and end apart: 86, of which 36 were waited for; matrix products, arithmetic and copies ran while one was open for 19% of the time, Pallas kernels for 25%

profile of v3, /device:TPU:0, one launch (start us, length us, event | category | flops | bytes accessed | tf_op | source)
XLA Modules:
  0.0 802.9 jit_solution(15036895993405007152)
XLA Ops:
  15.4 14.2 %collective-permute-done.6.refs_8_ = bf16[288,1280]{1,0:T(8,128)(2,1)} collective-permute-done((bf16[288,1280]{1,0:T(8,128)(2,1)S(1)}, bf16[288,1280]{1,0:T(8,128)(2,1)}, u32[]{:S(2)}, u32[]{:S(2)}) %collective-permute-start.6) | collective-permute-done | bytes 737312 | tf_op jit(solution)/shard_map/ppermute | solution.py:773
  33.8 22.8 %collective-permute-done.2.refs_2_.refs_10_ = bf16[160,1152]{1,0:T(8,128)(2,1)S(1)} collective-permute-done((bf16[160,1152]{1,0:T(8,128)(2,1)S(1)}, bf16[160,1152]{1,0:T(8,128)(2,1)S(1)}, u32[]{:S(2)}, u32[]{:S(2)}) %collective-permute-start.2) | collective-permute-done | bytes 368672 | tf_op jit(solution)/shard_map/ppermute | solution.py:776
  61.6 7.3 collective-permute-done.10.refs_6_.refs_14_
  69.0 15.7 %collective-permute-done.12.refs_8_.refs_16_ = bf16[160,1152]{1,0:T(8,128)(2,1)} collective-permute-done((bf16[160,1152]{1,0:T(8,128)(2,1)S(1)}, bf16[160,1152]{1,0:T(8,128)(2,1)}, u32[]{:S(2)}, u32[]{:S(2)}) %collective-permute-start.12) | collective-permute-done | bytes 368672 | tf_op jit(solution)/shard_map/ppermute | solution.py:773
  92.8 13.0 %collective-permute-done.20 = bf16[144,1280]{1,0:T(8,128)(2,1)S(1)} collective-permute-done((bf16[144,1280]{1,0:T(8,128)(2,1)S(1)}, bf16[144,1280]{1,0:T(8,128)(2,1)S(1)}, u32[]{:S(2)}, u32[]{:S(2)}) %collective-permute-start.20) | collective-permute-done | bytes 368672 | tf_op jit(solution)/shard_map/ppermute | solution.py:773
  117.4 3.7 reorder.4.refs_1_.tokens_ref
  129.6 10.0 %project.1 = (bf16[256,1152]{1,0:T(8,128)(2,1)}, f32[256,1152]{1,0:T(8,128)}, bf16[256,2560]{1,0:T(8,128)(2,1)}, bf16[2560,1152]{1,0:T(8,128)(2,1)}) custom-call(s32[4]{0:T(128)} %broadcast_xor_fusion.team_ref.refs_0_, bf16[256,2560]{1,0:T(8,128)(2,1)} %reorder.4.refs_1_.tokens_ref, f32[1,2560]{1,0:T(1,128)} %reshape.321.refs_2_.gain_ref, ...), custom_call_target="tpu_custom_call" | custom-call | flops 1 | bytes 30000000 | tf_op jit(solution)/shard_map/project/pallas_call | solution.py:383
  142.7 3.7 reorder.5
  149.1 16.8 %collective-permute-done.28.refs_6_.refs_3_ = bf16[320,1664]{1,0:T(8,128)(2,1)S(1)} collective-permute-done((bf16[320,1664]{1,0:T(8,128)(2,1)}, bf16[320,1664]{1,0:T(8,128)(2,1)S(1)}, u32[]{:S(2)}, u32[]{:S(2)}) %collective-permute-start.28) | collective-permute-done | bytes 1064992 | tf_op jit(solution)/shard_map/ppermute | solution.py:773
  167.5 3.5 paired.1.refs_0_.refs_1_.weights_ref
  174.9 7.2 assemble.1
  184.0 23.3 %attention_forward.1 = (bf16[1024,640]{1,0:T(8,128)(2,1)}, bf16[1024,1280]{1,0:T(8,128)(2,1)}, bf16[1024,1280]{1,0:T(8,128)(2,1)}, f32[5,2,1024]{2,1,0:T(2,128)}) custom-call(bf16[1024,1152]{1,0:T(8,128)(2,1)} %all-gather.5.cloned.1.call-done.xq_ref.lat_ref.latents_ref, bf16[1024,1152]{1,0:T(8,128)(2,1)} %all-gather.5.cloned.1.call-done.xq_ref.lat_ref.latents_ref, ...), custom_call_target="tpu_custom_call" | custom-call | flops 1 | bytes 69000000 | tf_op jit(solution)/shard_map/attention_forward/pallas_call | solution.py:148
  207.4 7.4 convolution_convert_fusion.4
  221.9 22.5 %collective-permute-done.32.refs_5_.refs_2_ = bf16[320,1664]{1,0:T(8,128)(2,1)S(1)} collective-permute-done((bf16[320,1664]{1,0:T(8,128)(2,1)}, bf16[320,1664]{1,0:T(8,128)(2,1)S(1)}, u32[]{:S(2)}, u32[]{:S(2)}) %collective-permute-start.32) | collective-permute-done | bytes 1064992 | tf_op jit(solution)/shard_map/ppermute | solution.py:773
  246.1 22.5 %reduce-scatter.5.cloned.1.call-done = bf16[256,2560]{1,0:T(8,128)(2,1)} async-done(((bf16[1024,2560]{1,0:T(8,128)(2,1)}), bf16[256,2560]{1,0:T(8,128)(2,1)}) %reduce-scatter.5.cloned.1.call-update) | async-done | bytes 1310736 | tf_op jit(solution)/shard_map/reduce_scatter | solution.py:1103
  272.2 12.6 %collective-permute-done.34.refs_6_.refs_3_ = bf16[320,3200]{1,0:T(8,128)(2,1)} collective-permute-done((bf16[320,3200]{1,0:T(8,128)(2,1)}, bf16[320,3200]{1,0:T(8,128)(2,1)}, u32[]{:S(2)}, u32[]{:S(2)}) %collective-permute-start.34) | collective-permute-done | bytes 2048032 | tf_op jit(solution)/shard_map/ppermute | solution.py:773
  290.4 7.0 collective-permute-done.36
  297.4 4.3 collective-permute-done.37
  305.4 15.3 %feed_product.1.refs_8_ = f32[1024,1664]{1,0:T(8,128)} custom-call(bf16[1024,2560]{1,0:T(8,128)(2,1)} %all-gather.7.cloned.1.call-done.left_ref, bf16[320,1664]{1,0:T(8,128)(2,1)} %copy-done.10, bf16[320,1664]{1,0:T(8,128)(2,1)} %collective-permute-done.27.refs_1_.refs_2_, bf16[320,1664]{1,0:T(8,128)(2,1)} %copy-done.21, ...), custom_call_target="tpu_custom_call" | custom-call | flops 1 | bytes 45000000 | tf_op jit(solution)/shard_map/feed_product/pallas_call | solution.py:511
  320.7 23.8 %collective-permute-done.38.refs_3_.refs_4_ = bf16[320,3200]{1,0:T(8,128)(2,1)S(1)} collective-permute-done((bf16[320,3200]{1,0:T(8,128)(2,1)}, bf16[320,3200]{1,0:T(8,128)(2,1)S(1)}, u32[]{:S(2)}, u32[]{:S(2)}) %collective-permute-start.38) | collective-permute-done | bytes 2048032 | tf_op jit(solution)/shard_map/ppermute | solution.py:776
  347.8 16.2 %collective-permute-done.40 = bf16[160,3200]{1,0:T(8,128)(2,1)S(1)} collective-permute-done((bf16[160,3200]{1,0:T(8,128)(2,1)S(1)}, bf16[160,3200]{1,0:T(8,128)(2,1)S(1)}, u32[]{:S(2)}, u32[]{:S(2)}) %collective-permute-start.40) | collective-permute-done | bytes 1024032 | tf_op jit(solution)/shard_map/ppermute | solution.py:773
  367.0 26.3 %feed_gate.1 = (bf16[1024,1664]{1,0:T(8,128)(2,1)}, bf16[1024,3200]{1,0:T(8,128)(2,1)}) custom-call(bf16[1024,2560]{1,0:T(8,128)(2,1)} %all-gather.9.cloned.1.call-done.left_ref, bf16[320,3200]{1,0:T(8,128)(2,1)} %paired.1.refs_0_.refs_1_.weights_ref, bf16[320,3200]{1,0:T(8,128)(2,1)} %collective-permute-done.31.refs_1_.refs_2_, ...), custom_call_target="tpu_custom_call" | custom-call | flops 1 | bytes 78000000 | tf_op jit(solution)/shard_map/feed_gate/pallas_call | solution.py:527
  393.3 7.9 convolution_convert_fusion.1
  405.2 9.6 %convolution_convert_fusion = bf16[1280,3200]{1,0:T(8,128)(2,1)S(1)} fusion(bf16[1024,3200]{1,0:T(8,128)(2,1)S(1)} %copy-done.3, bf16[1024,2560]{1,0:T(8,128)(2,1)S(1)} %bitcast.55), kind=kOutput, calls=%fused_computation.2 | convolution fusion | flops 8392704000 | bytes 17367040 | tf_op jit(solution)/shard_map/dot_general | solution.py:50
  426.5 18.1 %feed_terms.4.refs_5_ = bf16[1024,2560]{1,0:T(8,128)(2,1)} custom-call(bf16[1024,3200]{1,0:T(8,128)(2,1)} %get-tuple-element.185.refs_0_, bf16[320,3200]{1,0:T(8,128)(2,1)} %paired.1.refs_0_.refs_1_.weights_ref, bf16[320,3200]{1,0:T(8,128)(2,1)} %collective-permute-done.31.refs_1_.refs_2_, bf16[320,3200]{1,0:T(8,128)(2,1)} %collective-permute-done.35.refs_2_.refs_3_, ...), custom_call_target="tpu_custom_call" | custom-call | flops 1 | bytes 54000000 | tf_op jit(solution)/shard_map/feed_terms/pallas_call | solution.py:569
  451.8 18.1 %feed_terms.5 = bf16[1024,2560]{1,0:T(8,128)(2,1)} custom-call(bf16[1024,3200]{1,0:T(8,128)(2,1)} %get-tuple-element.185.refs_0_, bf16[320,3200]{1,0:T(8,128)(2,1)} %constant_dynamic-update-slice_fusion.2.refs_4_.refs_1_, bf16[320,3200]{1,0:T(8,128)(2,1)} %copy-done.5, ...), custom_call_target="tpu_custom_call", output_to_operand_aliasing={{}: (5, {})} | custom-call | flops 1 | bytes 54000000 | tf_op jit(solution)/shard_map/feed_terms/pallas_call | solution.py:569
  472.2 5.5 convolution_convert_fusion.6
  477.8 3.3 add_convert_fusion.8
  485.9 5.4 convolution_convert_fusion.5
  491.3 11.4 %feed_terms.6.refs_5_ = bf16[1024,2560]{1,0:T(8,128)(2,1)} custom-call(bf16[1024,1664]{1,0:T(8,128)(2,1)} %get-tuple-element.210.refs_0_, bf16[320,1664]{1,0:T(8,128)(2,1)} %copy-done.10, bf16[320,1664]{1,0:T(8,128)(2,1)} %collective-permute-done.27.refs_1_.refs_2_, bf16[320,1664]{1,0:T(8,128)(2,1)} %copy-done.21, ...), custom_call_target="tpu_custom_call" | custom-call | flops 1 | bytes 33000000 | tf_op jit(solution)/shard_map/feed_terms/pallas_call | solution.py:569
  502.7 8.2 %convolution_convert_fusion.2 = bf16[640,3200]{1,0:T(8,128)(2,1)S(1)} fusion(bf16[1024,3200]{1,0:T(8,128)(2,1)} %get-tuple-element.185.refs_0_, bf16[1024,2560]{1,0:T(8,128)(2,1)} %all-gather.9.cloned.1.call-done.left_ref), kind=kOutput, calls=%fused_computation.4 | convolution fusion | flops 4196352000 | bytes 11960320 | tf_op jit(solution)/shard_map/dot_general | solution.py:50
  510.9 9.3 %convolution_convert_fusion.3.own_ref = bf16[640,3200]{1,0:T(8,128)(2,1)} fusion(bf16[1024,3200]{1,0:T(8,128)(2,1)S(1)} %bitcast.53, bf16[1024,2560]{1,0:T(8,128)(2,1)} %all-gather.9.cloned.1.call-done.left_ref), kind=kOutput, calls=%fused_computation.5 | convolution fusion | flops 4196352000 | bytes 11960320 | tf_op jit(solution)/shard_map/dot_general | solution.py:50
  520.3 4.0 add_convert_fusion.4
  528.3 3.3 multiply_convert_fusion
  535.3 38.6 %collective-permute-done.53 = bf16[320,3200]{1,0:T(8,128)(2,1)S(1)} collective-permute-done((bf16[320,3200]{1,0:T(8,128)(2,1)}, bf16[320,3200]{1,0:T(8,128)(2,1)S(1)}, u32[]{:S(2)}, u32[]{:S(2)}) %collective-permute-start.53) | collective-permute-done | bytes 2048032 | tf_op jit(solution)/shard_map/ppermute | solution.py:776
  574.3 3.4 add_convert_fusion.1
  581.5 8.8 %convolution_convert_fusion.8.grad_ref = bf16[1024,640]{1,0:T(8,128)(2,1)} fusion(bf16[1024,2560]{1,0:T(8,128)(2,1)} %all-gather.11.cloned.1.call-done.upstream_ref, bf16[2560,640]{1,0:T(8,128)(2,1)} %get-tuple-element.154), kind=kOutput, calls=%fused_computation.36 | convolution fusion | flops 3356098560 | bytes 9830400 | tf_op jit(solution)/shard_map/dot_general | solution.py:46
  590.3 31.6 %attention_backward.1 = (bf16[1024,1280]{1,0:T(8,128)(2,1)}, bf16[1024,1280]{1,0:T(8,128)(2,1)}, f32[1024,128]{1,0:T(8,128)}) custom-call(bf16[1024,1280]{1,0:T(8,128)(2,1)} %get-tuple-element.191.q_ref, bf16[1024,1280]{1,0:T(8,128)(2,1)} %get-tuple-element.192.kv_ref, bf16[1024,640]{1,0:T(8,128)(2,1)} %convolution_convert_fusion.8.grad_ref, ...), custom_call_target="tpu_custom_call" | custom-call | flops 1 | bytes 93000000 | tf_op jit(solution)/shard_map/attention_backward/pallas_call | solution.py:249
  621.9 4.7 convolution_convert_fusion.7
  635.1 19.9 %head_sums.1 = bf16[2304,1280]{1,0:T(8,128)(2,1)} custom-call(s32[8]{0:T(128)} %compare_select_fusion.11.spots_ref.refs_0_, bf16[1024,1152]{1,0:T(8,128)(2,1)} %all-gather.5.cloned.1.call-done.xq_ref.lat_ref.latents_ref, bf16[1024,1280]{1,0:T(8,128)(2,1)} %get-tuple-element.206.query_ref, bf16[1024,1280]{1,0:T(8,128)(2,1)} %get-tuple-element.207.key_value_ref, ...), custom_call_target="tpu_custom_call" | custom-call | flops 1 | bytes 60000000 | tf_op jit(solution)/shard_map/head_sums/pallas_call | solution.py:689
  660.9 11.3 %feed_terms.7 = bf16[1024,2560]{1,0:T(8,128)(2,1)} custom-call(bf16[1024,1664]{1,0:T(8,128)(2,1)} %get-tuple-element.210.refs_0_, bf16[320,1664]{1,0:T(8,128)(2,1)} %constant_dynamic-update-slice_fusion.refs_4_.refs_1_, bf16[320,1664]{1,0:T(8,128)(2,1)} %copy-done.15, bf16[320,1664]{1,0:T(8,128)(2,1)} %copy-done.20, ...), custom_call_target="tpu_custom_call", output_to_operand_aliasing={{}: (5, {})} | custom-call | flops 1 | bytes 33000000 | tf_op jit(solution)/shard_map/feed_terms/pallas_call | solution.py:569
  672.3 7.7 latent_back.1
  685.8 9.5 %token_back.1.in_ref = f32[256,2560]{1,0:T(8,128)} custom-call(bf16[256,1152]{1,0:T(8,128)(2,1)} %get-tuple-element.216.grad_ref, bf16[2560,1152]{1,0:T(8,128)(2,1)} %get-tuple-element.217.weights_ref, bf16[256,2560]{1,0:T(8,128)(2,1)} %reorder.4.refs_1_.tokens_ref, f32[256,2560]{1,0:T(8,128)} %get-tuple-element.281.hidden_ref, ...), custom_call_target="tpu_custom_call" | custom-call | flops 1 | bytes 24000000 | tf_op jit(solution)/shard_map/token_back/pallas_call | solution.py:715
  720.8 5.1 reorder.6
  729.7 12.3 %collective-permute-done.71 = bf16[288,1280]{1,0:T(8,128)(2,1)S(1)} collective-permute-done((bf16[288,1280]{1,0:T(8,128)(2,1)}, bf16[288,1280]{1,0:T(8,128)(2,1)S(1)}, u32[]{:S(2)}, u32[]{:S(2)}) %collective-permute-start.71) | collective-permute-done | bytes 737312 | tf_op jit(solution)/shard_map/ppermute | solution.py:773
  754.2 6.5 unpaired.1
  761.7 10.0 %collective-permute-done.67 = bf16[160,1152]{1,0:T(8,128)(2,1)S(1)} collective-permute-done((bf16[160,1152]{1,0:T(8,128)(2,1)S(1)}, bf16[160,1152]{1,0:T(8,128)(2,1)S(1)}, u32[]{:S(2)}, u32[]{:S(2)}) %collective-permute-start.67) | collective-permute-done | bytes 368672 | tf_op jit(solution)/shard_map/ppermute | solution.py:773
  778.7 3.8 reorder.7
  (445 shorter events, 210.9 us)
Async XLA Ops:
  7.3 160.1 %all-gather.5.cloned.1.call-start = ((), (), s32[]{:S(2)}) async-start(), calls=%async_computation.4 | async-start | bytes 2949120 | tf_op jit(solution)/shard_map/all_gather | solution.py:1059
  29.6 27.0 %collective-permute-start.7 = (bf16[288,1280]{1,0:T(8,128)(2,1)}, bf16[288,1280]{1,0:T(8,128)(2,1)}, u32[]{:S(2)}, u32[]{:S(2)}) collective-permute-start(bf16[288,1280]{1,0:T(8,128)(2,1)} %collective-permute-done.6.refs_8_), channel_id=1, source_target_pairs={{0,8},{8,16},{16,24},{24,28},{28,20},{20,12},{12,4},{4,0},{1,9},{9... | collective-permute-start | bytes 2211848 | tf_op jit(solution)/shard_map/ppermute | solution.py:773
  31.4 25.2 %collective-permute-start.9 = (bf16[288,1280]{1,0:T(8,128)(2,1)}, bf16[288,1280]{1,0:T(8,128)(2,1)}, u32[]{:S(2)}, u32[]{:S(2)}) collective-permute-start(bf16[288,1280]{1,0:T(8,128)(2,1)} %collective-permute-done.8.refs_2_), channel_id=1, source_target_pairs={{8,0},{16,8},{24,16},{28,24},{20,28},{12,20},{4,12},{0,4},{9,1},{1... | collective-permute-start | bytes 2211848 | tf_op jit(solution)/shard_map/ppermute | solution.py:776
  31.7 24.9 %collective-permute-start.2 = (bf16[160,1152]{1,0:T(8,128)(2,1)S(1)}, bf16[160,1152]{1,0:T(8,128)(2,1)S(1)}, u32[]{:S(2)}, u32[]{:S(2)}) collective-permute-start(bf16[160,1152]{1,0:T(8,128)(2,1)S(1)} %pad_maximum_fusion.8.refs_0_.refs_8_), channel_id=1, source_target_pairs={{8,0},{16,8},{24,16},{28,24},{20,28},{12,20},{4,12},{0,4},{9,1},{1... | collective-permute-start | bytes 1105928 | tf_op jit(solution)/shard_map/ppermute | solution.py:776
  33.5 23.1 %collective-permute-start.1 = (bf16[160,1152]{1,0:T(8,128)(2,1)S(1)}, bf16[160,1152]{1,0:T(8,128)(2,1)S(1)}, u32[]{:S(2)}, u32[]{:S(2)}) collective-permute-start(bf16[160,1152]{1,0:T(8,128)(2,1)S(1)} %pad_maximum_fusion.8.refs_0_.refs_8_), channel_id=1, source_target_pairs={{0,1},{1,0},{2,3},{3,2},{4,5},{5,4},{6,7},{7,6},{8,9},{9,8},{10,11... | collective-permute-start | bytes 1105928 | tf_op jit(solution)/shard_map/ppermute | solution.py:908
  33.5 23.1 %collective-permute-start.4 = (bf16[160,1152]{1,0:T(8,128)(2,1)S(1)}, bf16[160,1152]{1,0:T(8,128)(2,1)S(1)}, u32[]{:S(2)}, u32[]{:S(2)}) collective-permute-start(bf16[160,1152]{1,0:T(8,128)(2,1)S(1)} %pad_maximum_fusion.8.refs_0_.refs_8_), channel_id=1, source_target_pairs={{0,8},{8,16},{16,24},{24,28},{28,20},{20,12},{12,4},{4,0},{1,9},{9... | collective-permute-start | bytes 1105928 | tf_op jit(solution)/shard_map/ppermute | solution.py:773
  57.9 26.8 %collective-permute-start.14 = (bf16[288,1280]{1,0:T(8,128)(2,1)}, bf16[288,1280]{1,0:T(8,128)(2,1)S(1)}, u32[]{:S(2)}, u32[]{:S(2)}) collective-permute-start(bf16[288,1280]{1,0:T(8,128)(2,1)} %collective-permute-done.7.refs_7_), channel_id=1, source_target_pairs={{0,8},{8,16},{16,24},{24,28},{28,20},{20,12},{12,4},{4,0},{1,9},{9... | collective-permute-start | bytes 2211848 | tf_op jit(solution)/shard_map/ppermute | solution.py:773
  59.4 26.1 %collective-permute-start.15 = (bf16[288,1280]{1,0:T(8,128)(2,1)}, bf16[288,1280]{1,0:T(8,128)(2,1)}, u32[]{:S(2)}, u32[]{:S(2)}) collective-permute-start(bf16[288,1280]{1,0:T(8,128)(2,1)} %collective-permute-done.9.refs_3_), channel_id=1, source_target_pairs={{8,0},{16,8},{24,16},{28,24},{20,28},{12,20},{4,12},{0,4},{9,1},{1... | collective-permute-start | bytes 2211848 | tf_op jit(solution)/shard_map/ppermute | solution.py:776
  60.0 24.8 %collective-permute-start.5 = (bf16[160,1152]{1,0:T(8,128)(2,1)S(1)}, bf16[160,1152]{1,0:T(8,128)(2,1)S(1)}, u32[]{:S(2)}, u32[]{:S(2)}) collective-permute-start(bf16[160,1152]{1,0:T(8,128)(2,1)S(1)} %collective-permute-done.4.refs_4_.refs_12_), channel_id=1, source_target_pairs={{0,1},{1,0},{2,3},{3,2},{4,5},{5,4},{6,7},{7,6},{8,9},{9,8},{10,11... | collective-permute-start | bytes 1105928 | tf_op jit(solution)/shard_map/ppermute | solution.py:908
  60.1 24.7 %collective-permute-start.12 = (bf16[160,1152]{1,0:T(8,128)(2,1)S(1)}, bf16[160,1152]{1,0:T(8,128)(2,1)}, u32[]{:S(2)}, u32[]{:S(2)}) collective-permute-start(bf16[160,1152]{1,0:T(8,128)(2,1)S(1)} %collective-permute-done.4.refs_4_.refs_12_), channel_id=1, source_target_pairs={{0,8},{8,16},{16,24},{24,28},{28,20},{20,12},{12,4},{4,0},{1,9},{9... | collective-permute-start | bytes 1105928 | tf_op jit(solution)/shard_map/ppermute | solution.py:773
  114.8 25.2 %collective-permute-start.26 = (bf16[320,1664]{1,0:T(8,128)(2,1)S(1)}, bf16[320,1664]{1,0:T(8,128)(2,1)}, u32[]{:S(2)}, u32[]{:S(2)}) collective-permute-start(bf16[320,1664]{1,0:T(8,128)(2,1)S(1)} %pad.18.refs_0_.refs_1_), channel_id=1, source_target_pairs={{0,8},{8,16},{16,24},{24,28},{28,20},{20,12},{12,4},{4,0},{1,9},{9... | collective-permute-start | bytes 3194888 | tf_op jit(solution)/shard_map/ppermute | solution.py:773
  116.4 23.9 %collective-permute-start.27 = (bf16[320,1664]{1,0:T(8,128)(2,1)S(1)}, bf16[320,1664]{1,0:T(8,128)(2,1)}, u32[]{:S(2)}, u32[]{:S(2)}) collective-permute-start(bf16[320,1664]{1,0:T(8,128)(2,1)S(1)} %pad.18.refs_0_.refs_1_), channel_id=1, source_target_pairs={{8,0},{16,8},{24,16},{28,24},{20,28},{12,20},{4,12},{0,4},{9,1},{1... | collective-permute-start | bytes 3194888 | tf_op jit(solution)/shard_map/ppermute | solution.py:776
  140.3 77.3 %all-gather.7.cloned.1.call-start = ((), (), s32[]{:S(2)}) async-start(), calls=%async_computation.5 | async-start | bytes 6553600 | tf_op jit(solution)/shard_map/all_gather | solution.py:1096
  140.4 25.5 %collective-permute-start.28 = (bf16[320,1664]{1,0:T(8,128)(2,1)}, bf16[320,1664]{1,0:T(8,128)(2,1)S(1)}, u32[]{:S(2)}, u32[]{:S(2)}) collective-permute-start(bf16[320,1664]{1,0:T(8,128)(2,1)} %collective-permute-done.26.refs_7_.refs_4_), channel_id=1, source_target_pairs={{0,8},{8,16},{16,24},{24,28},{28,20},{20,12},{12,4},{4,0},{1,9},{9... | collective-permute-start | bytes 3194888 | tf_op jit(solution)/shard_map/ppermute | solution.py:773
  142.0 25.3 %collective-permute-start.29 = (bf16[320,1664]{1,0:T(8,128)(2,1)}, bf16[320,1664]{1,0:T(8,128)(2,1)S(1)}, u32[]{:S(2)}, u32[]{:S(2)}) collective-permute-start(bf16[320,1664]{1,0:T(8,128)(2,1)} %collective-permute-done.27.refs_1_.refs_2_), channel_id=1, source_target_pairs={{8,0},{16,8},{24,16},{28,24},{20,28},{12,20},{4,12},{0,4},{9,1},{1... | collective-permute-start | bytes 3194888 | tf_op jit(solution)/shard_map/ppermute | solution.py:776
  167.4 101.1 %reduce-scatter.5.cloned.1.call-start = ((), (), s32[]{:S(2)}) async-start(), calls=%async_computation.6 | async-start | bytes 6553600 | tf_op jit(solution)/shard_map/reduce_scatter | solution.py:1103
  170.9 45.4 %collective-permute-start.30 = (bf16[320,3200]{1,0:T(8,128)(2,1)}, bf16[320,3200]{1,0:T(8,128)(2,1)}, u32[]{:S(2)}, u32[]{:S(2)}) collective-permute-start(bf16[320,3200]{1,0:T(8,128)(2,1)} %paired.1.refs_0_.refs_1_.weights_ref), channel_id=1, source_target_pairs={{0,8},{8,16},{16,24},{24,28},{28,20},{20,12},{12,4},{4,0},{1,9},{9... | collective-permute-start | bytes 6144008 | tf_op jit(solution)/shard_map/ppermute | solution.py:773
  172.5 45.1 %collective-permute-start.31 = (bf16[320,3200]{1,0:T(8,128)(2,1)}, bf16[320,3200]{1,0:T(8,128)(2,1)}, u32[]{:S(2)}, u32[]{:S(2)}) collective-permute-start(bf16[320,3200]{1,0:T(8,128)(2,1)} %paired.1.refs_0_.refs_1_.weights_ref), channel_id=1, source_target_pairs={{8,0},{16,8},{24,16},{28,24},{20,28},{12,20},{4,12},{0,4},{9,1},{1... | collective-permute-start | bytes 6144008 | tf_op jit(solution)/shard_map/ppermute | solution.py:776
  217.7 149.3 %all-gather.9.cloned.1.call-start = ((), (), s32[]{:S(2)}) async-start(), calls=%async_computation.7 | async-start | bytes 6553600 | tf_op jit(solution)/shard_map/all_gather | solution.py:1113
  217.7 26.7 %collective-permute-start.32 = (bf16[320,1664]{1,0:T(8,128)(2,1)}, bf16[320,1664]{1,0:T(8,128)(2,1)S(1)}, u32[]{:S(2)}, u32[]{:S(2)}) collective-permute-start(bf16[320,1664]{1,0:T(8,128)(2,1)} %copy-done.20), channel_id=1, source_target_pairs={{0,8},{8,16},{16,24},{24,28},{28,20},{20,12},{12,4},{4,0},{1,9},{9... | collective-permute-start | bytes 3194888 | tf_op jit(solution)/shard_map/ppermute | solution.py:773
  219.3 26.8 %collective-permute-start.33 = (bf16[320,1664]{1,0:T(8,128)(2,1)}, bf16[320,1664]{1,0:T(8,128)(2,1)}, u32[]{:S(2)}, u32[]{:S(2)}) collective-permute-start(bf16[320,1664]{1,0:T(8,128)(2,1)} %copy-done.21), channel_id=1, source_target_pairs={{8,0},{16,8},{24,16},{28,24},{20,28},{12,20},{4,12},{0,4},{9,1},{1... | collective-permute-start | bytes 3194888 | tf_op jit(solution)/shard_map/ppermute | solution.py:776
  219.8 65.0 %collective-permute-start.34 = (bf16[320,3200]{1,0:T(8,128)(2,1)}, bf16[320,3200]{1,0:T(8,128)(2,1)}, u32[]{:S(2)}, u32[]{:S(2)}) collective-permute-start(bf16[320,3200]{1,0:T(8,128)(2,1)} %collective-permute-done.30.refs_7_.refs_4_), channel_id=1, source_target_pairs={{0,8},{8,16},{16,24},{24,28},{28,20},{20,12},{12,4},{4,0},{1,9},{9... | collective-permute-start | bytes 6144008 | tf_op jit(solution)/shard_map/ppermute | solution.py:773
  221.3 64.7 %collective-permute-start.35 = (bf16[320,3200]{1,0:T(8,128)(2,1)}, bf16[320,3200]{1,0:T(8,128)(2,1)}, u32[]{:S(2)}, u32[]{:S(2)}) collective-permute-start(bf16[320,3200]{1,0:T(8,128)(2,1)} %collective-permute-done.31.refs_1_.refs_2_), channel_id=1, source_target_pairs={{8,0},{16,8},{24,16},{28,24},{20,28},{12,20},{4,12},{0,4},{9,1},{1... | collective-permute-start | bytes 6144008 | tf_op jit(solution)/shard_map/ppermute | solution.py:776
  286.0 240.0 %reduce-scatter.7.cloned.1.call-start = ((), (), s32[]{:S(2)}) async-start(), calls=%async_computation.8 | async-start | bytes 6553600 | tf_op jit(solution)/shard_map/reduce_scatter | solution.py:1138
  301.7 42.8 %collective-permute-start.38 = (bf16[320,3200]{1,0:T(8,128)(2,1)}, bf16[320,3200]{1,0:T(8,128)(2,1)S(1)}, u32[]{:S(2)}, u32[]{:S(2)}) collective-permute-start(bf16[320,3200]{1,0:T(8,128)(2,1)} %collective-permute-done.35.refs_2_.refs_3_), channel_id=1, source_target_pairs={{8,0},{16,8},{24,16},{28,24},{20,28},{12,20},{4,12},{0,4},{9,1},{1... | collective-permute-start | bytes 6144008 | tf_op jit(solution)/shard_map/ppermute | solution.py:776
  302.0 42.4 %collective-permute-start.39 = (bf16[320,3200]{1,0:T(8,128)(2,1)}, bf16[320,3200]{1,0:T(8,128)(2,1)S(1)}, u32[]{:S(2)}, u32[]{:S(2)}) collective-permute-start(bf16[320,3200]{1,0:T(8,128)(2,1)} %collective-permute-done.34.refs_6_.refs_3_), channel_id=1, source_target_pairs={{0,8},{8,16},{16,24},{24,28},{28,20},{20,12},{12,4},{4,0},{1,9},{9... | collective-permute-start | bytes 6144008 | tf_op jit(solution)/shard_map/ppermute | solution.py:773
  418.7 25.9 %collective-permute-start.44 = (bf16[160,3200]{1,0:T(8,128)(2,1)}, bf16[160,3200]{1,0:T(8,128)(2,1)}, u32[]{:S(2)}, u32[]{:S(2)}) collective-permute-start(bf16[160,3200]{1,0:T(8,128)(2,1)} %get-tuple-element.285), channel_id=1, source_target_pairs={{0,8},{8,16},{16,24},{24,28},{28,20},{20,12},{12,4},{4,0},{1,9},{9... | collective-permute-start | bytes 3072008 | tf_op jit(solution)/shard_map/ppermute | solution.py:773
  420.4 25.9 %collective-permute-start.45 = (bf16[160,3200]{1,0:T(8,128)(2,1)}, bf16[160,3200]{1,0:T(8,128)(2,1)}, u32[]{:S(2)}, u32[]{:S(2)}) collective-permute-start(bf16[160,3200]{1,0:T(8,128)(2,1)} %get-tuple-element.284), channel_id=1, source_target_pairs={{8,0},{16,8},{24,16},{28,24},{20,28},{12,20},{4,12},{0,4},{9,1},{1... | collective-permute-start | bytes 3072008 | tf_op jit(solution)/shard_map/ppermute | solution.py:776
  423.3 46.6 %collective-permute-start.47 = (bf16[320,1664]{1,0:T(8,128)(2,1)}, bf16[320,1664]{1,0:T(8,128)(2,1)}, u32[]{:S(2)}, u32[]{:S(2)}) collective-permute-start(bf16[320,1664]{1,0:T(8,128)(2,1)} %pad_maximum_fusion.4), channel_id=1, source_target_pairs={{8,0},{16,8},{24,16},{28,24},{20,28},{12,20},{4,12},{0,4},{9,1},{1... | collective-permute-start | bytes 3194888 | tf_op jit(solution)/shard_map/ppermute | solution.py:776
  424.6 45.3 %collective-permute-start.46 = (bf16[320,1664]{1,0:T(8,128)(2,1)}, bf16[320,1664]{1,0:T(8,128)(2,1)}, u32[]{:S(2)}, u32[]{:S(2)}) collective-permute-start(bf16[320,1664]{1,0:T(8,128)(2,1)} %pad_maximum_fusion.3), channel_id=1, source_target_pairs={{0,8},{8,16},{16,24},{24,28},{28,20},{20,12},{12,4},{4,0},{1,9},{9... | collective-permute-start | bytes 3194888 | tf_op jit(solution)/shard_map/ppermute | solution.py:773
  469.9 111.5 %all-gather.11.cloned.1.call-start = ((), (), s32[]{:S(2)}) async-start(), calls=%async_computation.9 | async-start | bytes 6553600 | tf_op jit(solution)/shard_map/all_gather | solution.py:1154
  470.0 50.3 %collective-permute-start.49 = (bf16[320,3200]{1,0:T(8,128)(2,1)}, bf16[320,3200]{1,0:T(8,128)(2,1)S(1)}, u32[]{:S(2)}, u32[]{:S(2)}) collective-permute-start(bf16[320,3200]{1,0:T(8,128)(2,1)} %pad_maximum_fusion.2), channel_id=1, source_target_pairs={{8,0},{16,8},{24,16},{28,24},{20,28},{12,20},{4,12},{0,4},{9,1},{1... | collective-permute-start | bytes 6144008 | tf_op jit(solution)/shard_map/ppermute | solution.py:776
  470.3 49.9 %collective-permute-start.48 = (bf16[320,3200]{1,0:T(8,128)(2,1)}, bf16[320,3200]{1,0:T(8,128)(2,1)}, u32[]{:S(2)}, u32[]{:S(2)}) collective-permute-start(bf16[320,3200]{1,0:T(8,128)(2,1)} %pad_maximum_fusion.1), channel_id=1, source_target_pairs={{0,8},{8,16},{16,24},{24,28},{28,20},{20,12},{12,4},{4,0},{1,9},{9... | collective-permute-start | bytes 6144008 | tf_op jit(solution)/shard_map/ppermute | solution.py:773
  481.1 51.7 %collective-permute-start.51 = (bf16[320,1664]{1,0:T(8,128)(2,1)}, bf16[320,1664]{1,0:T(8,128)(2,1)}, u32[]{:S(2)}, u32[]{:S(2)}) collective-permute-start(bf16[320,1664]{1,0:T(8,128)(2,1)} %add_convert_fusion.8), channel_id=1, source_target_pairs={{8,0},{16,8},{24,16},{28,24},{20,28},{12,20},{4,12},{0,4},{9,1},{1... | collective-permute-start | bytes 3194888 | tf_op jit(solution)/shard_map/ppermute | solution.py:776
  484.0 48.8 %collective-permute-start.50 = (bf16[320,1664]{1,0:T(8,128)(2,1)}, bf16[320,1664]{1,0:T(8,128)(2,1)}, u32[]{:S(2)}, u32[]{:S(2)}) collective-permute-start(bf16[320,1664]{1,0:T(8,128)(2,1)} %add_convert_fusion.9), channel_id=1, source_target_pairs={{0,8},{8,16},{16,24},{24,28},{28,20},{20,12},{12,4},{4,0},{1,9},{9... | collective-permute-start | bytes 3194888 | tf_op jit(solution)/shard_map/ppermute | solution.py:773
  532.8 139.4 %reduce-scatter.11.cloned.1.call-start = ((), (), s32[]{:S(2)}) async-start(), calls=%async_computation.11 | async-start | bytes 2949120 | tf_op jit(solution)/shard_map/reduce_scatter | solution.py:1173
  532.9 41.0 %collective-permute-start.53 = (bf16[320,3200]{1,0:T(8,128)(2,1)}, bf16[320,3200]{1,0:T(8,128)(2,1)S(1)}, u32[]{:S(2)}, u32[]{:S(2)}) collective-permute-start(bf16[320,3200]{1,0:T(8,128)(2,1)} %add_convert_fusion.3), channel_id=1, source_target_pairs={{8,0},{16,8},{24,16},{28,24},{20,28},{12,20},{4,12},{0,4},{9,1},{1... | collective-permute-start | bytes 6144008 | tf_op jit(solution)/shard_map/ppermute | solution.py:776
  534.0 40.3 %collective-permute-start.52 = (bf16[320,3200]{1,0:T(8,128)(2,1)}, bf16[320,3200]{1,0:T(8,128)(2,1)S(1)}, u32[]{:S(2)}, u32[]{:S(2)}) collective-permute-start(bf16[320,3200]{1,0:T(8,128)(2,1)} %add_convert_fusion.4), channel_id=1, source_target_pairs={{0,8},{8,16},{16,24},{24,28},{28,20},{20,12},{12,4},{4,0},{1,9},{9... | collective-permute-start | bytes 6144008 | tf_op jit(solution)/shard_map/ppermute | solution.py:773
  579.4 42.4 %collective-permute-start.55 = (bf16[320,3200]{1,0:T(8,128)(2,1)}, bf16[320,3200]{1,0:T(8,128)(2,1)S(1)}, u32[]{:S(2)}, u32[]{:S(2)}) collective-permute-start(bf16[320,3200]{1,0:T(8,128)(2,1)} %add_convert_fusion.1), channel_id=1, source_target_pairs={{8,0},{16,8},{24,16},{28,24},{20,28},{12,20},{4,12},{0,4},{9,1},{1... | collective-permute-start | bytes 6144008 | tf_op jit(solution)/shard_map/ppermute | solution.py:776
  580.9 40.9 %collective-permute-start.54 = (bf16[320,3200]{1,0:T(8,128)(2,1)}, bf16[320,3200]{1,0:T(8,128)(2,1)}, u32[]{:S(2)}, u32[]{:S(2)}) collective-permute-start(bf16[320,3200]{1,0:T(8,128)(2,1)} %add_convert_fusion.2), channel_id=1, source_target_pairs={{0,8},{8,16},{16,24},{24,28},{28,20},{20,12},{12,4},{4,0},{1,9},{9... | collective-permute-start | bytes 6144008 | tf_op jit(solution)/shard_map/ppermute | solution.py:773
  629.3 146.2 %reduce-scatter.9.cloned.1.call-start = ((), (), s32[]{:S(2)}) async-start(), calls=%async_computation.10 | async-start | bytes 6553600 | tf_op jit(solution)/shard_map/reduce_scatter | solution.py:1200
  633.1 22.0 %collective-permute-start.57 = (bf16[320,1664]{1,0:T(8,128)(2,1)S(1)}, bf16[320,1664]{1,0:T(8,128)(2,1)S(1)}, u32[]{:S(2)}, u32[]{:S(2)}) collective-permute-start(bf16[320,1664]{1,0:T(8,128)(2,1)S(1)} %add_convert_fusion.6), channel_id=1, source_target_pairs={{8,0},{16,8},{24,16},{28,24},{20,28},{12,20},{4,12},{0,4},{9,1},{1... | collective-permute-start | bytes 3194888 | tf_op jit(solution)/shard_map/ppermute | solution.py:776
  718.3 23.8 %collective-permute-start.71 = (bf16[288,1280]{1,0:T(8,128)(2,1)}, bf16[288,1280]{1,0:T(8,128)(2,1)S(1)}, u32[]{:S(2)}, u32[]{:S(2)}) collective-permute-start(bf16[288,1280]{1,0:T(8,128)(2,1)} %get-tuple-element.291), channel_id=1, source_target_pairs={{0,8},{8,16},{16,24},{24,28},{28,20},{20,12},{12,4},{4,0},{1,9},{9... | collective-permute-start | bytes 2211848 | tf_op jit(solution)/shard_map/ppermute | solution.py:773
  719.9 22.2 %collective-permute-start.72 = (bf16[288,1280]{1,0:T(8,128)(2,1)S(1)}, bf16[288,1280]{1,0:T(8,128)(2,1)}, u32[]{:S(2)}, u32[]{:S(2)}) collective-permute-start(bf16[288,1280]{1,0:T(8,128)(2,1)S(1)} %get-tuple-element.290), channel_id=1, source_target_pairs={{8,0},{16,8},{24,16},{28,24},{20,28},{12,20},{4,12},{0,4},{9,1},{1... | collective-permute-start | bytes 2211848 | tf_op jit(solution)/shard_map/ppermute | solution.py:776
  727.6 22.3 %collective-permute-start.65 = (bf16[160,1152]{1,0:T(8,128)(2,1)S(1)}, bf16[160,1152]{1,0:T(8,128)(2,1)S(1)}, u32[]{:S(2)}, u32[]{:S(2)}) collective-permute-start(bf16[160,1152]{1,0:T(8,128)(2,1)S(1)} %get-tuple-element.307), channel_id=1, source_target_pairs={{0,8},{8,16},{16,24},{24,28},{28,20},{20,12},{12,4},{4,0},{1,9},{9... | collective-permute-start | bytes 1105928 | tf_op jit(solution)/shard_map/ppermute | solution.py:773
  745.1 27.4 %collective-permute-start.73 = (bf16[288,1280]{1,0:T(8,128)(2,1)}, bf16[288,1280]{1,0:T(8,128)(2,1)S(1)}, u32[]{:S(2)}, u32[]{:S(2)}) collective-permute-start(bf16[288,1280]{1,0:T(8,128)(2,1)} %get-tuple-element.289), channel_id=1, source_target_pairs={{0,8},{8,16},{16,24},{24,28},{28,20},{20,12},{12,4},{4,0},{1,9},{9... | collective-permute-start | bytes 2211848 | tf_op jit(solution)/shard_map/ppermute | solution.py:773
  746.0 26.6 %collective-permute-start.74 = (bf16[288,1280]{1,0:T(8,128)(2,1)}, bf16[288,1280]{1,0:T(8,128)(2,1)}, u32[]{:S(2)}, u32[]{:S(2)}) collective-permute-start(bf16[288,1280]{1,0:T(8,128)(2,1)} %get-tuple-element.288), channel_id=1, source_target_pairs={{8,0},{16,8},{24,16},{28,24},{20,28},{12,20},{4,12},{0,4},{9,1},{1... | collective-permute-start | bytes 2211848 | tf_op jit(solution)/shard_map/ppermute | solution.py:776
  750.1 21.6 %collective-permute-start.67 = (bf16[160,1152]{1,0:T(8,128)(2,1)S(1)}, bf16[160,1152]{1,0:T(8,128)(2,1)S(1)}, u32[]{:S(2)}, u32[]{:S(2)}) collective-permute-start(bf16[160,1152]{1,0:T(8,128)(2,1)S(1)} %get-tuple-element.305), channel_id=1, source_target_pairs={{0,8},{8,16},{16,24},{24,28},{28,20},{20,12},{12,4},{4,0},{1,9},{9... | collective-permute-start | bytes 1105928 | tf_op jit(solution)/shard_map/ppermute | solution.py:773
  (116 other events, 1724.3 us)
Sparse Core Ops, SparseCore 0:
  140.5 25.1 all-gather.4
  167.8 40.4 all-gather.6
  217.8 50.6 reduce-scatter.4
  286.2 39.1 all-gather.8
  470.0 48.8 reduce-scatter.6
  532.9 41.1 all-gather.10
  629.4 32.9 reduce-scatter.10
  680.2 51.4 reduce-scatter.8

commit v4 on v3

--- a/solution.py
+++ b/solution.py
@@ -553,11 +553,12 @@
         copy.start()
     copies[0].wait()
     ready = 0
-    for start in range(0, right_ref.shape[0], TILE):
-        while ready * rows < min(start + TILE, right_ref.shape[0]):
+    for start in range(0, right_ref.shape[0], 2 * TILE):
+        stop = min(start + 2 * TILE, right_ref.shape[0])
+        while ready * rows < stop:
             copies[ready + 1].wait()
             ready += 1
-        part = slice(start, start + TILE)
+        part = slice(start, stop)
         out_ref[:, part] = product_right(left_ref[...], right_ref[part, :]).astype(jnp.bfloat16)
 
 
@@ -994,21 +995,19 @@
     ahead, behind = ring.ahead, ring.behind
     team_ids = shard ^ jnp.asarray([0, 2, 1, 3], jnp.int32)
 
-    small_up = Gather(ring, jnp.concatenate([packed, swap(packed, 2)], axis=0))
+    small_up = Gather(ring, packed)
     pieces, copies = [], []
 
-    def collect(block, spot, team):
-        for first, piece in ((team, block), (team + 2, swap(block, 1))):
-            for part in range(block.shape[0] // down_rows):
-                copies.append(
-                    (len(pieces), part * down_rows, down_rows, spot * teams, first + part)
-                )
+    def collect(block, spot, first):
+        across = swap(block, 2)
+        for team, piece in enumerate((block, across, swap(block, 1), swap(across, 1))):
+            rows = block.shape[0]
+            copies.append((len(pieces), 0, rows, spot * teams, team, first))
             pieces.append(piece)
 
     collect(small_up.low, 0, 0)
-    mixed_up.advance()
     while not small_up.done:
-        swapped = pieces[1::2]
+        swapped = [piece for place, piece in enumerate(pieces) if place % 4]
         small_up.advance()
         mixed_up.advance()
         if not small_up.done:
@@ -1016,8 +1015,8 @@
             collect(small_up.low, ring.count - small_up.step, 0)
             hold(small_up, ends(mixed_up), swapped)
             hold(mixed_up, ends(small_up))
-    collect(small_up.low, ring.half, 0)
-    collect(small_up.high, ring.half, 1)
+    collect(jnp.concatenate([small_up.low, small_up.high], axis=0), ring.half, 0)
+    copies = [(piece, row, rows, block, team) for piece, row, rows, block, team, _ in copies]
     hold(down_up, ends(mixed_up, small_up))
     down_up.advance()
     if down_rows % 16:
@@ -1239,14 +1238,15 @@
     hold(grad_down, ends(grad_small))
     hold(grad_small, token_grad)
     grad_small.advance()
-    hold(grad_pair, grad_small.sent)
-    grad_mixed.advance()
-    grad_small.advance()
     feed_branch = follow(feed_branch, grad_small.sent)
     output = hidden + RESIDUAL * feed_branch.astype(jnp.float32)
     output = reorder(output.astype(low), ring.behind)
+    grad_mixed.advance()
+    hold(grad_small, output)
+    grad_small.advance()
+    hold(grad_pair, grad_small.sent)
     small_own = grad_small.finish()
-    small_other = follow(small_own[down_rows:].astype(low), ends(grad_mixed), output)
+    small_other = follow(small_own[down_rows:].astype(low), ends(grad_mixed))
     packed_own = small_own[:down_rows] + swap(small_other, 2).astype(jnp.float32)
     rope_from = rank + KVR + NOPE
     lanes = jnp.arange(down_width) < rope_from + ROPE

time: 812 us -> 801 us (0.986)
  waiting for transfers between devices: 287 us -> 271 us
  starting transfers between devices: 74.2 us -> 84.9 us
    ppermute x32, waiting for transfers between devices: 154 us -> 115 us  [send_up(): return lax.ppermute(block, self.axis, self.up)]
    ppermute x14 -> x28, waiting for transfers between devices: 2.3 us -> 18.7 us  [swap(): return lax.ppermute(values, 'tensor', [(i, i ^ bit) for i in range(count)])]
    ppermute x14 -> x28, starting transfers between devices: 4.69 us -> 14.1 us  [swap(): return lax.ppermute(values, 'tensor', [(i, i ^ bit) for i in range(count)])]
  transfers between devices with their start and end apart: 86 -> 100, of which waited for: 36 -> 43; matrix products, arithmetic and copies ran while one was open for 19% -> 19% of each run, Pallas kernels for 25% -> 27%
where the time goes in v4:
time: 801 us; the launch traced here: 792 us
  waiting for transfers between devices  271 us (34%)
  Pallas kernels  237 us (30%)
  starting transfers between devices  84.9 us (11%)
  other arithmetic  82.4 us (10%)
  matrix products  67.3 us (8%)
  local copies, waits for them, and re-layouts  33.3 us (4%)
  between operations  15.8 us (2%)
    ppermute x32, waiting for transfers between devices, send_up(): return lax.ppermute(block, self.axis, self.up)  115 us
    ppermute x32, waiting for transfers between devices, send_down(): return lax.ppermute(block, self.axis, self.down)  114 us
    pallas_call x4, Pallas kernels, feed_terms(): pl.pallas_call(functools.partial(terms_kernel, len(pieces)), grid=(1,), i...  59.5 us
    dot_general x6, matrix products, product_left(): lax.dot_general(left, right, (((0,), (0,)), ((), ())), preferred_element_...  45.6 us
    ppermute x32, starting transfers between devices, send_up(): return lax.ppermute(block, self.axis, self.up)  40.1 us
    convert_element_type x16, other arithmetic, add(): return (a.astype(jnp.float32) + b.astype(jnp.float32)).astype(b.dtype)  35.5 us
    pallas_call x1, Pallas kernels, attention_backward(): pl.pallas_call(backward_kernel, grid=(pairs,), in_specs=[mine(2 * LANES),...  31.8 us
    ppermute x32, starting transfers between devices, send_down(): return lax.ppermute(block, self.axis, self.down)  30.4 us
  transfers between devices with their start and end apart: 100, of which 43 were waited for; matrix products, arithmetic and copies ran while one was open for 19% of the time, Pallas kernels for 27%

profile of v4, /device:TPU:0, one launch (start us, length us, event | category | flops | bytes accessed | tf_op | source)
XLA Modules:
  0.0 791.9 jit_solution(16773960150781946295)
XLA Ops:
  21.3 13.6 %collective-permute-done.3.refs_4_.refs_12_ = bf16[80,1152]{1,0:T(8,128)(2,1)S(1)} collective-permute-done((bf16[80,1152]{1,0:T(8,128)(2,1)S(1)}, bf16[80,1152]{1,0:T(8,128)(2,1)S(1)}, u32[]{:S(2)}, u32[]{:S(2)}) %collective-permute-start.3) | collective-permute-done | bytes 184352 | tf_op jit(solution)/shard_map/ppermute | solution.py:777
  39.1 4.6 collective-permute-done.8.refs_9_.refs_17_
  48.7 8.8 %collective-permute-done.13.refs_12_.refs_20_ = bf16[80,1152]{1,0:T(8,128)(2,1)} collective-permute-done((bf16[80,1152]{1,0:T(8,128)(2,1)S(1)}, bf16[80,1152]{1,0:T(8,128)(2,1)}, u32[]{:S(2)}, u32[]{:S(2)}) %collective-permute-start.13) | collective-permute-done | bytes 184352 | tf_op jit(solution)/shard_map/ppermute | solution.py:777
  73.1 7.2 collective-permute-done.23.refs_20_.refs_28_
  88.3 3.5 collective-permute-done.34
  98.2 3.6 collective-permute-done.39
  105.1 3.7 reorder.4.refs_1_.tokens_ref
  118.0 10.0 %project.1 = (bf16[256,1152]{1,0:T(8,128)(2,1)}, f32[256,1152]{1,0:T(8,128)}, bf16[256,2560]{1,0:T(8,128)(2,1)}, bf16[2560,1152]{1,0:T(8,128)(2,1)}) custom-call(s32[4]{0:T(128)} %broadcast_xor_fusion.team_ref.refs_0_, bf16[256,2560]{1,0:T(8,128)(2,1)} %reorder.4.refs_1_.tokens_ref, f32[1,2560]{1,0:T(1,128)} %reshape.321.refs_2_.gain_ref, ...), custom_call_target="tpu_custom_call" | custom-call | flops 1 | bytes 30000000 | tf_op jit(solution)/shard_map/project/pallas_call | solution.py:383
  131.6 3.7 reorder.5
  138.1 16.0 %collective-permute-done.42.refs_6_.refs_3_ = bf16[320,1664]{1,0:T(8,128)(2,1)S(1)} collective-permute-done((bf16[320,1664]{1,0:T(8,128)(2,1)}, bf16[320,1664]{1,0:T(8,128)(2,1)S(1)}, u32[]{:S(2)}, u32[]{:S(2)}) %collective-permute-start.42) | collective-permute-done | bytes 1064992 | tf_op jit(solution)/shard_map/ppermute | solution.py:774
  163.6 6.4 assemble.1
  171.8 23.4 %attention_forward.1 = (bf16[1024,640]{1,0:T(8,128)(2,1)}, bf16[1024,1280]{1,0:T(8,128)(2,1)}, bf16[1024,1280]{1,0:T(8,128)(2,1)}, f32[5,2,1024]{2,1,0:T(2,128)}) custom-call(bf16[1024,1152]{1,0:T(8,128)(2,1)} %all-gather.5.cloned.1.call-done.xq_ref.lat_ref.latents_ref, bf16[1024,1152]{1,0:T(8,128)(2,1)} %all-gather.5.cloned.1.call-done.xq_ref.lat_ref.latents_ref, ...), custom_call_target="tpu_custom_call" | custom-call | flops 1 | bytes 69000000 | tf_op jit(solution)/shard_map/attention_forward/pallas_call | solution.py:148
  195.2 7.4 convolution_convert_fusion.4
  208.0 22.5 %collective-permute-done.46.refs_5_.refs_2_ = bf16[320,1664]{1,0:T(8,128)(2,1)S(1)} collective-permute-done((bf16[320,1664]{1,0:T(8,128)(2,1)}, bf16[320,1664]{1,0:T(8,128)(2,1)S(1)}, u32[]{:S(2)}, u32[]{:S(2)}) %collective-permute-start.46) | collective-permute-done | bytes 1064992 | tf_op jit(solution)/shard_map/ppermute | solution.py:774
  231.6 23.9 %reduce-scatter.5.cloned.1.call-done = bf16[256,2560]{1,0:T(8,128)(2,1)} async-done(((bf16[1024,2560]{1,0:T(8,128)(2,1)}), bf16[256,2560]{1,0:T(8,128)(2,1)}) %reduce-scatter.5.cloned.1.call-update) | async-done | bytes 1310736 | tf_op jit(solution)/shard_map/reduce_scatter | solution.py:1102
  259.2 11.5 %collective-permute-done.48.refs_6_.refs_3_ = bf16[320,3200]{1,0:T(8,128)(2,1)} collective-permute-done((bf16[320,3200]{1,0:T(8,128)(2,1)}, bf16[320,3200]{1,0:T(8,128)(2,1)}, u32[]{:S(2)}, u32[]{:S(2)}) %collective-permute-start.48) | collective-permute-done | bytes 2048032 | tf_op jit(solution)/shard_map/ppermute | solution.py:774
  275.9 7.0 collective-permute-done.50
  282.9 4.4 collective-permute-done.51
  291.1 15.2 %feed_product.1.refs_8_ = f32[1024,1664]{1,0:T(8,128)} custom-call(bf16[1024,2560]{1,0:T(8,128)(2,1)} %all-gather.7.cloned.1.call-done.left_ref, bf16[320,1664]{1,0:T(8,128)(2,1)} %copy-done.9, bf16[320,1664]{1,0:T(8,128)(2,1)} %collective-permute-done.41.refs_1_.refs_2_, bf16[320,1664]{1,0:T(8,128)(2,1)} %copy-done.18, ...), custom_call_target="tpu_custom_call" | custom-call | flops 1 | bytes 45000000 | tf_op jit(solution)/shard_map/feed_product/pallas_call | solution.py:511
  306.3 24.7 %collective-permute-done.52.refs_3_.refs_4_ = bf16[320,3200]{1,0:T(8,128)(2,1)S(1)} collective-permute-done((bf16[320,3200]{1,0:T(8,128)(2,1)}, bf16[320,3200]{1,0:T(8,128)(2,1)S(1)}, u32[]{:S(2)}, u32[]{:S(2)}) %collective-permute-start.52) | collective-permute-done | bytes 2048032 | tf_op jit(solution)/shard_map/ppermute | solution.py:777
  333.5 15.7 %collective-permute-done.54 = bf16[160,3200]{1,0:T(8,128)(2,1)S(1)} collective-permute-done((bf16[160,3200]{1,0:T(8,128)(2,1)S(1)}, bf16[160,3200]{1,0:T(8,128)(2,1)S(1)}, u32[]{:S(2)}, u32[]{:S(2)}) %collective-permute-start.54) | collective-permute-done | bytes 1024032 | tf_op jit(solution)/shard_map/ppermute | solution.py:774
  352.0 26.3 %feed_gate.1 = (bf16[1024,1664]{1,0:T(8,128)(2,1)}, bf16[1024,3200]{1,0:T(8,128)(2,1)}) custom-call(bf16[1024,2560]{1,0:T(8,128)(2,1)} %all-gather.9.cloned.1.call-done.left_ref, bf16[320,3200]{1,0:T(8,128)(2,1)} %paired.1.refs_0_.refs_1_.weights_ref, bf16[320,3200]{1,0:T(8,128)(2,1)} %collective-permute-done.45.refs_1_.refs_2_, ...), custom_call_target="tpu_custom_call" | custom-call | flops 1 | bytes 78000000 | tf_op jit(solution)/shard_map/feed_gate/pallas_call | solution.py:527
  378.3 7.9 convolution_convert_fusion.1
  390.2 9.6 %convolution_convert_fusion = bf16[1280,3200]{1,0:T(8,128)(2,1)S(1)} fusion(bf16[1024,3200]{1,0:T(8,128)(2,1)S(1)} %copy-done.3, bf16[1024,2560]{1,0:T(8,128)(2,1)S(1)} %bitcast.55), kind=kOutput, calls=%fused_computation.2 | convolution fusion | flops 8392704000 | bytes 17367040 | tf_op jit(solution)/shard_map/dot_general | solution.py:50
  411.8 18.3 %feed_terms.4.refs_5_ = bf16[1024,2560]{1,0:T(8,128)(2,1)} custom-call(bf16[1024,3200]{1,0:T(8,128)(2,1)} %get-tuple-element.187.refs_0_, bf16[320,3200]{1,0:T(8,128)(2,1)} %paired.1.refs_0_.refs_1_.weights_ref, bf16[320,3200]{1,0:T(8,128)(2,1)} %collective-permute-done.45.refs_1_.refs_2_, bf16[320,3200]{1,0:T(8,128)(2,1)} %collective-permute-done.49.refs_2_.refs_3_, ...), custom_call_target="tpu_custom_call" | custom-call | flops 1 | bytes 54000000 | tf_op jit(solution)/shard_map/feed_terms/pallas_call | solution.py:570
  436.4 18.5 %feed_terms.5 = bf16[1024,2560]{1,0:T(8,128)(2,1)} custom-call(bf16[1024,3200]{1,0:T(8,128)(2,1)} %get-tuple-element.187.refs_0_, bf16[320,3200]{1,0:T(8,128)(2,1)} %constant_dynamic-update-slice_fusion.4.refs_4_.refs_1_, bf16[320,3200]{1,0:T(8,128)(2,1)} %copy-done.5, ...), custom_call_target="tpu_custom_call", output_to_operand_aliasing={{}: (5, {})} | custom-call | flops 1 | bytes 54000000 | tf_op jit(solution)/shard_map/feed_terms/pallas_call | solution.py:570
  457.1 5.6 convolution_convert_fusion.6
  471.0 5.3 convolution_convert_fusion.5
  476.3 11.4 %feed_terms.6.refs_5_ = bf16[1024,2560]{1,0:T(8,128)(2,1)} custom-call(bf16[1024,1664]{1,0:T(8,128)(2,1)} %get-tuple-element.212.refs_0_, bf16[320,1664]{1,0:T(8,128)(2,1)} %copy-done.9, bf16[320,1664]{1,0:T(8,128)(2,1)} %collective-permute-done.41.refs_1_.refs_2_, bf16[320,1664]{1,0:T(8,128)(2,1)} %copy-done.18, ...), custom_call_target="tpu_custom_call" | custom-call | flops 1 | bytes 33000000 | tf_op jit(solution)/shard_map/feed_terms/pallas_call | solution.py:570
  487.6 8.0 %convolution_convert_fusion.2 = bf16[640,3200]{1,0:T(8,128)(2,1)S(1)} fusion(bf16[1024,3200]{1,0:T(8,128)(2,1)} %get-tuple-element.187.refs_0_, bf16[1024,2560]{1,0:T(8,128)(2,1)} %all-gather.9.cloned.1.call-done.left_ref), kind=kOutput, calls=%fused_computation.4 | convolution fusion | flops 4196352000 | bytes 11960320 | tf_op jit(solution)/shard_map/dot_general | solution.py:50
  495.7 9.2 %convolution_convert_fusion.3.own_ref = bf16[640,3200]{1,0:T(8,128)(2,1)} fusion(bf16[1024,3200]{1,0:T(8,128)(2,1)S(1)} %bitcast.53, bf16[1024,2560]{1,0:T(8,128)(2,1)} %all-gather.9.cloned.1.call-done.left_ref), kind=kOutput, calls=%fused_computation.5 | convolution fusion | flops 4196352000 | bytes 11960320 | tf_op jit(solution)/shard_map/dot_general | solution.py:50
  505.0 4.0 add_convert_fusion.4
  518.5 39.7 %collective-permute-done.67 = bf16[320,3200]{1,0:T(8,128)(2,1)S(1)} collective-permute-done((bf16[320,3200]{1,0:T(8,128)(2,1)}, bf16[320,3200]{1,0:T(8,128)(2,1)S(1)}, u32[]{:S(2)}, u32[]{:S(2)}) %collective-permute-start.67) | collective-permute-done | bytes 2048032 | tf_op jit(solution)/shard_map/ppermute | solution.py:777
  566.3 8.8 %convolution_convert_fusion.8.grad_ref = bf16[1024,640]{1,0:T(8,128)(2,1)} fusion(bf16[1024,2560]{1,0:T(8,128)(2,1)} %all-gather.11.cloned.1.call-done.upstream_ref, bf16[2560,640]{1,0:T(8,128)(2,1)} %get-tuple-element.156), kind=kOutput, calls=%fused_computation.36 | convolution fusion | flops 3356098560 | bytes 9830400 | tf_op jit(solution)/shard_map/dot_general | solution.py:46
  575.1 31.8 %attention_backward.1 = (bf16[1024,1280]{1,0:T(8,128)(2,1)}, bf16[1024,1280]{1,0:T(8,128)(2,1)}, f32[1024,128]{1,0:T(8,128)}) custom-call(bf16[1024,1280]{1,0:T(8,128)(2,1)} %get-tuple-element.193.q_ref, bf16[1024,1280]{1,0:T(8,128)(2,1)} %get-tuple-element.194.kv_ref, bf16[1024,640]{1,0:T(8,128)(2,1)} %convolution_convert_fusion.8.grad_ref, ...), custom_call_target="tpu_custom_call" | custom-call | flops 1 | bytes 93000000 | tf_op jit(solution)/shard_map/attention_backward/pallas_call | solution.py:249
  607.0 4.6 convolution_convert_fusion.7
  620.2 19.9 %head_sums.1 = bf16[2304,1280]{1,0:T(8,128)(2,1)} custom-call(s32[8]{0:T(128)} %compare_select_fusion.11.spots_ref.refs_0_, bf16[1024,1152]{1,0:T(8,128)(2,1)} %all-gather.5.cloned.1.call-done.xq_ref.lat_ref.latents_ref, bf16[1024,1280]{1,0:T(8,128)(2,1)} %get-tuple-element.208.query_ref, bf16[1024,1280]{1,0:T(8,128)(2,1)} %get-tuple-element.209.key_value_ref, ...), custom_call_target="tpu_custom_call" | custom-call | flops 1 | bytes 60000000 | tf_op jit(solution)/shard_map/head_sums/pallas_call | solution.py:690
  643.9 11.3 %feed_terms.7 = bf16[1024,2560]{1,0:T(8,128)(2,1)} custom-call(bf16[1024,1664]{1,0:T(8,128)(2,1)} %get-tuple-element.212.refs_0_, bf16[320,1664]{1,0:T(8,128)(2,1)} %constant_dynamic-update-slice_fusion.2.refs_4_.refs_1_, bf16[320,1664]{1,0:T(8,128)(2,1)} %copy-done.12, bf16[320,1664]{1,0:T(8,128)(2,1)} %copy-done.17, ...), custom_call_target="tpu_custom_call", output_to_operand_aliasing={{}: (5, {})} | custom-call | flops 1 | bytes 33000000 | tf_op jit(solution)/shard_map/feed_terms/pallas_call | solution.py:570
  657.4 5.8 collective-permute-done.72
  664.1 8.2 %latent_back.1 = (bf16[1280,1152]{1,0:T(8,128)(2,1)}, bf16[1280,1152]{1,0:T(8,128)(2,1)}, bf16[256,1152]{1,0:T(8,128)(2,1)}) custom-call(s32[4]{0:T(128)} %broadcast_xor_fusion.team_ref.refs_0_, bf16[256,1152]{1,0:T(8,128)(2,1)} %reduce-scatter.11.cloned.1.call-done.back_ref, f32[256,1152]{1,0:T(8,128)} %get-tuple-element.214.raw_ref, ...), custom_call_target="tpu_custom_call" | custom-call | flops 1 | bytes 24000000 | tf_op jit(solution)/shard_map/latent_back/pallas_call | solution.py:628
  678.0 7.9 token_back.1.in_ref
  685.9 3.5 add_convert_fusion
  708.3 5.1 reorder.6
  720.8 9.9 %collective-permute-done.85 = bf16[288,1280]{1,0:T(8,128)(2,1)S(1)} collective-permute-done((bf16[288,1280]{1,0:T(8,128)(2,1)}, bf16[288,1280]{1,0:T(8,128)(2,1)S(1)}, u32[]{:S(2)}, u32[]{:S(2)}) %collective-permute-start.85) | collective-permute-done | bytes 737312 | tf_op jit(solution)/shard_map/ppermute | solution.py:774
  738.8 13.8 %collective-permute-done.87 = bf16[288,1280]{1,0:T(8,128)(2,1)S(1)} collective-permute-done((bf16[288,1280]{1,0:T(8,128)(2,1)}, bf16[288,1280]{1,0:T(8,128)(2,1)S(1)}, u32[]{:S(2)}, u32[]{:S(2)}) %collective-permute-start.87) | collective-permute-done | bytes 737312 | tf_op jit(solution)/shard_map/ppermute | solution.py:774
  754.2 3.7 reorder.7
  761.9 6.5 unpaired.1
  778.6 4.0 collective-permute-done.89
  (491 shorter events, 231.2 us)
Async XLA Ops:
  7.3 147.7 %all-gather.5.cloned.1.call-start = ((), (), s32[]{:S(2)}) async-start(), calls=%async_computation.4 | async-start | bytes 2949120 | tf_op jit(solution)/shard_map/all_gather | solution.py:1058
  10.0 25.0 %collective-permute-start.11 = (bf16[288,1280]{1,0:T(8,128)(2,1)S(1)}, bf16[288,1280]{1,0:T(8,128)(2,1)S(1)}, u32[]{:S(2)}, u32[]{:S(2)}) collective-permute-start(bf16[288,1280]{1,0:T(8,128)(2,1)S(1)} %maximum_maximum_fusion.refs_1_), channel_id=1, source_target_pairs={{0,8},{8,16},{16,24},{24,28},{28,20},{20,12},{12,4},{4,0},{1,9},{9... | collective-permute-start | bytes 2211848 | tf_op jit(solution)/shard_map/ppermute | solution.py:774
  13.1 21.9 %collective-permute-start.12 = (bf16[288,1280]{1,0:T(8,128)(2,1)S(1)}, bf16[288,1280]{1,0:T(8,128)(2,1)S(1)}, u32[]{:S(2)}, u32[]{:S(2)}) collective-permute-start(bf16[288,1280]{1,0:T(8,128)(2,1)S(1)} %maximum_maximum_fusion.refs_1_), channel_id=1, source_target_pairs={{8,0},{16,8},{24,16},{28,24},{20,28},{12,20},{4,12},{0,4},{9,1},{1... | collective-permute-start | bytes 2211848 | tf_op jit(solution)/shard_map/ppermute | solution.py:777
  15.4 19.5 %collective-permute-start.3 = (bf16[80,1152]{1,0:T(8,128)(2,1)S(1)}, bf16[80,1152]{1,0:T(8,128)(2,1)S(1)}, u32[]{:S(2)}, u32[]{:S(2)}) collective-permute-start(bf16[80,1152]{1,0:T(8,128)(2,1)S(1)} %concatenate.65.refs_0_.refs_8_), channel_id=1, source_target_pairs={{8,0},{16,8},{24,16},{28,24},{20,28},{12,20},{4,12},{0,4},{9,1},{1... | collective-permute-start | bytes 552968 | tf_op jit(solution)/shard_map/ppermute | solution.py:777
  35.0 24.5 %collective-permute-start.21 = (bf16[288,1280]{1,0:T(8,128)(2,1)S(1)}, bf16[288,1280]{1,0:T(8,128)(2,1)}, u32[]{:S(2)}, u32[]{:S(2)}) collective-permute-start(bf16[288,1280]{1,0:T(8,128)(2,1)S(1)} %collective-permute-done.11.refs_8_), channel_id=1, source_target_pairs={{0,8},{8,16},{16,24},{24,28},{28,20},{20,12},{12,4},{4,0},{1,9},{9... | collective-permute-start | bytes 2211848 | tf_op jit(solution)/shard_map/ppermute | solution.py:774
  36.7 22.9 %collective-permute-start.22 = (bf16[288,1280]{1,0:T(8,128)(2,1)S(1)}, bf16[288,1280]{1,0:T(8,128)(2,1)}, u32[]{:S(2)}, u32[]{:S(2)}) collective-permute-start(bf16[288,1280]{1,0:T(8,128)(2,1)S(1)} %collective-permute-done.12.refs_2_), channel_id=1, source_target_pairs={{8,0},{16,8},{24,16},{28,24},{20,28},{12,20},{4,12},{0,4},{9,1},{1... | collective-permute-start | bytes 2211848 | tf_op jit(solution)/shard_map/ppermute | solution.py:777
  59.5 20.8 %collective-permute-start.31 = (bf16[288,1280]{1,0:T(8,128)(2,1)}, bf16[288,1280]{1,0:T(8,128)(2,1)}, u32[]{:S(2)}, u32[]{:S(2)}) collective-permute-start(bf16[288,1280]{1,0:T(8,128)(2,1)} %collective-permute-done.21.refs_7_), channel_id=1, source_target_pairs={{0,8},{8,16},{16,24},{24,28},{28,20},{20,12},{12,4},{4,0},{1,9},{9... | collective-permute-start | bytes 2211848 | tf_op jit(solution)/shard_map/ppermute | solution.py:774
  61.2 19.2 %collective-permute-start.32 = (bf16[288,1280]{1,0:T(8,128)(2,1)}, bf16[288,1280]{1,0:T(8,128)(2,1)}, u32[]{:S(2)}, u32[]{:S(2)}) collective-permute-start(bf16[288,1280]{1,0:T(8,128)(2,1)} %collective-permute-done.22.refs_3_), channel_id=1, source_target_pairs={{8,0},{16,8},{24,16},{28,24},{20,28},{12,20},{4,12},{0,4},{9,1},{1... | collective-permute-start | bytes 2211848 | tf_op jit(solution)/shard_map/ppermute | solution.py:777
  102.5 26.0 %collective-permute-start.40 = (bf16[320,1664]{1,0:T(8,128)(2,1)S(1)}, bf16[320,1664]{1,0:T(8,128)(2,1)}, u32[]{:S(2)}, u32[]{:S(2)}) collective-permute-start(bf16[320,1664]{1,0:T(8,128)(2,1)S(1)} %pad.18.refs_0_.refs_1_), channel_id=1, source_target_pairs={{0,8},{8,16},{16,24},{24,28},{28,20},{20,12},{12,4},{4,0},{1,9},{9... | collective-permute-start | bytes 3194888 | tf_op jit(solution)/shard_map/ppermute | solution.py:774
  103.3 25.7 %collective-permute-start.41 = (bf16[320,1664]{1,0:T(8,128)(2,1)S(1)}, bf16[320,1664]{1,0:T(8,128)(2,1)}, u32[]{:S(2)}, u32[]{:S(2)}) collective-permute-start(bf16[320,1664]{1,0:T(8,128)(2,1)S(1)} %pad.18.refs_0_.refs_1_), channel_id=1, source_target_pairs={{8,0},{16,8},{24,16},{28,24},{20,28},{12,20},{4,12},{0,4},{9,1},{1... | collective-permute-start | bytes 3194888 | tf_op jit(solution)/shard_map/ppermute | solution.py:777
  129.0 74.7 %all-gather.7.cloned.1.call-start = ((), (), s32[]{:S(2)}) async-start(), calls=%async_computation.5 | async-start | bytes 6553600 | tf_op jit(solution)/shard_map/all_gather | solution.py:1095
  129.0 25.0 %collective-permute-start.42 = (bf16[320,1664]{1,0:T(8,128)(2,1)}, bf16[320,1664]{1,0:T(8,128)(2,1)S(1)}, u32[]{:S(2)}, u32[]{:S(2)}) collective-permute-start(bf16[320,1664]{1,0:T(8,128)(2,1)} %collective-permute-done.40.refs_7_.refs_4_), channel_id=1, source_target_pairs={{0,8},{8,16},{16,24},{24,28},{28,20},{20,12},{12,4},{4,0},{1,9},{9... | collective-permute-start | bytes 3194888 | tf_op jit(solution)/shard_map/ppermute | solution.py:774
  129.7 25.2 %collective-permute-start.43 = (bf16[320,1664]{1,0:T(8,128)(2,1)}, bf16[320,1664]{1,0:T(8,128)(2,1)S(1)}, u32[]{:S(2)}, u32[]{:S(2)}) collective-permute-start(bf16[320,1664]{1,0:T(8,128)(2,1)} %collective-permute-done.41.refs_1_.refs_2_), channel_id=1, source_target_pairs={{8,0},{16,8},{24,16},{28,24},{20,28},{12,20},{4,12},{0,4},{9,1},{1... | collective-permute-start | bytes 3194888 | tf_op jit(solution)/shard_map/ppermute | solution.py:777
  155.0 100.6 %reduce-scatter.5.cloned.1.call-start = ((), (), s32[]{:S(2)}) async-start(), calls=%async_computation.6 | async-start | bytes 6553600 | tf_op jit(solution)/shard_map/reduce_scatter | solution.py:1102
  158.4 44.9 %collective-permute-start.44 = (bf16[320,3200]{1,0:T(8,128)(2,1)}, bf16[320,3200]{1,0:T(8,128)(2,1)}, u32[]{:S(2)}, u32[]{:S(2)}) collective-permute-start(bf16[320,3200]{1,0:T(8,128)(2,1)} %paired.1.refs_0_.refs_1_.weights_ref), channel_id=1, source_target_pairs={{0,8},{8,16},{16,24},{24,28},{28,20},{20,12},{12,4},{4,0},{1,9},{9... | collective-permute-start | bytes 6144008 | tf_op jit(solution)/shard_map/ppermute | solution.py:774
  159.0 44.7 %collective-permute-start.45 = (bf16[320,3200]{1,0:T(8,128)(2,1)}, bf16[320,3200]{1,0:T(8,128)(2,1)}, u32[]{:S(2)}, u32[]{:S(2)}) collective-permute-start(bf16[320,3200]{1,0:T(8,128)(2,1)} %paired.1.refs_0_.refs_1_.weights_ref), channel_id=1, source_target_pairs={{8,0},{16,8},{24,16},{28,24},{20,28},{12,20},{4,12},{0,4},{9,1},{1... | collective-permute-start | bytes 6144008 | tf_op jit(solution)/shard_map/ppermute | solution.py:777
  203.7 148.2 %all-gather.9.cloned.1.call-start = ((), (), s32[]{:S(2)}) async-start(), calls=%async_computation.7 | async-start | bytes 6553600 | tf_op jit(solution)/shard_map/all_gather | solution.py:1112
  203.8 26.7 %collective-permute-start.46 = (bf16[320,1664]{1,0:T(8,128)(2,1)}, bf16[320,1664]{1,0:T(8,128)(2,1)S(1)}, u32[]{:S(2)}, u32[]{:S(2)}) collective-permute-start(bf16[320,1664]{1,0:T(8,128)(2,1)} %copy-done.17), channel_id=1, source_target_pairs={{0,8},{8,16},{16,24},{24,28},{28,20},{20,12},{12,4},{4,0},{1,9},{9... | collective-permute-start | bytes 3194888 | tf_op jit(solution)/shard_map/ppermute | solution.py:774
  204.9 26.8 %collective-permute-start.47 = (bf16[320,1664]{1,0:T(8,128)(2,1)}, bf16[320,1664]{1,0:T(8,128)(2,1)}, u32[]{:S(2)}, u32[]{:S(2)}) collective-permute-start(bf16[320,1664]{1,0:T(8,128)(2,1)} %copy-done.18), channel_id=1, source_target_pairs={{8,0},{16,8},{24,16},{28,24},{20,28},{12,20},{4,12},{0,4},{9,1},{1... | collective-permute-start | bytes 3194888 | tf_op jit(solution)/shard_map/ppermute | solution.py:777
  205.9 64.8 %collective-permute-start.48 = (bf16[320,3200]{1,0:T(8,128)(2,1)}, bf16[320,3200]{1,0:T(8,128)(2,1)}, u32[]{:S(2)}, u32[]{:S(2)}) collective-permute-start(bf16[320,3200]{1,0:T(8,128)(2,1)} %collective-permute-done.44.refs_7_.refs_4_), channel_id=1, source_target_pairs={{0,8},{8,16},{16,24},{24,28},{28,20},{20,12},{12,4},{4,0},{1,9},{9... | collective-permute-start | bytes 6144008 | tf_op jit(solution)/shard_map/ppermute | solution.py:774
  206.9 64.7 %collective-permute-start.49 = (bf16[320,3200]{1,0:T(8,128)(2,1)}, bf16[320,3200]{1,0:T(8,128)(2,1)}, u32[]{:S(2)}, u32[]{:S(2)}) collective-permute-start(bf16[320,3200]{1,0:T(8,128)(2,1)} %collective-permute-done.45.refs_1_.refs_2_), channel_id=1, source_target_pairs={{8,0},{16,8},{24,16},{28,24},{20,28},{12,20},{4,12},{0,4},{9,1},{1... | collective-permute-start | bytes 6144008 | tf_op jit(solution)/shard_map/ppermute | solution.py:777
  271.6 239.1 %reduce-scatter.7.cloned.1.call-start = ((), (), s32[]{:S(2)}) async-start(), calls=%async_computation.8 | async-start | bytes 6553600 | tf_op jit(solution)/shard_map/reduce_scatter | solution.py:1137
  287.4 43.6 %collective-permute-start.52 = (bf16[320,3200]{1,0:T(8,128)(2,1)}, bf16[320,3200]{1,0:T(8,128)(2,1)S(1)}, u32[]{:S(2)}, u32[]{:S(2)}) collective-permute-start(bf16[320,3200]{1,0:T(8,128)(2,1)} %collective-permute-done.49.refs_2_.refs_3_), channel_id=1, source_target_pairs={{8,0},{16,8},{24,16},{28,24},{20,28},{12,20},{4,12},{0,4},{9,1},{1... | collective-permute-start | bytes 6144008 | tf_op jit(solution)/shard_map/ppermute | solution.py:777
  288.0 43.0 %collective-permute-start.53 = (bf16[320,3200]{1,0:T(8,128)(2,1)}, bf16[320,3200]{1,0:T(8,128)(2,1)S(1)}, u32[]{:S(2)}, u32[]{:S(2)}) collective-permute-start(bf16[320,3200]{1,0:T(8,128)(2,1)} %collective-permute-done.48.refs_6_.refs_3_), channel_id=1, source_target_pairs={{0,8},{8,16},{16,24},{24,28},{28,20},{20,12},{12,4},{4,0},{1,9},{9... | collective-permute-start | bytes 6144008 | tf_op jit(solution)/shard_map/ppermute | solution.py:774
  403.7 26.4 %collective-permute-start.58 = (bf16[160,3200]{1,0:T(8,128)(2,1)}, bf16[160,3200]{1,0:T(8,128)(2,1)}, u32[]{:S(2)}, u32[]{:S(2)}) collective-permute-start(bf16[160,3200]{1,0:T(8,128)(2,1)} %get-tuple-element.289), channel_id=1, source_target_pairs={{0,8},{8,16},{16,24},{24,28},{28,20},{20,12},{12,4},{4,0},{1,9},{9... | collective-permute-start | bytes 3072008 | tf_op jit(solution)/shard_map/ppermute | solution.py:774
  405.0 25.9 %collective-permute-start.59 = (bf16[160,3200]{1,0:T(8,128)(2,1)}, bf16[160,3200]{1,0:T(8,128)(2,1)}, u32[]{:S(2)}, u32[]{:S(2)}) collective-permute-start(bf16[160,3200]{1,0:T(8,128)(2,1)} %get-tuple-element.288), channel_id=1, source_target_pairs={{8,0},{16,8},{24,16},{28,24},{20,28},{12,20},{4,12},{0,4},{9,1},{1... | collective-permute-start | bytes 3072008 | tf_op jit(solution)/shard_map/ppermute | solution.py:777
  408.3 46.6 %collective-permute-start.61 = (bf16[320,1664]{1,0:T(8,128)(2,1)}, bf16[320,1664]{1,0:T(8,128)(2,1)}, u32[]{:S(2)}, u32[]{:S(2)}) collective-permute-start(bf16[320,1664]{1,0:T(8,128)(2,1)} %pad_maximum_fusion.4), channel_id=1, source_target_pairs={{8,0},{16,8},{24,16},{28,24},{20,28},{12,20},{4,12},{0,4},{9,1},{1... | collective-permute-start | bytes 3194888 | tf_op jit(solution)/shard_map/ppermute | solution.py:777
  410.1 44.8 %collective-permute-start.60 = (bf16[320,1664]{1,0:T(8,128)(2,1)}, bf16[320,1664]{1,0:T(8,128)(2,1)}, u32[]{:S(2)}, u32[]{:S(2)}) collective-permute-start(bf16[320,1664]{1,0:T(8,128)(2,1)} %pad_maximum_fusion.3), channel_id=1, source_target_pairs={{0,8},{8,16},{16,24},{24,28},{28,20},{20,12},{12,4},{4,0},{1,9},{9... | collective-permute-start | bytes 3194888 | tf_op jit(solution)/shard_map/ppermute | solution.py:774
  454.9 111.4 %all-gather.11.cloned.1.call-start = ((), (), s32[]{:S(2)}) async-start(), calls=%async_computation.9 | async-start | bytes 6553600 | tf_op jit(solution)/shard_map/all_gather | solution.py:1153
  455.0 50.0 %collective-permute-start.63 = (bf16[320,3200]{1,0:T(8,128)(2,1)}, bf16[320,3200]{1,0:T(8,128)(2,1)S(1)}, u32[]{:S(2)}, u32[]{:S(2)}) collective-permute-start(bf16[320,3200]{1,0:T(8,128)(2,1)} %pad_maximum_fusion.2), channel_id=1, source_target_pairs={{8,0},{16,8},{24,16},{28,24},{20,28},{12,20},{4,12},{0,4},{9,1},{1... | collective-permute-start | bytes 6144008 | tf_op jit(solution)/shard_map/ppermute | solution.py:777
  455.8 49.2 %collective-permute-start.62 = (bf16[320,3200]{1,0:T(8,128)(2,1)}, bf16[320,3200]{1,0:T(8,128)(2,1)}, u32[]{:S(2)}, u32[]{:S(2)}) collective-permute-start(bf16[320,3200]{1,0:T(8,128)(2,1)} %pad_maximum_fusion.1), channel_id=1, source_target_pairs={{0,8},{8,16},{16,24},{24,28},{28,20},{20,12},{12,4},{4,0},{1,9},{9... | collective-permute-start | bytes 6144008 | tf_op jit(solution)/shard_map/ppermute | solution.py:774
  466.1 50.2 %collective-permute-start.65 = (bf16[320,1664]{1,0:T(8,128)(2,1)}, bf16[320,1664]{1,0:T(8,128)(2,1)}, u32[]{:S(2)}, u32[]{:S(2)}) collective-permute-start(bf16[320,1664]{1,0:T(8,128)(2,1)} %add_convert_fusion.8), channel_id=1, source_target_pairs={{8,0},{16,8},{24,16},{28,24},{20,28},{12,20},{4,12},{0,4},{9,1},{1... | collective-permute-start | bytes 3194888 | tf_op jit(solution)/shard_map/ppermute | solution.py:777
  469.2 47.1 %collective-permute-start.64 = (bf16[320,1664]{1,0:T(8,128)(2,1)}, bf16[320,1664]{1,0:T(8,128)(2,1)}, u32[]{:S(2)}, u32[]{:S(2)}) collective-permute-start(bf16[320,1664]{1,0:T(8,128)(2,1)} %add_convert_fusion.9), channel_id=1, source_target_pairs={{0,8},{8,16},{16,24},{24,28},{28,20},{20,12},{12,4},{4,0},{1,9},{9... | collective-permute-start | bytes 3194888 | tf_op jit(solution)/shard_map/ppermute | solution.py:774
  516.3 147.7 %reduce-scatter.11.cloned.1.call-start = ((), (), s32[]{:S(2)}) async-start(), calls=%async_computation.11 | async-start | bytes 2949120 | tf_op jit(solution)/shard_map/reduce_scatter | solution.py:1172
  516.4 41.8 %collective-permute-start.67 = (bf16[320,3200]{1,0:T(8,128)(2,1)}, bf16[320,3200]{1,0:T(8,128)(2,1)S(1)}, u32[]{:S(2)}, u32[]{:S(2)}) collective-permute-start(bf16[320,3200]{1,0:T(8,128)(2,1)} %add_convert_fusion.3), channel_id=1, source_target_pairs={{8,0},{16,8},{24,16},{28,24},{20,28},{12,20},{4,12},{0,4},{9,1},{1... | collective-permute-start | bytes 6144008 | tf_op jit(solution)/shard_map/ppermute | solution.py:777
  516.8 42.4 %collective-permute-start.66 = (bf16[320,3200]{1,0:T(8,128)(2,1)}, bf16[320,3200]{1,0:T(8,128)(2,1)S(1)}, u32[]{:S(2)}, u32[]{:S(2)}) collective-permute-start(bf16[320,3200]{1,0:T(8,128)(2,1)} %add_convert_fusion.4), channel_id=1, source_target_pairs={{0,8},{8,16},{16,24},{24,28},{28,20},{20,12},{12,4},{4,0},{1,9},{9... | collective-permute-start | bytes 6144008 | tf_op jit(solution)/shard_map/ppermute | solution.py:774
  564.3 42.6 %collective-permute-start.69 = (bf16[320,3200]{1,0:T(8,128)(2,1)}, bf16[320,3200]{1,0:T(8,128)(2,1)S(1)}, u32[]{:S(2)}, u32[]{:S(2)}) collective-permute-start(bf16[320,3200]{1,0:T(8,128)(2,1)} %add_convert_fusion.1), channel_id=1, source_target_pairs={{8,0},{16,8},{24,16},{28,24},{20,28},{12,20},{4,12},{0,4},{9,1},{1... | collective-permute-start | bytes 6144008 | tf_op jit(solution)/shard_map/ppermute | solution.py:777
  565.2 41.8 %collective-permute-start.68 = (bf16[320,3200]{1,0:T(8,128)(2,1)}, bf16[320,3200]{1,0:T(8,128)(2,1)}, u32[]{:S(2)}, u32[]{:S(2)}) collective-permute-start(bf16[320,3200]{1,0:T(8,128)(2,1)} %add_convert_fusion.2), channel_id=1, source_target_pairs={{0,8},{8,16},{16,24},{24,28},{28,20},{20,12},{12,4},{4,0},{1,9},{9... | collective-permute-start | bytes 6144008 | tf_op jit(solution)/shard_map/ppermute | solution.py:774
  614.4 121.3 %reduce-scatter.9.cloned.1.call-start = ((), (), s32[]{:S(2)}) async-start(), calls=%async_computation.10 | async-start | bytes 6553600 | tf_op jit(solution)/shard_map/reduce_scatter | solution.py:1199
  618.1 22.0 %collective-permute-start.71 = (bf16[320,1664]{1,0:T(8,128)(2,1)S(1)}, bf16[320,1664]{1,0:T(8,128)(2,1)S(1)}, u32[]{:S(2)}, u32[]{:S(2)}) collective-permute-start(bf16[320,1664]{1,0:T(8,128)(2,1)S(1)} %add_convert_fusion.6), channel_id=1, source_target_pairs={{8,0},{16,8},{24,16},{28,24},{20,28},{12,20},{4,12},{0,4},{9,1},{1... | collective-permute-start | bytes 3194888 | tf_op jit(solution)/shard_map/ppermute | solution.py:777
  619.4 20.7 %collective-permute-start.70 = (bf16[320,1664]{1,0:T(8,128)(2,1)S(1)}, bf16[320,1664]{1,0:T(8,128)(2,1)S(1)}, u32[]{:S(2)}, u32[]{:S(2)}) collective-permute-start(bf16[320,1664]{1,0:T(8,128)(2,1)S(1)} %add_convert_fusion.7), channel_id=1, source_target_pairs={{0,8},{8,16},{16,24},{24,28},{28,20},{20,12},{12,4},{4,0},{1,9},{9... | collective-permute-start | bytes 3194888 | tf_op jit(solution)/shard_map/ppermute | solution.py:774
  674.9 19.5 %collective-permute-start.84 = (bf16[288,1280]{1,0:T(8,128)(2,1)}, bf16[288,1280]{1,0:T(8,128)(2,1)S(1)}, u32[]{:S(2)}, u32[]{:S(2)}) collective-permute-start(bf16[288,1280]{1,0:T(8,128)(2,1)} %pad_maximum_fusion.7), channel_id=1, source_target_pairs={{8,0},{16,8},{24,16},{28,24},{20,28},{12,20},{4,12},{0,4},{9,1},{1... | collective-permute-start | bytes 2211848 | tf_op jit(solution)/shard_map/ppermute | solution.py:777
  677.2 19.7 %collective-permute-start.83 = (bf16[288,1280]{1,0:T(8,128)(2,1)}, bf16[288,1280]{1,0:T(8,128)(2,1)S(1)}, u32[]{:S(2)}, u32[]{:S(2)}) collective-permute-start(bf16[288,1280]{1,0:T(8,128)(2,1)} %pad_maximum_fusion.6), channel_id=1, source_target_pairs={{0,8},{8,16},{16,24},{24,28},{28,20},{20,12},{12,4},{4,0},{1,9},{9... | collective-permute-start | bytes 2211848 | tf_op jit(solution)/shard_map/ppermute | solution.py:774
  706.3 24.4 %collective-permute-start.85 = (bf16[288,1280]{1,0:T(8,128)(2,1)}, bf16[288,1280]{1,0:T(8,128)(2,1)S(1)}, u32[]{:S(2)}, u32[]{:S(2)}) collective-permute-start(bf16[288,1280]{1,0:T(8,128)(2,1)} %get-tuple-element.295), channel_id=1, source_target_pairs={{0,8},{8,16},{16,24},{24,28},{28,20},{20,12},{12,4},{4,0},{1,9},{9... | collective-permute-start | bytes 2211848 | tf_op jit(solution)/shard_map/ppermute | solution.py:774
  706.9 23.8 %collective-permute-start.86 = (bf16[288,1280]{1,0:T(8,128)(2,1)S(1)}, bf16[288,1280]{1,0:T(8,128)(2,1)}, u32[]{:S(2)}, u32[]{:S(2)}) collective-permute-start(bf16[288,1280]{1,0:T(8,128)(2,1)S(1)} %get-tuple-element.294), channel_id=1, source_target_pairs={{8,0},{16,8},{24,16},{28,24},{20,28},{12,20},{4,12},{0,4},{9,1},{1... | collective-permute-start | bytes 2211848 | tf_op jit(solution)/shard_map/ppermute | solution.py:777
  717.1 40.8 %collective-permute-start.79 = (bf16[160,1152]{1,0:T(8,128)(2,1)}, bf16[160,1152]{1,0:T(8,128)(2,1)}, u32[]{:S(2)}, u32[]{:S(2)}) collective-permute-start(bf16[160,1152]{1,0:T(8,128)(2,1)} %get-tuple-element.311), channel_id=1, source_target_pairs={{0,8},{8,16},{16,24},{24,28},{28,20},{20,12},{12,4},{4,0},{1,9},{9... | collective-permute-start | bytes 1105928 | tf_op jit(solution)/shard_map/ppermute | solution.py:774
  717.7 40.2 %collective-permute-start.80 = (bf16[160,1152]{1,0:T(8,128)(2,1)}, bf16[160,1152]{1,0:T(8,128)(2,1)}, u32[]{:S(2)}, u32[]{:S(2)}) collective-permute-start(bf16[160,1152]{1,0:T(8,128)(2,1)} %get-tuple-element.310), channel_id=1, source_target_pairs={{8,0},{16,8},{24,16},{28,24},{20,28},{12,20},{4,12},{0,4},{9,1},{1... | collective-permute-start | bytes 1105928 | tf_op jit(solution)/shard_map/ppermute | solution.py:777
  733.7 18.9 %collective-permute-start.87 = (bf16[288,1280]{1,0:T(8,128)(2,1)}, bf16[288,1280]{1,0:T(8,128)(2,1)S(1)}, u32[]{:S(2)}, u32[]{:S(2)}) collective-permute-start(bf16[288,1280]{1,0:T(8,128)(2,1)} %get-tuple-element.293), channel_id=1, source_target_pairs={{0,8},{8,16},{16,24},{24,28},{28,20},{20,12},{12,4},{4,0},{1,9},{9... | collective-permute-start | bytes 2211848 | tf_op jit(solution)/shard_map/ppermute | solution.py:774
  (138 other events, 1952.7 us)
Sparse Core Ops, SparseCore 0:
  129.1 22.6 all-gather.4
  155.1 39.8 all-gather.6
  203.9 51.6 reduce-scatter.4
  271.7 40.0 all-gather.8
  455.1 49.7 reduce-scatter.6
  516.4 40.0 all-gather.10
  614.5 32.4 reduce-scatter.10
  655.4 51.1 reduce-scatter.8

commit v5 on v4

--- a/solution.py
+++ b/solution.py
@@ -1192,10 +1192,11 @@
         )
     grad_mixed = stacked(ring, follow(mixed_sums, ends(grad_down)))
     grad_mixed.advance()
+    grad_mixed.advance()
     if len(downs) > half:
         activated = follow(activated, grad_mixed.sent)
         feed_branch = feed_terms(activated, downs[half:], width, 1, feed_branch, lasting(11))
-    latent_grad = follow(latent_grad, ends(grad_mixed), feed_branch)
+    latent_grad = follow(latent_grad, feed_branch, ends(grad_mixed))
     feed_branch = lax.psum_scatter(feed_branch, "tensor", scatter_dimension=0, tiled=True)
     pair = 2 * down_rows
     height = ring.count * pair
@@ -1222,11 +1223,11 @@
         return (a.astype(jnp.float32) + b.astype(jnp.float32)).astype(low)
 
     other_sums = swap(sent[1], 1)
+    token_grad = token_back(
+        latent_low, down_projections, tokens_ring, hidden_grad, gain_in
+    )
     hold(grad_mixed, latent_low)
     grad_mixed.advance()
-    token_grad = token_back(
-        latent_low, down_projections, tokens_ring, hidden_grad, gain_in
-    )
     other_sums = follow(other_sums, token_grad)
     grad_small = stacked(ring, add_low(sent[0], other_sums))
     grad_small.advance()
@@ -1234,45 +1235,43 @@
     grad_mixed.advance()
     grad_small.advance()
     token_grad = reorder(follow(token_grad, grad_small.sent), ring.behind)
-    hold(grad_mixed, grad_small.sent)
     hold(grad_down, ends(grad_small))
     hold(grad_small, token_grad)
+    grad_small.advance()
+    while not grad_pair.done:
+        grad_pair.advance()
+    hold(grad_pair, grad_small.sent)
+    grad_gate_own, grad_up_own, pair_sums = unpaired(
+        grad_pair.parts[0], grad_pair.low, grad_pair.high, pair_own, feed_width
+    )
+    hold(grad_small, pair_sums)
     grad_small.advance()
     feed_branch = follow(feed_branch, grad_small.sent)
     output = hidden + RESIDUAL * feed_branch.astype(jnp.float32)
     output = reorder(output.astype(low), ring.behind)
-    grad_mixed.advance()
-    hold(grad_small, output)
-    grad_small.advance()
-    hold(grad_pair, grad_small.sent)
+    grad_mixed_own = grad_mixed.finish()
+    row_sums = lambda weights, grads: jnp.sum(weights.astype(jnp.float32) * grads, axis=1)
+    head_rows = query_rows + latent_rows
+    gain_sums = jnp.concatenate(
+        [pair_sums[:, 0], row_sums(mixed[:head_rows], grad_mixed_own[:head_rows])]
+    )
+    gain_sums = jnp.pad(gain_sums, (0, -gain_sums.shape[0] % LANES))[None]
+    gain_sums = gain_sums + swap(gain_sums, 1)
+    gain_sums = (gain_sums + swap(gain_sums, 2))[0]
+    hold(grad_small, output, gain_sums)
     small_own = grad_small.finish()
-    small_other = follow(small_own[down_rows:].astype(low), ends(grad_mixed))
+    small_other = small_own[down_rows:].astype(low)
     packed_own = small_own[:down_rows] + swap(small_other, 2).astype(jnp.float32)
     rope_from = rank + KVR + NOPE
     lanes = jnp.arange(down_width) < rope_from + ROPE
     grad_gain_input = jnp.sum(
         jnp.where(lanes, packed.astype(jnp.float32) * packed_own, 0.0), axis=1
     ) / norm_input.astype(jnp.float32)
-    grad_mixed_own = grad_mixed.finish()
-    while not grad_pair.done:
-        grad_pair.advance()
     grad_query_own = grad_mixed_own[:query_rows].reshape(query_rows, local_heads, LANES)
     grad_out_own = grad_mixed_own[query_rows + latent_rows :]
     grad_out_own = jnp.concatenate(
         [grad_out_own[:, :out_width], grad_out_own[:, out_width:]], axis=0
     )
-    grad_gate_own, grad_up_own, pair_sums = unpaired(
-        grad_pair.parts[0], grad_pair.low, grad_pair.high, pair_own, feed_width
-    )
-    row_sums = lambda weights, grads: jnp.sum(weights.astype(jnp.float32) * grads, axis=1)
-    head_rows = query_rows + latent_rows
-    gain_sums = jnp.concatenate(
-        [pair_sums[:, 0], row_sums(mixed[:head_rows], grad_mixed_own[:head_rows])]
-    )
-    gain_sums = jnp.pad(gain_sums, (0, -gain_sums.shape[0] % LANES))[None]
-    gain_sums = follow(gain_sums, small_other)
-    gain_sums = gain_sums + swap(gain_sums, 1)
-    gain_sums = (gain_sums + swap(gain_sums, 2))[0]
     gain_grads = []
     start = 0
     for gain in (norm_hidden, norm_query, norm_latent):

time: 801 us -> 786 us (0.981)
  waiting for transfers between devices: 271 us -> 253 us
    ppermute x32, waiting for transfers between devices: 115 us -> 91.5 us  [send_up(): return lax.ppermute(block, self.axis, self.up)]
  transfers between devices with their start and end apart: 100 -> 100, of which waited for: 43 -> 46; matrix products, arithmetic and copies ran while one was open for 19% -> 20% of each run, Pallas kernels for 27% -> 27%
where the time goes in v5:
time: 786 us; the launch traced here: 776 us
  waiting for transfers between devices  253 us (32%)
  Pallas kernels  237 us (30%)
  starting transfers between devices  86.2 us (11%)
  other arithmetic  82.8 us (11%)
  matrix products  67.4 us (9%)
  local copies, waits for them, and re-layouts  33.3 us (4%)
  between operations  15.8 us (2%)
    ppermute x32, waiting for transfers between devices, send_down(): return lax.ppermute(block, self.axis, self.down)  120 us
    ppermute x32, waiting for transfers between devices, send_up(): return lax.ppermute(block, self.axis, self.up)  91.5 us
    pallas_call x4, Pallas kernels, feed_terms(): pl.pallas_call(functools.partial(terms_kernel, len(pieces)), grid=(1,), i...  59.5 us
    ppermute x32, starting transfers between devices, send_up(): return lax.ppermute(block, self.axis, self.up)  46.2 us
    dot_general x6, matrix products, product_left(): lax.dot_general(left, right, (((0,), (0,)), ((), ())), preferred_element_...  45.7 us
    convert_element_type x16, other arithmetic, add(): return (a.astype(jnp.float32) + b.astype(jnp.float32)).astype(b.dtype)  36 us
    pallas_call x1, Pallas kernels, attention_backward(): pl.pallas_call(backward_kernel, grid=(pairs,), in_specs=[mine(2 * LANES),...  31.8 us
    pallas_call x1, Pallas kernels, feed_gate(): pl.pallas_call(functools.partial(gate_kernel, len(pieces), pair_width //...  26.3 us
  transfers between devices with their start and end apart: 100, of which 46 were waited for; matrix products, arithmetic and copies ran while one was open for 20% of the time, Pallas kernels for 27%

profile of v5, /device:TPU:0, one launch (start us, length us, event | category | flops | bytes accessed | tf_op | source)
XLA Modules:
  0.0 775.8 jit_solution(11616110321265336868)
XLA Ops:
  21.3 13.6 %collective-permute-done.3.refs_4_.refs_12_ = bf16[80,1152]{1,0:T(8,128)(2,1)S(1)} collective-permute-done((bf16[80,1152]{1,0:T(8,128)(2,1)S(1)}, bf16[80,1152]{1,0:T(8,128)(2,1)S(1)}, u32[]{:S(2)}, u32[]{:S(2)}) %collective-permute-start.3) | collective-permute-done | bytes 184352 | tf_op jit(solution)/shard_map/ppermute | solution.py:777
  39.1 4.6 collective-permute-done.8.refs_9_.refs_17_
  48.7 8.8 %collective-permute-done.13.refs_12_.refs_20_ = bf16[80,1152]{1,0:T(8,128)(2,1)} collective-permute-done((bf16[80,1152]{1,0:T(8,128)(2,1)S(1)}, bf16[80,1152]{1,0:T(8,128)(2,1)}, u32[]{:S(2)}, u32[]{:S(2)}) %collective-permute-start.13) | collective-permute-done | bytes 184352 | tf_op jit(solution)/shard_map/ppermute | solution.py:777
  73.2 7.2 collective-permute-done.23.refs_20_.refs_28_
  88.3 3.5 collective-permute-done.34
  98.2 3.6 collective-permute-done.39
  105.1 3.7 reorder.4.refs_1_.tokens_ref
  118.1 10.0 %project.1 = (bf16[256,1152]{1,0:T(8,128)(2,1)}, f32[256,1152]{1,0:T(8,128)}, bf16[256,2560]{1,0:T(8,128)(2,1)}, bf16[2560,1152]{1,0:T(8,128)(2,1)}) custom-call(s32[4]{0:T(128)} %broadcast_xor_fusion.team_ref.refs_0_, bf16[256,2560]{1,0:T(8,128)(2,1)} %reorder.4.refs_1_.tokens_ref, f32[1,2560]{1,0:T(1,128)} %reshape.321.refs_2_.gain_ref, ...), custom_call_target="tpu_custom_call" | custom-call | flops 1 | bytes 30000000 | tf_op jit(solution)/shard_map/project/pallas_call | solution.py:383
  131.6 3.7 reorder.5
  138.1 16.0 %collective-permute-done.42.refs_6_.refs_3_ = bf16[320,1664]{1,0:T(8,128)(2,1)S(1)} collective-permute-done((bf16[320,1664]{1,0:T(8,128)(2,1)}, bf16[320,1664]{1,0:T(8,128)(2,1)S(1)}, u32[]{:S(2)}, u32[]{:S(2)}) %collective-permute-start.42) | collective-permute-done | bytes 1064992 | tf_op jit(solution)/shard_map/ppermute | solution.py:774
  163.4 6.4 assemble.1
  171.8 23.4 %attention_forward.1 = (bf16[1024,640]{1,0:T(8,128)(2,1)}, bf16[1024,1280]{1,0:T(8,128)(2,1)}, bf16[1024,1280]{1,0:T(8,128)(2,1)}, f32[5,2,1024]{2,1,0:T(2,128)}) custom-call(bf16[1024,1152]{1,0:T(8,128)(2,1)} %all-gather.5.cloned.1.call-done.xq_ref.lat_ref.latents_ref, bf16[1024,1152]{1,0:T(8,128)(2,1)} %all-gather.5.cloned.1.call-done.xq_ref.lat_ref.latents_ref, ...), custom_call_target="tpu_custom_call" | custom-call | flops 1 | bytes 69000000 | tf_op jit(solution)/shard_map/attention_forward/pallas_call | solution.py:148
  195.1 7.4 convolution_convert_fusion.4
  207.9 22.5 %collective-permute-done.46.refs_5_.refs_2_ = bf16[320,1664]{1,0:T(8,128)(2,1)S(1)} collective-permute-done((bf16[320,1664]{1,0:T(8,128)(2,1)}, bf16[320,1664]{1,0:T(8,128)(2,1)S(1)}, u32[]{:S(2)}, u32[]{:S(2)}) %collective-permute-start.46) | collective-permute-done | bytes 1064992 | tf_op jit(solution)/shard_map/ppermute | solution.py:774
  231.6 23.9 %reduce-scatter.5.cloned.1.call-done = bf16[256,2560]{1,0:T(8,128)(2,1)} async-done(((bf16[1024,2560]{1,0:T(8,128)(2,1)}), bf16[256,2560]{1,0:T(8,128)(2,1)}) %reduce-scatter.5.cloned.1.call-update) | async-done | bytes 1310736 | tf_op jit(solution)/shard_map/reduce_scatter | solution.py:1102
  259.2 11.5 %collective-permute-done.48.refs_6_.refs_3_ = bf16[320,3200]{1,0:T(8,128)(2,1)} collective-permute-done((bf16[320,3200]{1,0:T(8,128)(2,1)}, bf16[320,3200]{1,0:T(8,128)(2,1)}, u32[]{:S(2)}, u32[]{:S(2)}) %collective-permute-start.48) | collective-permute-done | bytes 2048032 | tf_op jit(solution)/shard_map/ppermute | solution.py:774
  276.0 7.1 collective-permute-done.50
  283.0 4.4 collective-permute-done.51
  291.1 15.2 %feed_product.1.refs_8_ = f32[1024,1664]{1,0:T(8,128)} custom-call(bf16[1024,2560]{1,0:T(8,128)(2,1)} %all-gather.7.cloned.1.call-done.left_ref, bf16[320,1664]{1,0:T(8,128)(2,1)} %copy-done.9, bf16[320,1664]{1,0:T(8,128)(2,1)} %collective-permute-done.41.refs_1_.refs_2_, bf16[320,1664]{1,0:T(8,128)(2,1)} %copy-done.18, ...), custom_call_target="tpu_custom_call" | custom-call | flops 1 | bytes 45000000 | tf_op jit(solution)/shard_map/feed_product/pallas_call | solution.py:511
  306.4 24.7 %collective-permute-done.52.refs_3_.refs_4_ = bf16[320,3200]{1,0:T(8,128)(2,1)S(1)} collective-permute-done((bf16[320,3200]{1,0:T(8,128)(2,1)}, bf16[320,3200]{1,0:T(8,128)(2,1)S(1)}, u32[]{:S(2)}, u32[]{:S(2)}) %collective-permute-start.52) | collective-permute-done | bytes 2048032 | tf_op jit(solution)/shard_map/ppermute | solution.py:777
  333.7 15.6 %collective-permute-done.54 = bf16[160,3200]{1,0:T(8,128)(2,1)S(1)} collective-permute-done((bf16[160,3200]{1,0:T(8,128)(2,1)S(1)}, bf16[160,3200]{1,0:T(8,128)(2,1)S(1)}, u32[]{:S(2)}, u32[]{:S(2)}) %collective-permute-start.54) | collective-permute-done | bytes 1024032 | tf_op jit(solution)/shard_map/ppermute | solution.py:774
  352.1 26.3 %feed_gate.1 = (bf16[1024,1664]{1,0:T(8,128)(2,1)}, bf16[1024,3200]{1,0:T(8,128)(2,1)}) custom-call(bf16[1024,2560]{1,0:T(8,128)(2,1)} %all-gather.9.cloned.1.call-done.left_ref, bf16[320,3200]{1,0:T(8,128)(2,1)} %paired.1.refs_0_.refs_1_.weights_ref, bf16[320,3200]{1,0:T(8,128)(2,1)} %collective-permute-done.45.refs_1_.refs_2_, ...), custom_call_target="tpu_custom_call" | custom-call | flops 1 | bytes 78000000 | tf_op jit(solution)/shard_map/feed_gate/pallas_call | solution.py:527
  378.4 7.9 %convolution_convert_fusion.1 = bf16[1280,1664]{1,0:T(8,128)(2,1)S(1)} fusion(bf16[1024,1664]{1,0:T(8,128)(2,1)} %get-tuple-element.212.refs_0_, bf16[1024,2560]{1,0:T(8,128)(2,1)} %all-gather.7.cloned.1.call-done.left_ref), kind=kOutput, calls=%fused_computation.3 | convolution fusion | flops 4364206080 | bytes 10289152 | tf_op jit(solution)/shard_map/dot_general | solution.py:50
  390.3 9.6 %convolution_convert_fusion = bf16[1280,3200]{1,0:T(8,128)(2,1)S(1)} fusion(bf16[1024,3200]{1,0:T(8,128)(2,1)S(1)} %copy-done.3, bf16[1024,2560]{1,0:T(8,128)(2,1)S(1)} %bitcast.55), kind=kOutput, calls=%fused_computation.2 | convolution fusion | flops 8392704000 | bytes 17367040 | tf_op jit(solution)/shard_map/dot_general | solution.py:50
  411.9 18.4 %feed_terms.4.refs_5_ = bf16[1024,2560]{1,0:T(8,128)(2,1)} custom-call(bf16[1024,3200]{1,0:T(8,128)(2,1)} %get-tuple-element.185.refs_0_, bf16[320,3200]{1,0:T(8,128)(2,1)} %paired.1.refs_0_.refs_1_.weights_ref, bf16[320,3200]{1,0:T(8,128)(2,1)} %collective-permute-done.45.refs_1_.refs_2_, bf16[320,3200]{1,0:T(8,128)(2,1)} %collective-permute-done.49.refs_2_.refs_3_, ...), custom_call_target="tpu_custom_call" | custom-call | flops 1 | bytes 54000000 | tf_op jit(solution)/shard_map/feed_terms/pallas_call | solution.py:570
  436.5 18.5 %feed_terms.5 = bf16[1024,2560]{1,0:T(8,128)(2,1)} custom-call(bf16[1024,3200]{1,0:T(8,128)(2,1)} %get-tuple-element.185.refs_0_, bf16[320,3200]{1,0:T(8,128)(2,1)} %constant_dynamic-update-slice_fusion.4.refs_4_.refs_1_, bf16[320,3200]{1,0:T(8,128)(2,1)} %copy-done.5, ...), custom_call_target="tpu_custom_call", output_to_operand_aliasing={{}: (5, {})} | custom-call | flops 1 | bytes 54000000 | tf_op jit(solution)/shard_map/feed_terms/pallas_call | solution.py:570
  457.2 5.7 convolution_convert_fusion.6
  471.2 5.3 convolution_convert_fusion.5
  476.5 11.4 %feed_terms.6.refs_5_ = bf16[1024,2560]{1,0:T(8,128)(2,1)} custom-call(bf16[1024,1664]{1,0:T(8,128)(2,1)} %get-tuple-element.212.refs_0_, bf16[320,1664]{1,0:T(8,128)(2,1)} %copy-done.9, bf16[320,1664]{1,0:T(8,128)(2,1)} %collective-permute-done.41.refs_1_.refs_2_, bf16[320,1664]{1,0:T(8,128)(2,1)} %copy-done.18, ...), custom_call_target="tpu_custom_call" | custom-call | flops 1 | bytes 33000000 | tf_op jit(solution)/shard_map/feed_terms/pallas_call | solution.py:570
  487.9 8.1 %convolution_convert_fusion.2 = bf16[640,3200]{1,0:T(8,128)(2,1)S(1)} fusion(bf16[1024,3200]{1,0:T(8,128)(2,1)} %get-tuple-element.185.refs_0_, bf16[1024,2560]{1,0:T(8,128)(2,1)} %all-gather.9.cloned.1.call-done.left_ref), kind=kOutput, calls=%fused_computation.4 | convolution fusion | flops 4196352000 | bytes 11960320 | tf_op jit(solution)/shard_map/dot_general | solution.py:50
  496.1 9.1 %convolution_convert_fusion.3.own_ref = bf16[640,3200]{1,0:T(8,128)(2,1)} fusion(bf16[1024,3200]{1,0:T(8,128)(2,1)S(1)} %bitcast.53, bf16[1024,2560]{1,0:T(8,128)(2,1)} %all-gather.9.cloned.1.call-done.left_ref), kind=kOutput, calls=%fused_computation.5 | convolution fusion | flops 4196352000 | bytes 11960320 | tf_op jit(solution)/shard_map/dot_general | solution.py:50
  505.2 4.0 add_convert_fusion.4
  518.7 39.9 %collective-permute-done.67 = bf16[320,3200]{1,0:T(8,128)(2,1)S(1)} collective-permute-done((bf16[320,3200]{1,0:T(8,128)(2,1)}, bf16[320,3200]{1,0:T(8,128)(2,1)S(1)}, u32[]{:S(2)}, u32[]{:S(2)}) %collective-permute-start.67) | collective-permute-done | bytes 2048032 | tf_op jit(solution)/shard_map/ppermute | solution.py:777
  566.5 8.8 %convolution_convert_fusion.8.grad_ref = bf16[1024,640]{1,0:T(8,128)(2,1)} fusion(bf16[1024,2560]{1,0:T(8,128)(2,1)} %all-gather.11.cloned.1.call-done.upstream_ref, bf16[2560,640]{1,0:T(8,128)(2,1)} %get-tuple-element.154), kind=kOutput, calls=%fused_computation.36 | convolution fusion | flops 3356098560 | bytes 9830400 | tf_op jit(solution)/shard_map/dot_general | solution.py:46
  575.2 31.8 %attention_backward.1 = (bf16[1024,1280]{1,0:T(8,128)(2,1)}, bf16[1024,1280]{1,0:T(8,128)(2,1)}, f32[1024,128]{1,0:T(8,128)}) custom-call(bf16[1024,1280]{1,0:T(8,128)(2,1)} %get-tuple-element.191.q_ref, bf16[1024,1280]{1,0:T(8,128)(2,1)} %get-tuple-element.192.kv_ref, bf16[1024,640]{1,0:T(8,128)(2,1)} %convolution_convert_fusion.8.grad_ref, ...), custom_call_target="tpu_custom_call" | custom-call | flops 1 | bytes 93000000 | tf_op jit(solution)/shard_map/attention_backward/pallas_call | solution.py:249
  607.1 4.7 convolution_convert_fusion.7
  620.3 19.8 %head_sums.1 = bf16[2304,1280]{1,0:T(8,128)(2,1)} custom-call(s32[8]{0:T(128)} %compare_select_fusion.11.spots_ref.refs_0_, bf16[1024,1152]{1,0:T(8,128)(2,1)} %all-gather.5.cloned.1.call-done.xq_ref.lat_ref.latents_ref, bf16[1024,1280]{1,0:T(8,128)(2,1)} %get-tuple-element.206.query_ref, bf16[1024,1280]{1,0:T(8,128)(2,1)} %get-tuple-element.207.key_value_ref, ...), custom_call_target="tpu_custom_call" | custom-call | flops 1 | bytes 60000000 | tf_op jit(solution)/shard_map/head_sums/pallas_call | solution.py:690
  644.4 5.5 collective-permute-done.72
  649.9 3.9 collective-permute-done.73
  659.6 11.2 %feed_terms.7 = bf16[1024,2560]{1,0:T(8,128)(2,1)} custom-call(bf16[1024,1664]{1,0:T(8,128)(2,1)} %get-tuple-element.212.refs_0_, bf16[320,1664]{1,0:T(8,128)(2,1)} %constant_dynamic-update-slice_fusion.2.refs_4_.refs_1_, bf16[320,1664]{1,0:T(8,128)(2,1)} %copy-done.12, bf16[320,1664]{1,0:T(8,128)(2,1)} %copy-done.17, ...), custom_call_target="tpu_custom_call", output_to_operand_aliasing={{}: (5, {})} | custom-call | flops 1 | bytes 33000000 | tf_op jit(solution)/shard_map/feed_terms/pallas_call | solution.py:570
  670.9 8.1 %latent_back.1 = (bf16[1280,1152]{1,0:T(8,128)(2,1)}, bf16[1280,1152]{1,0:T(8,128)(2,1)}, bf16[256,1152]{1,0:T(8,128)(2,1)}) custom-call(s32[4]{0:T(128)} %broadcast_xor_fusion.team_ref.refs_0_, bf16[256,1152]{1,0:T(8,128)(2,1)} %reduce-scatter.11.cloned.1.call-done.back_ref, f32[256,1152]{1,0:T(8,128)} %get-tuple-element.214.raw_ref, ...), custom_call_target="tpu_custom_call" | custom-call | flops 1 | bytes 24000000 | tf_op jit(solution)/shard_map/latent_back/pallas_call | solution.py:628
  679.1 3.9 add_convert_fusion.14
  685.2 7.9 %token_back.1.in_ref = f32[256,2560]{1,0:T(8,128)} custom-call(bf16[256,1152]{1,0:T(8,128)(2,1)} %get-tuple-element.218.grad_ref, bf16[2560,1152]{1,0:T(8,128)(2,1)} %get-tuple-element.219.weights_ref, bf16[256,2560]{1,0:T(8,128)(2,1)} %reorder.4.refs_1_.tokens_ref, f32[256,2560]{1,0:T(8,128)} %get-tuple-element.281.hidden_ref, ...), custom_call_target="tpu_custom_call" | custom-call | flops 1 | bytes 24000000 | tf_op jit(solution)/shard_map/token_back/pallas_call | solution.py:716
  693.1 4.1 add_convert_fusion
  714.7 5.0 reorder.6
  725.0 6.7 unpaired.1
  754.1 3.7 reorder.7
  763.0 3.6 collective-permute-done.85
  (487 shorter events, 230.9 us)
Async XLA Ops:
  7.3 147.6 %all-gather.5.cloned.1.call-start = ((), (), s32[]{:S(2)}) async-start(), calls=%async_computation.4 | async-start | bytes 2949120 | tf_op jit(solution)/shard_map/all_gather | solution.py:1058
  10.0 25.0 %collective-permute-start.11 = (bf16[288,1280]{1,0:T(8,128)(2,1)S(1)}, bf16[288,1280]{1,0:T(8,128)(2,1)S(1)}, u32[]{:S(2)}, u32[]{:S(2)}) collective-permute-start(bf16[288,1280]{1,0:T(8,128)(2,1)S(1)} %maximum_maximum_fusion.refs_1_), channel_id=1, source_target_pairs={{0,8},{8,16},{16,24},{24,28},{28,20},{20,12},{12,4},{4,0},{1,9},{9... | collective-permute-start | bytes 2211848 | tf_op jit(solution)/shard_map/ppermute | solution.py:774
  13.1 21.9 %collective-permute-start.12 = (bf16[288,1280]{1,0:T(8,128)(2,1)S(1)}, bf16[288,1280]{1,0:T(8,128)(2,1)S(1)}, u32[]{:S(2)}, u32[]{:S(2)}) collective-permute-start(bf16[288,1280]{1,0:T(8,128)(2,1)S(1)} %maximum_maximum_fusion.refs_1_), channel_id=1, source_target_pairs={{8,0},{16,8},{24,16},{28,24},{20,28},{12,20},{4,12},{0,4},{9,1},{1... | collective-permute-start | bytes 2211848 | tf_op jit(solution)/shard_map/ppermute | solution.py:777
  15.4 19.5 %collective-permute-start.3 = (bf16[80,1152]{1,0:T(8,128)(2,1)S(1)}, bf16[80,1152]{1,0:T(8,128)(2,1)S(1)}, u32[]{:S(2)}, u32[]{:S(2)}) collective-permute-start(bf16[80,1152]{1,0:T(8,128)(2,1)S(1)} %concatenate.65.refs_0_.refs_8_), channel_id=1, source_target_pairs={{8,0},{16,8},{24,16},{28,24},{20,28},{12,20},{4,12},{0,4},{9,1},{1... | collective-permute-start | bytes 552968 | tf_op jit(solution)/shard_map/ppermute | solution.py:777
  35.0 24.5 %collective-permute-start.21 = (bf16[288,1280]{1,0:T(8,128)(2,1)S(1)}, bf16[288,1280]{1,0:T(8,128)(2,1)}, u32[]{:S(2)}, u32[]{:S(2)}) collective-permute-start(bf16[288,1280]{1,0:T(8,128)(2,1)S(1)} %collective-permute-done.11.refs_8_), channel_id=1, source_target_pairs={{0,8},{8,16},{16,24},{24,28},{28,20},{20,12},{12,4},{4,0},{1,9},{9... | collective-permute-start | bytes 2211848 | tf_op jit(solution)/shard_map/ppermute | solution.py:774
  36.7 22.9 %collective-permute-start.22 = (bf16[288,1280]{1,0:T(8,128)(2,1)S(1)}, bf16[288,1280]{1,0:T(8,128)(2,1)}, u32[]{:S(2)}, u32[]{:S(2)}) collective-permute-start(bf16[288,1280]{1,0:T(8,128)(2,1)S(1)} %collective-permute-done.12.refs_2_), channel_id=1, source_target_pairs={{8,0},{16,8},{24,16},{28,24},{20,28},{12,20},{4,12},{0,4},{9,1},{1... | collective-permute-start | bytes 2211848 | tf_op jit(solution)/shard_map/ppermute | solution.py:777
  59.5 20.8 %collective-permute-start.31 = (bf16[288,1280]{1,0:T(8,128)(2,1)}, bf16[288,1280]{1,0:T(8,128)(2,1)}, u32[]{:S(2)}, u32[]{:S(2)}) collective-permute-start(bf16[288,1280]{1,0:T(8,128)(2,1)} %collective-permute-done.21.refs_7_), channel_id=1, source_target_pairs={{0,8},{8,16},{16,24},{24,28},{28,20},{20,12},{12,4},{4,0},{1,9},{9... | collective-permute-start | bytes 2211848 | tf_op jit(solution)/shard_map/ppermute | solution.py:774
  61.2 19.2 %collective-permute-start.32 = (bf16[288,1280]{1,0:T(8,128)(2,1)}, bf16[288,1280]{1,0:T(8,128)(2,1)}, u32[]{:S(2)}, u32[]{:S(2)}) collective-permute-start(bf16[288,1280]{1,0:T(8,128)(2,1)} %collective-permute-done.22.refs_3_), channel_id=1, source_target_pairs={{8,0},{16,8},{24,16},{28,24},{20,28},{12,20},{4,12},{0,4},{9,1},{1... | collective-permute-start | bytes 2211848 | tf_op jit(solution)/shard_map/ppermute | solution.py:777
  102.5 26.0 %collective-permute-start.40 = (bf16[320,1664]{1,0:T(8,128)(2,1)S(1)}, bf16[320,1664]{1,0:T(8,128)(2,1)}, u32[]{:S(2)}, u32[]{:S(2)}) collective-permute-start(bf16[320,1664]{1,0:T(8,128)(2,1)S(1)} %pad.18.refs_0_.refs_1_), channel_id=1, source_target_pairs={{0,8},{8,16},{16,24},{24,28},{28,20},{20,12},{12,4},{4,0},{1,9},{9... | collective-permute-start | bytes 3194888 | tf_op jit(solution)/shard_map/ppermute | solution.py:774
  103.3 25.7 %collective-permute-start.41 = (bf16[320,1664]{1,0:T(8,128)(2,1)S(1)}, bf16[320,1664]{1,0:T(8,128)(2,1)}, u32[]{:S(2)}, u32[]{:S(2)}) collective-permute-start(bf16[320,1664]{1,0:T(8,128)(2,1)S(1)} %pad.18.refs_0_.refs_1_), channel_id=1, source_target_pairs={{8,0},{16,8},{24,16},{28,24},{20,28},{12,20},{4,12},{0,4},{9,1},{1... | collective-permute-start | bytes 3194888 | tf_op jit(solution)/shard_map/ppermute | solution.py:777
  129.0 74.6 %all-gather.7.cloned.1.call-start = ((), (), s32[]{:S(2)}) async-start(), calls=%async_computation.5 | async-start | bytes 6553600 | tf_op jit(solution)/shard_map/all_gather | solution.py:1095
  129.0 25.0 %collective-permute-start.42 = (bf16[320,1664]{1,0:T(8,128)(2,1)}, bf16[320,1664]{1,0:T(8,128)(2,1)S(1)}, u32[]{:S(2)}, u32[]{:S(2)}) collective-permute-start(bf16[320,1664]{1,0:T(8,128)(2,1)} %collective-permute-done.40.refs_7_.refs_4_), channel_id=1, source_target_pairs={{0,8},{8,16},{16,24},{24,28},{28,20},{20,12},{12,4},{4,0},{1,9},{9... | collective-permute-start | bytes 3194888 | tf_op jit(solution)/shard_map/ppermute | solution.py:774
  129.7 25.1 %collective-permute-start.43 = (bf16[320,1664]{1,0:T(8,128)(2,1)}, bf16[320,1664]{1,0:T(8,128)(2,1)S(1)}, u32[]{:S(2)}, u32[]{:S(2)}) collective-permute-start(bf16[320,1664]{1,0:T(8,128)(2,1)} %collective-permute-done.41.refs_1_.refs_2_), channel_id=1, source_target_pairs={{8,0},{16,8},{24,16},{28,24},{20,28},{12,20},{4,12},{0,4},{9,1},{1... | collective-permute-start | bytes 3194888 | tf_op jit(solution)/shard_map/ppermute | solution.py:777
  154.9 100.5 %reduce-scatter.5.cloned.1.call-start = ((), (), s32[]{:S(2)}) async-start(), calls=%async_computation.6 | async-start | bytes 6553600 | tf_op jit(solution)/shard_map/reduce_scatter | solution.py:1102
  158.3 44.9 %collective-permute-start.44 = (bf16[320,3200]{1,0:T(8,128)(2,1)}, bf16[320,3200]{1,0:T(8,128)(2,1)}, u32[]{:S(2)}, u32[]{:S(2)}) collective-permute-start(bf16[320,3200]{1,0:T(8,128)(2,1)} %paired.1.refs_0_.refs_1_.weights_ref), channel_id=1, source_target_pairs={{0,8},{8,16},{16,24},{24,28},{28,20},{20,12},{12,4},{4,0},{1,9},{9... | collective-permute-start | bytes 6144008 | tf_op jit(solution)/shard_map/ppermute | solution.py:774
  158.9 44.7 %collective-permute-start.45 = (bf16[320,3200]{1,0:T(8,128)(2,1)}, bf16[320,3200]{1,0:T(8,128)(2,1)}, u32[]{:S(2)}, u32[]{:S(2)}) collective-permute-start(bf16[320,3200]{1,0:T(8,128)(2,1)} %paired.1.refs_0_.refs_1_.weights_ref), channel_id=1, source_target_pairs={{8,0},{16,8},{24,16},{28,24},{20,28},{12,20},{4,12},{0,4},{9,1},{1... | collective-permute-start | bytes 6144008 | tf_op jit(solution)/shard_map/ppermute | solution.py:777
  203.6 148.4 %all-gather.9.cloned.1.call-start = ((), (), s32[]{:S(2)}) async-start(), calls=%async_computation.7 | async-start | bytes 6553600 | tf_op jit(solution)/shard_map/all_gather | solution.py:1112
  203.7 26.7 %collective-permute-start.46 = (bf16[320,1664]{1,0:T(8,128)(2,1)}, bf16[320,1664]{1,0:T(8,128)(2,1)S(1)}, u32[]{:S(2)}, u32[]{:S(2)}) collective-permute-start(bf16[320,1664]{1,0:T(8,128)(2,1)} %copy-done.17), channel_id=1, source_target_pairs={{0,8},{8,16},{16,24},{24,28},{28,20},{20,12},{12,4},{4,0},{1,9},{9... | collective-permute-start | bytes 3194888 | tf_op jit(solution)/shard_map/ppermute | solution.py:774
  204.8 26.8 %collective-permute-start.47 = (bf16[320,1664]{1,0:T(8,128)(2,1)}, bf16[320,1664]{1,0:T(8,128)(2,1)}, u32[]{:S(2)}, u32[]{:S(2)}) collective-permute-start(bf16[320,1664]{1,0:T(8,128)(2,1)} %copy-done.18), channel_id=1, source_target_pairs={{8,0},{16,8},{24,16},{28,24},{20,28},{12,20},{4,12},{0,4},{9,1},{1... | collective-permute-start | bytes 3194888 | tf_op jit(solution)/shard_map/ppermute | solution.py:777
  205.8 64.8 %collective-permute-start.48 = (bf16[320,3200]{1,0:T(8,128)(2,1)}, bf16[320,3200]{1,0:T(8,128)(2,1)}, u32[]{:S(2)}, u32[]{:S(2)}) collective-permute-start(bf16[320,3200]{1,0:T(8,128)(2,1)} %collective-permute-done.44.refs_7_.refs_4_), channel_id=1, source_target_pairs={{0,8},{8,16},{16,24},{24,28},{28,20},{20,12},{12,4},{4,0},{1,9},{9... | collective-permute-start | bytes 6144008 | tf_op jit(solution)/shard_map/ppermute | solution.py:774
  206.9 64.7 %collective-permute-start.49 = (bf16[320,3200]{1,0:T(8,128)(2,1)}, bf16[320,3200]{1,0:T(8,128)(2,1)}, u32[]{:S(2)}, u32[]{:S(2)}) collective-permute-start(bf16[320,3200]{1,0:T(8,128)(2,1)} %collective-permute-done.45.refs_1_.refs_2_), channel_id=1, source_target_pairs={{8,0},{16,8},{24,16},{28,24},{20,28},{12,20},{4,12},{0,4},{9,1},{1... | collective-permute-start | bytes 6144008 | tf_op jit(solution)/shard_map/ppermute | solution.py:777
  271.6 239.4 %reduce-scatter.7.cloned.1.call-start = ((), (), s32[]{:S(2)}) async-start(), calls=%async_computation.8 | async-start | bytes 6553600 | tf_op jit(solution)/shard_map/reduce_scatter | solution.py:1137
  287.4 43.6 %collective-permute-start.52 = (bf16[320,3200]{1,0:T(8,128)(2,1)}, bf16[320,3200]{1,0:T(8,128)(2,1)S(1)}, u32[]{:S(2)}, u32[]{:S(2)}) collective-permute-start(bf16[320,3200]{1,0:T(8,128)(2,1)} %collective-permute-done.49.refs_2_.refs_3_), channel_id=1, source_target_pairs={{8,0},{16,8},{24,16},{28,24},{20,28},{12,20},{4,12},{0,4},{9,1},{1... | collective-permute-start | bytes 6144008 | tf_op jit(solution)/shard_map/ppermute | solution.py:777
  288.0 43.0 %collective-permute-start.53 = (bf16[320,3200]{1,0:T(8,128)(2,1)}, bf16[320,3200]{1,0:T(8,128)(2,1)S(1)}, u32[]{:S(2)}, u32[]{:S(2)}) collective-permute-start(bf16[320,3200]{1,0:T(8,128)(2,1)} %collective-permute-done.48.refs_6_.refs_3_), channel_id=1, source_target_pairs={{0,8},{8,16},{16,24},{24,28},{28,20},{20,12},{12,4},{4,0},{1,9},{9... | collective-permute-start | bytes 6144008 | tf_op jit(solution)/shard_map/ppermute | solution.py:774
  331.1 18.2 %collective-permute-start.54 = (bf16[160,3200]{1,0:T(8,128)(2,1)S(1)}, bf16[160,3200]{1,0:T(8,128)(2,1)S(1)}, u32[]{:S(2)}, u32[]{:S(2)}) collective-permute-start(bf16[160,3200]{1,0:T(8,128)(2,1)S(1)} %slice.286), channel_id=1, source_target_pairs={{0,8},{8,16},{16,24},{24,28},{28,20},{20,12},{12,4},{4,0},{1,9},{9... | collective-permute-start | bytes 3072008 | tf_op jit(solution)/shard_map/ppermute | solution.py:774
  403.8 26.5 %collective-permute-start.58 = (bf16[160,3200]{1,0:T(8,128)(2,1)}, bf16[160,3200]{1,0:T(8,128)(2,1)}, u32[]{:S(2)}, u32[]{:S(2)}) collective-permute-start(bf16[160,3200]{1,0:T(8,128)(2,1)} %get-tuple-element.285), channel_id=1, source_target_pairs={{0,8},{8,16},{16,24},{24,28},{28,20},{20,12},{12,4},{4,0},{1,9},{9... | collective-permute-start | bytes 3072008 | tf_op jit(solution)/shard_map/ppermute | solution.py:774
  405.1 25.9 %collective-permute-start.59 = (bf16[160,3200]{1,0:T(8,128)(2,1)}, bf16[160,3200]{1,0:T(8,128)(2,1)}, u32[]{:S(2)}, u32[]{:S(2)}) collective-permute-start(bf16[160,3200]{1,0:T(8,128)(2,1)} %get-tuple-element.284), channel_id=1, source_target_pairs={{8,0},{16,8},{24,16},{28,24},{20,28},{12,20},{4,12},{0,4},{9,1},{1... | collective-permute-start | bytes 3072008 | tf_op jit(solution)/shard_map/ppermute | solution.py:777
  408.4 46.6 %collective-permute-start.61 = (bf16[320,1664]{1,0:T(8,128)(2,1)}, bf16[320,1664]{1,0:T(8,128)(2,1)}, u32[]{:S(2)}, u32[]{:S(2)}) collective-permute-start(bf16[320,1664]{1,0:T(8,128)(2,1)} %pad_maximum_fusion.4), channel_id=1, source_target_pairs={{8,0},{16,8},{24,16},{28,24},{20,28},{12,20},{4,12},{0,4},{9,1},{1... | collective-permute-start | bytes 3194888 | tf_op jit(solution)/shard_map/ppermute | solution.py:777
  410.2 44.8 %collective-permute-start.60 = (bf16[320,1664]{1,0:T(8,128)(2,1)}, bf16[320,1664]{1,0:T(8,128)(2,1)}, u32[]{:S(2)}, u32[]{:S(2)}) collective-permute-start(bf16[320,1664]{1,0:T(8,128)(2,1)} %pad_maximum_fusion.3), channel_id=1, source_target_pairs={{0,8},{8,16},{16,24},{24,28},{28,20},{20,12},{12,4},{4,0},{1,9},{9... | collective-permute-start | bytes 3194888 | tf_op jit(solution)/shard_map/ppermute | solution.py:774
  455.1 111.4 %all-gather.11.cloned.1.call-start = ((), (), s32[]{:S(2)}) async-start(), calls=%async_computation.9 | async-start | bytes 6553600 | tf_op jit(solution)/shard_map/all_gather | solution.py:1153
  455.1 50.1 %collective-permute-start.63 = (bf16[320,3200]{1,0:T(8,128)(2,1)}, bf16[320,3200]{1,0:T(8,128)(2,1)S(1)}, u32[]{:S(2)}, u32[]{:S(2)}) collective-permute-start(bf16[320,3200]{1,0:T(8,128)(2,1)} %pad_maximum_fusion.2), channel_id=1, source_target_pairs={{8,0},{16,8},{24,16},{28,24},{20,28},{12,20},{4,12},{0,4},{9,1},{1... | collective-permute-start | bytes 6144008 | tf_op jit(solution)/shard_map/ppermute | solution.py:777
  455.9 49.3 %collective-permute-start.62 = (bf16[320,3200]{1,0:T(8,128)(2,1)}, bf16[320,3200]{1,0:T(8,128)(2,1)}, u32[]{:S(2)}, u32[]{:S(2)}) collective-permute-start(bf16[320,3200]{1,0:T(8,128)(2,1)} %pad_maximum_fusion.1), channel_id=1, source_target_pairs={{0,8},{8,16},{16,24},{24,28},{28,20},{20,12},{12,4},{4,0},{1,9},{9... | collective-permute-start | bytes 6144008 | tf_op jit(solution)/shard_map/ppermute | solution.py:774
  466.3 50.2 %collective-permute-start.65 = (bf16[320,1664]{1,0:T(8,128)(2,1)}, bf16[320,1664]{1,0:T(8,128)(2,1)}, u32[]{:S(2)}, u32[]{:S(2)}) collective-permute-start(bf16[320,1664]{1,0:T(8,128)(2,1)} %add_convert_fusion.8), channel_id=1, source_target_pairs={{8,0},{16,8},{24,16},{28,24},{20,28},{12,20},{4,12},{0,4},{9,1},{1... | collective-permute-start | bytes 3194888 | tf_op jit(solution)/shard_map/ppermute | solution.py:777
  469.3 47.3 %collective-permute-start.64 = (bf16[320,1664]{1,0:T(8,128)(2,1)}, bf16[320,1664]{1,0:T(8,128)(2,1)}, u32[]{:S(2)}, u32[]{:S(2)}) collective-permute-start(bf16[320,1664]{1,0:T(8,128)(2,1)} %add_convert_fusion.9), channel_id=1, source_target_pairs={{0,8},{8,16},{16,24},{24,28},{28,20},{20,12},{12,4},{4,0},{1,9},{9... | collective-permute-start | bytes 3194888 | tf_op jit(solution)/shard_map/ppermute | solution.py:774
  516.6 154.3 %reduce-scatter.11.cloned.1.call-start = ((), (), s32[]{:S(2)}) async-start(), calls=%async_computation.11 | async-start | bytes 2949120 | tf_op jit(solution)/shard_map/reduce_scatter | solution.py:1172
  516.7 42.0 %collective-permute-start.67 = (bf16[320,3200]{1,0:T(8,128)(2,1)}, bf16[320,3200]{1,0:T(8,128)(2,1)S(1)}, u32[]{:S(2)}, u32[]{:S(2)}) collective-permute-start(bf16[320,3200]{1,0:T(8,128)(2,1)} %add_convert_fusion.3), channel_id=1, source_target_pairs={{8,0},{16,8},{24,16},{28,24},{20,28},{12,20},{4,12},{0,4},{9,1},{1... | collective-permute-start | bytes 6144008 | tf_op jit(solution)/shard_map/ppermute | solution.py:777
  517.4 41.9 %collective-permute-start.66 = (bf16[320,3200]{1,0:T(8,128)(2,1)}, bf16[320,3200]{1,0:T(8,128)(2,1)S(1)}, u32[]{:S(2)}, u32[]{:S(2)}) collective-permute-start(bf16[320,3200]{1,0:T(8,128)(2,1)} %add_convert_fusion.4), channel_id=1, source_target_pairs={{0,8},{8,16},{16,24},{24,28},{28,20},{20,12},{12,4},{4,0},{1,9},{9... | collective-permute-start | bytes 6144008 | tf_op jit(solution)/shard_map/ppermute | solution.py:774
  564.4 42.6 %collective-permute-start.69 = (bf16[320,3200]{1,0:T(8,128)(2,1)}, bf16[320,3200]{1,0:T(8,128)(2,1)S(1)}, u32[]{:S(2)}, u32[]{:S(2)}) collective-permute-start(bf16[320,3200]{1,0:T(8,128)(2,1)} %add_convert_fusion.1), channel_id=1, source_target_pairs={{8,0},{16,8},{24,16},{28,24},{20,28},{12,20},{4,12},{0,4},{9,1},{1... | collective-permute-start | bytes 6144008 | tf_op jit(solution)/shard_map/ppermute | solution.py:777
  565.6 41.5 %collective-permute-start.68 = (bf16[320,3200]{1,0:T(8,128)(2,1)}, bf16[320,3200]{1,0:T(8,128)(2,1)}, u32[]{:S(2)}, u32[]{:S(2)}) collective-permute-start(bf16[320,3200]{1,0:T(8,128)(2,1)} %add_convert_fusion.2), channel_id=1, source_target_pairs={{0,8},{8,16},{16,24},{24,28},{28,20},{20,12},{12,4},{4,0},{1,9},{9... | collective-permute-start | bytes 6144008 | tf_op jit(solution)/shard_map/ppermute | solution.py:774
  614.5 136.0 %reduce-scatter.9.cloned.1.call-start = ((), (), s32[]{:S(2)}) async-start(), calls=%async_computation.10 | async-start | bytes 6553600 | tf_op jit(solution)/shard_map/reduce_scatter | solution.py:1200
  618.2 21.9 %collective-permute-start.71 = (bf16[320,1664]{1,0:T(8,128)(2,1)S(1)}, bf16[320,1664]{1,0:T(8,128)(2,1)S(1)}, u32[]{:S(2)}, u32[]{:S(2)}) collective-permute-start(bf16[320,1664]{1,0:T(8,128)(2,1)S(1)} %add_convert_fusion.6), channel_id=1, source_target_pairs={{8,0},{16,8},{24,16},{28,24},{20,28},{12,20},{4,12},{0,4},{9,1},{1... | collective-permute-start | bytes 3194888 | tf_op jit(solution)/shard_map/ppermute | solution.py:777
  619.5 21.0 %collective-permute-start.70 = (bf16[320,1664]{1,0:T(8,128)(2,1)S(1)}, bf16[320,1664]{1,0:T(8,128)(2,1)S(1)}, u32[]{:S(2)}, u32[]{:S(2)}) collective-permute-start(bf16[320,1664]{1,0:T(8,128)(2,1)S(1)} %add_convert_fusion.7), channel_id=1, source_target_pairs={{0,8},{8,16},{16,24},{24,28},{28,20},{20,12},{12,4},{4,0},{1,9},{9... | collective-permute-start | bytes 3194888 | tf_op jit(solution)/shard_map/ppermute | solution.py:774
  683.0 19.5 %collective-permute-start.86 = (bf16[288,1280]{1,0:T(8,128)(2,1)}, bf16[288,1280]{1,0:T(8,128)(2,1)S(1)}, u32[]{:S(2)}, u32[]{:S(2)}) collective-permute-start(bf16[288,1280]{1,0:T(8,128)(2,1)} %get-tuple-element.291), channel_id=1, source_target_pairs={{0,8},{8,16},{16,24},{24,28},{28,20},{20,12},{12,4},{4,0},{1,9},{9... | collective-permute-start | bytes 2211848 | tf_op jit(solution)/shard_map/ppermute | solution.py:774
  685.0 19.7 %collective-permute-start.87 = (bf16[288,1280]{1,0:T(8,128)(2,1)}, bf16[288,1280]{1,0:T(8,128)(2,1)S(1)}, u32[]{:S(2)}, u32[]{:S(2)}) collective-permute-start(bf16[288,1280]{1,0:T(8,128)(2,1)} %get-tuple-element.290), channel_id=1, source_target_pairs={{8,0},{16,8},{24,16},{28,24},{20,28},{12,20},{4,12},{0,4},{9,1},{1... | collective-permute-start | bytes 2211848 | tf_op jit(solution)/shard_map/ppermute | solution.py:777
  712.6 24.1 %collective-permute-start.88 = (bf16[288,1280]{1,0:T(8,128)(2,1)S(1)}, bf16[288,1280]{1,0:T(8,128)(2,1)S(1)}, u32[]{:S(2)}, u32[]{:S(2)}) collective-permute-start(bf16[288,1280]{1,0:T(8,128)(2,1)S(1)} %get-tuple-element.288), channel_id=1, source_target_pairs={{0,8},{8,16},{16,24},{24,28},{28,20},{20,12},{12,4},{4,0},{1,9},{9... | collective-permute-start | bytes 2211848 | tf_op jit(solution)/shard_map/ppermute | solution.py:774
  713.2 23.5 %collective-permute-start.89 = (bf16[288,1280]{1,0:T(8,128)(2,1)S(1)}, bf16[288,1280]{1,0:T(8,128)(2,1)S(1)}, u32[]{:S(2)}, u32[]{:S(2)}) collective-permute-start(bf16[288,1280]{1,0:T(8,128)(2,1)S(1)} %get-tuple-element.289), channel_id=1, source_target_pairs={{8,0},{16,8},{24,16},{28,24},{20,28},{12,20},{4,12},{0,4},{9,1},{1... | collective-permute-start | bytes 2211848 | tf_op jit(solution)/shard_map/ppermute | solution.py:777
  723.0 23.1 %collective-permute-start.81 = (bf16[160,1152]{1,0:T(8,128)(2,1)}, bf16[160,1152]{1,0:T(8,128)(2,1)}, u32[]{:S(2)}, u32[]{:S(2)}) collective-permute-start(bf16[160,1152]{1,0:T(8,128)(2,1)} %get-tuple-element.307), channel_id=1, source_target_pairs={{0,8},{8,16},{16,24},{24,28},{28,20},{20,12},{12,4},{4,0},{1,9},{9... | collective-permute-start | bytes 1105928 | tf_op jit(solution)/shard_map/ppermute | solution.py:774
  724.7 21.3 %collective-permute-start.82 = (bf16[160,1152]{1,0:T(8,128)(2,1)}, bf16[160,1152]{1,0:T(8,128)(2,1)}, u32[]{:S(2)}, u32[]{:S(2)}) collective-permute-start(bf16[160,1152]{1,0:T(8,128)(2,1)} %get-tuple-element.306), channel_id=1, source_target_pairs={{8,0},{16,8},{24,16},{28,24},{20,28},{12,20},{4,12},{0,4},{9,1},{1... | collective-permute-start | bytes 1105928 | tf_op jit(solution)/shard_map/ppermute | solution.py:777
  (136 other events, 1962.8 us)
Sparse Core Ops, SparseCore 0:
  129.1 22.6 all-gather.4
  155.0 39.8 all-gather.6
  203.8 51.6 reduce-scatter.4
  271.7 39.9 all-gather.8
  455.2 49.6 reduce-scatter.6
  516.7 39.7 all-gather.10
  614.6 32.2 reduce-scatter.10
  671.0 54.2 reduce-scatter.8
